TPU v7x, 32 devices: a whole 2x2x4 slice. The times are simulated.
32 devices in a mesh: gx: 16 (over z, y, core), gy: 2 (over x).
Axes of the slice: x: 2, y: 2, z: 4, core: 2. Of those that a mesh axis runs over, the one named last changes fastest.
Arguments:
- latents: int32 [768, 64, 32], P('gy', 'gx'), may hold values from 0 to 31
- actions: int32 [768, 64], P('gy', 'gx'), may hold values from 0 to 17
- segment_ids: int32 [768, 64], replicated, may hold values from 0 to 3, never falling along the last dimension, each value on 1 to 32 neighbouring positions
- cotangent: bfloat16 [768, 64, 512], P('gy', 'gx'), may hold values from -6 to 6
- stem_weight: bfloat16 [1024, 512], replicated, may hold values from -1 to 1
- action_table: bfloat16 [18, 512], replicated, may hold values from -1 to 1
- first_gain: float32 [512], replicated, may hold values from 0.5 to 1.5
- first_bias: float32 [512], replicated, may hold values from -1 to 1
- query_weight: bfloat16 [512, 512], P(None, 'gy'), may hold values from -0.25 to 0.25
- key_weight: bfloat16 [512, 512], P(None, 'gy'), may hold values from -0.25 to 0.25
- value_weight: bfloat16 [512, 512], P(None, 'gy'), may hold values from -0.25 to 0.25
- out_weight: bfloat16 [512, 512], P('gy'), may hold values from -1 to 1
- second_gain: float32 [512], replicated, may hold values from 0.5 to 1.5
- second_bias: float32 [512], replicated, may hold values from -1 to 1
- up_weight: bfloat16 [512, 2048], P(None, 'gy'), may hold values from -0.25 to 0.25
- up_bias: float32 [2048], P('gy'), may hold values from -1 to 1
- down_weight: bfloat16 [2048, 512], P('gy'), may hold values from -0.125 to 0.125
- down_bias: float32 [512], replicated, may hold values from -1 to 1
Outputs:
- output: bfloat16 [768, 64, 512], P('gy', 'gx')
- token_grad: bfloat16 [768, 64, 512], P('gy', 'gx')
- stem_grad: float32 [1024, 512], replicated
- action_grad: float32 [18, 512], replicated
- first_gain_grad: float32 [512], replicated
- first_bias_grad: float32 [512], replicated
- query_grad: float32 [512, 512], P(None, 'gy')
- key_grad: float32 [512, 512], P(None, 'gy')
- value_grad: float32 [512, 512], P(None, 'gy')
- out_grad: float32 [512, 512], P('gy')
- second_gain_grad: float32 [512], replicated
- second_bias_grad: float32 [512], replicated
- up_grad: float32 [512, 2048], P(None, 'gy')
- up_bias_grad: float32 [2048], P('gy')
- down_grad: float32 [2048, 512], P('gy')
- down_bias_grad: float32 [512], replicated
Inputs may be any that keep to these rules, and one draw needn't show every extreme that they name: `segment_ids`: along each sequence of 64 frames the segment id never falls; each segment holds 1 to 32 frames.
All inputs are finite; a program needn't handle non-finite values.
Results may differ from a plain program's by a relative error of at most 0.012.
Values may be sent and summed in bfloat16 or wider, within the bound.
A program may use at most 192 MiB of HBM per device.

v0:
```python
import jax
import jax.numpy as jnp
from jax import lax
from jax.sharding import PartitionSpec as P

HD = 64


EPSILON = 1e-05
FLOAT = jnp.float32
BFLOAT = jnp.bfloat16


def norm_rows(values, gain, bias):
    average = jnp.mean(values, axis=-1, keepdims=True)
    centred = values - average
    spread = jnp.mean(centred * centred, axis=-1, keepdims=True)
    return centred * lax.rsqrt(spread + EPSILON) * gain + bias


def inner(left, right):
    return lax.dot_general(left, right, (((0,), (0,)), ((), ())), preferred_element_type=FLOAT)


def outer(left, right):
    return lax.dot_general(left, right, (((1,), (1,)), ((), ())), preferred_element_type=FLOAT)


def product(left, right):
    return jnp.dot(left, right, preferred_element_type=FLOAT)


def split_heads(block):
    return block.reshape(block.shape[0], block.shape[1], -1, HD)


def block_probs(query_block, key_block, label_block):
    length = query_block.shape[1]
    scores = 0.125 * jnp.einsum(
        "sqhd,skhd->shqk",
        split_heads(query_block),
        split_heads(key_block),
        preferred_element_type=FLOAT,
    )
    place = jnp.arange(length)
    allowed = (label_block[:, :, None] == label_block[:, None, :]) & (
        place[:, None] >= place[None, :]
    )[None]
    return jax.nn.softmax(jnp.where(allowed[:, None], scores, -1e30), axis=-1)


def block_forward(pieces):
    query_block, key_block, value_block, label_block = pieces
    probs_low = block_probs(query_block, key_block, label_block).astype(BFLOAT)
    mixed = jnp.einsum(
        "shqk,skhd->sqhd", probs_low, split_heads(value_block), preferred_element_type=FLOAT
    )
    return mixed.reshape(query_block.shape[0], query_block.shape[1], -1).astype(BFLOAT)


def block_backward(pieces):
    query_block, key_block, value_block, label_block, grad_block = pieces
    probs = block_probs(query_block, key_block, label_block)
    grad_heads = split_heads(grad_block)
    grad_probs = jnp.einsum(
        "sqhd,skhd->shqk", grad_heads, split_heads(value_block), preferred_element_type=FLOAT
    )
    grad_probs = lax.optimization_barrier(grad_probs.astype(BFLOAT)).astype(FLOAT)
    centre = jnp.sum(probs * grad_probs, axis=-1, keepdims=True)
    grad_scores = (probs * (grad_probs - centre)).astype(BFLOAT)
    grad_query = 0.125 * jnp.einsum(
        "shqk,skhd->sqhd", grad_scores, split_heads(key_block), preferred_element_type=FLOAT
    )
    grad_key = 0.125 * jnp.einsum(
        "shqk,sqhd->skhd", grad_scores, split_heads(query_block), preferred_element_type=FLOAT
    )
    grad_value = jnp.einsum(
        "shqk,sqhd->skhd", probs.astype(BFLOAT), grad_heads, preferred_element_type=FLOAT
    )
    shape = (query_block.shape[0], query_block.shape[1], -1)
    return tuple(
        (item.reshape(shape).astype(BFLOAT) for item in (grad_query, grad_key, grad_value))
    )


def layer_pass(seq_tokens, seq_cot, seg_rows, weights):
    (
        first_gain,
        first_bias,
        query_weight,
        key_weight,
        value_weight,
        out_weight,
        second_gain,
        second_bias,
        up_weight,
        up_bias,
        down_weight,
        down_bias,
    ) = weights
    seqs, length, width = seq_tokens.shape
    rows = seqs * length
    block = min(512, rows)
    blocks = rows // block
    within = block // length
    scale = 0.5
    inputs = seq_tokens.reshape(rows, width).astype(FLOAT)
    normed_one = norm_rows(inputs, first_gain, first_bias).astype(BFLOAT)
    query = product(normed_one, query_weight).astype(BFLOAT)
    key_rows = product(normed_one, key_weight).astype(BFLOAT)
    value_rows = product(normed_one, value_weight).astype(BFLOAT)
    labels = seg_rows.reshape(blocks, within, length)

    def split_rows(array):
        return array.reshape(blocks, within, length, -1)

    mixed = lax.map(
        block_forward, (split_rows(query), split_rows(key_rows), split_rows(value_rows), labels)
    )
    mixed = mixed.reshape(rows, -1)
    branch = product(mixed, out_weight)
    branch = lax.psum(branch, "gy")
    resid = inputs + branch
    normed_two = norm_rows(resid, second_gain, second_bias).astype(BFLOAT)
    pre_act = product(normed_two, up_weight) + up_bias
    hidden = jax.nn.gelu(pre_act).astype(BFLOAT)
    out_part = scale * (resid + down_bias) + product(hidden, down_weight)
    cot_rows = seq_cot.reshape(rows, width)
    cot_float = cot_rows.astype(FLOAT)
    down_bias_part = jnp.sum(cot_float, axis=0)
    down_part = inner(hidden, cot_rows)
    d_hidden = outer(cot_rows, down_weight)
    act_input = product(normed_two, up_weight) + up_bias
    _, gelu_pull = jax.vjp(jax.nn.gelu, act_input)
    d_pre = gelu_pull(d_hidden)[0].astype(BFLOAT)
    up_bias_part = jnp.sum(d_pre.astype(FLOAT), axis=0)
    up_part = inner(normed_two, d_pre)
    d_normed_two = outer(d_pre, up_weight)
    d_normed_two = lax.psum(d_normed_two, "gy")
    _, second_pull = jax.vjp(norm_rows, resid, second_gain, second_bias)
    d_resid_norm, second_gain_part, second_bias_part = second_pull(d_normed_two)
    d_resid = cot_float + d_resid_norm
    d_branch = d_resid.astype(BFLOAT)
    out_part_grad = inner(mixed, d_branch)
    d_mixed = outer(d_branch, out_weight).astype(BFLOAT)
    d_query, d_key, d_value = lax.map(
        block_backward,
        (
            split_rows(query),
            split_rows(key_rows),
            split_rows(value_rows),
            labels,
            split_rows(d_mixed),
        ),
    )
    d_query = d_query.reshape(rows, -1)
    d_key = d_key.reshape(rows, -1)
    d_value = d_value.reshape(rows, -1)
    query_part = inner(normed_one, d_query)
    key_part = inner(normed_one, d_key)
    value_part = inner(normed_one, d_value)
    d_normed_one = (
        outer(d_query, query_weight) + outer(d_key, key_weight) + outer(d_value, value_weight)
    )
    _, first_pull = jax.vjp(norm_rows, inputs, first_gain, first_bias)
    d_input_norm, first_gain_part, first_bias_part = first_pull(d_normed_one)
    d_tokens_part = scale * d_resid + d_input_norm
    parts = (
        first_gain_part,
        first_bias_part,
        query_part,
        key_part,
        value_part,
        out_part_grad,
        second_gain_part,
        second_bias_part,
        up_part,
        up_bias_part,
        down_part,
        down_bias_part,
    )
    return (
        out_part.reshape(seqs, length, width),
        d_tokens_part.reshape(seqs, length, width),
        parts,
    )


def per_device(
    latents,
    actions,
    segment_ids,
    cotangent,
    stem_weight,
    action_table,
    first_gain,
    first_bias,
    query_weight,
    key_weight,
    value_weight,
    out_weight,
    second_gain,
    second_bias,
    up_weight,
    up_bias,
    down_weight,
    down_bias,
):
    half_seqs, local_len, groups = latents.shape
    frames = half_seqs * local_len
    classes = stem_weight.shape[0] // groups
    latent_hot = (latents[..., None] == jnp.arange(classes, dtype=jnp.int32)).reshape(
        frames, groups * classes
    )
    latent_hot = latent_hot.astype(BFLOAT)
    action_hot = (
        actions.reshape(frames, 1) == jnp.arange(action_table.shape[0], dtype=jnp.int32)[None, :]
    )
    action_hot = action_hot.astype(BFLOAT)
    stem = product(latent_hot, stem_weight) + product(action_hot, action_table)
    tokens = stem.astype(BFLOAT).reshape(half_seqs, local_len, -1)
    token_all, cot_all = (
        lax.all_gather(tokens, "gy", axis=0, tiled=True),
        lax.all_gather(cotangent, "gy", axis=0, tiled=True),
    )
    seq_tokens, seq_cot = (
        lax.all_to_all(token_all, "gx", split_axis=0, concat_axis=1, tiled=True),
        lax.all_to_all(cot_all, "gx", split_axis=0, concat_axis=1, tiled=True),
    )
    seqs = seq_tokens.shape[0]
    first_seq = lax.axis_index("gx") * seqs
    weights = (
        first_gain,
        first_bias,
        query_weight,
        key_weight,
        value_weight,
        out_weight,
        second_gain,
        second_bias,
        up_weight,
        up_bias,
        down_weight,
        down_bias,
    )
    seg_rows = lax.dynamic_slice_in_dim(segment_ids, first_seq, seqs, 0)
    out_seq, grad_seq, parts = layer_pass(seq_tokens, seq_cot, seg_rows, weights)
    out_moved, grad_moved = (
        lax.all_to_all(out_seq, "gx", split_axis=1, concat_axis=0, tiled=True),
        lax.all_to_all(grad_seq, "gx", split_axis=1, concat_axis=0, tiled=True),
    )
    out_frames, grad_frames = (
        lax.psum_scatter(out_moved, "gy", scatter_dimension=0, tiled=True),
        lax.psum_scatter(grad_moved, "gy", scatter_dimension=0, tiled=True),
    )
    output = out_frames.astype(BFLOAT)
    token_grad = grad_frames.astype(BFLOAT)
    width = stem_weight.shape[1]
    grad_flat = token_grad.reshape(frames, width)
    stem_part = inner(latent_hot, grad_flat)
    action_part = inner(action_hot, grad_flat)
    (
        first_gain_part,
        first_bias_part,
        query_part,
        key_part,
        value_part,
        out_part_grad,
        second_gain_part,
        second_bias_part,
        up_part,
        up_bias_part,
        down_part,
        down_bias_part,
    ) = parts
    stem_grad, action_grad, first_gain_grad, first_bias_grad = lax.psum(
        (stem_part, action_part, first_gain_part, first_bias_part), ("gx", "gy")
    )
    (
        query_grad,
        key_grad,
        value_grad,
        out_grad,
        second_gain_grad,
        second_bias_grad,
        up_grad,
        up_bias_grad,
        down_grad,
        down_bias_grad,
    ) = lax.psum(
        (
            query_part,
            key_part,
            value_part,
            out_part_grad,
            second_gain_part,
            second_bias_part,
            up_part,
            up_bias_part,
            down_part,
            down_bias_part,
        ),
        "gx",
    )
    return (
        output,
        token_grad,
        stem_grad,
        action_grad,
        first_gain_grad,
        first_bias_grad,
        query_grad,
        key_grad,
        value_grad,
        out_grad,
        second_gain_grad,
        second_bias_grad,
        up_grad,
        up_bias_grad,
        down_grad,
        down_bias_grad,
    )


def solution(mesh):
    return jax.shard_map(
        per_device,
        mesh=mesh,
        in_specs=(
            P("gy", "gx", None),
            P("gy", "gx"),
            P(),
            P("gy", "gx", None),
            P(),
            P(),
            P(),
            P(),
            P(None, "gy"),
            P(None, "gy"),
            P(None, "gy"),
            P("gy", None),
            P(),
            P(),
            P(None, "gy"),
            P("gy"),
            P("gy", None),
            P(),
        ),
        out_specs=(
            P("gy", "gx", None),
            P("gy", "gx", None),
            P(),
            P(),
            P(),
            P(),
            P(None, "gy"),
            P(None, "gy"),
            P(None, "gy"),
            P("gy", None),
            P(),
            P(),
            P(None, "gy"),
            P("gy"),
            P("gy", None),
            P(),
        ),
        check_vma=False,
    )
```

profile of v0, /device:TPU:0, one launch (start us, length us, event | category | flops | bytes accessed | tf_op | source)
XLA Modules:
  0.0 1381.9 jit_solution(16798744642058293899)
XLA Ops:
  8.6 9.8 eq.86
  18.4 19.9 %eq.87 = s32[1536,1024]{1,0:T(8,128)} reshape(s32[384,4,32,32]{3,2,1,0:T(8,128)} %eq.86) | data formatting | bytes 12582912 | tf_op jit(solution)/shard_map/eq | solution.py:212
  38.7 4.8 fusion.28
  46.1 47.8 %all-gather.3.cloned.1.call-done = bf16[768,4,512]{2,1,0:T(4,128)(2,1)} async-done(((bf16[384,4,512]{2,1,0:T(4,128)(2,1)}), bf16[768,4,512]{2,1,0:T(4,128)(2,1)}) %all-gather.3.cloned.1.call-update) | async-done | bytes 3145744 | tf_op jit(solution)/shard_map/all_gather | solution.py:223
  93.9 5.7 all-to-all-start
  101.5 57.4 %all-to-all-done = bf16[768,4,512]{2,1,0:T(4,128)(2,1)} async-done(((bf16[768,4,512]{2,1,0:T(4,128)(2,1)}), bf16[768,4,512]{2,1,0:T(4,128)(2,1)}, u32[]{:S(2)}, u32[]{:S(2)}) %all-to-all-start) | async-done | bytes 3145760 | tf_op jit(solution)/shard_map/all_to_all | solution.py:227
  158.9 3.2 fusion.38
  162.2 4.4 multiply_reduce_fusion.5
  166.9 6.3 copy_bitcast_fusion
  174.3 7.6 reshape.397
  182.0 3.8 add_convert_fusion.2
  185.8 2.1 convolution_convert_fusion.6
  187.9 2.1 convolution_convert_fusion.5
  190.0 2.1 convolution_convert_fusion.4
  193.5 43.5 %while.24 = (s32[]{:T(128)}, bf16[6,8,64,256]{3,2,1,0:T(8,128)(2,1)}, bf16[6,8,64,256]{3,2,1,0:T(8,128)(2,1)}, s32[6,8,64]{2,1,0:T(8,128)S(1)}, bf16[6,8,64,256]...) while((s32[]{:T(128)}, bf16[6,8,64,256]{3,2,1,0:T(8,128)(2,1)}, ...), condition=%wide.region_5.6_spmd, body=%wide.region_2.5_spmd.sunk | while | flops 34674816 | bytes 9009781 | solution.py:117
  237.0 5.0 fusion.46
  242.1 85.7 %all_to_all.60 = bf16[768,4,512]{2,1,0:T(4,128)(2,1)S(1)} all-to-all(bf16[768,4,512]{2,1,0:T(4,128)(2,1)} %all-gather.5.cloned.1.call-done), channel_id=1, replica_groups=mesh['gx'=16,'gy'=2] {'gx'}, dimensions={0} | all-to-all | bytes 6291456 | tf_op jit(solution)/shard_map/all_to_all | solution.py:228
  329.4 3.4 copy.146
  332.8 5.7 reshape.390
  338.5 66.7 %all-reduce.12.cloned.1.call-done = f32[3072,512]{1,0:T(8,128)} async-done(((f32[3072,512]{1,0:T(8,128)}), f32[3072,512]{1,0:T(8,128)}) %all-reduce.12.cloned.1.call-update) | async-done | bytes 6291472 | tf_op jit(solution)/shard_map/psum | solution.py:122
  405.2 5.3 fusion.43
  410.6 2.1 multiply_reduce_fusion.4
  412.7 9.9 multiply_convert_fusion
  422.7 13.3 convert_reduce_fusion
  436.0 2.6 copy-done.57
  438.6 5.8 fusion.47
  445.0 9.6 multiply_add_fusion
  454.7 6.4 copy.108
  461.0 5.9 all-to-all-start.1
  466.9 130.8 %all-reduce.14.cloned.1.call-done = f32[3072,512]{1,0:T(8,128)} async-done(((f32[3072,512]{1,0:T(8,128)}), f32[3072,512]{1,0:T(8,128)}) %all-reduce.14.cloned.1.call-update) | async-done | bytes 6291472 | tf_op jit(solution)/shard_map/psum | solution.py:139
  597.7 6.1 multiply_reduce_fusion
  604.2 5.5 fusion.42
  612.3 2.2 convolution_convert_fusion.3
  618.5 89.6 %while.25 = (s32[]{:T(128)}, bf16[6,8,64,256]{3,2,1,0:T(8,128)(2,1)}, bf16[6,8,64,256]{3,2,1,0:T(8,128)(2,1)}, bf16[6,8,64,256]{3,2,1,0:T(8,128)(2,1)}, bf16[6,8...) while((s32[]{:T(128)}, ...), condition=%wide.region_17.18_spmd, body=%wide.region_13.17_spmd.sunk | while | flops 86839424 | bytes 17955988 | solution.py:146
  628.5 2.0 convolution_convert_fusion.12
  643.4 2.0 convolution_convert_fusion.12
  658.3 2.0 convolution_convert_fusion.12
  673.3 2.0 convolution_convert_fusion.12
  688.2 2.0 convolution_convert_fusion.12
  708.1 2.6 fusion.48
  710.8 4.2 fusion.49
  716.4 8.2 multiply_reduce_fusion.1
  724.7 5.8 fusion.41
  732.1 6.3 copy.113
  738.4 5.8 all-to-all-start.3
  744.3 9.9 iota_compare_fusion.2
  754.2 15.2 %eq.98 = pred[1536,1024]{1,0:T(32,128)(4,1)} reshape(pred[384,4,32,32]{3,2,1,0:T(32,128)(4,1)} %iota_compare_fusion.2) | data formatting | bytes 3145728 | tf_op jit(solution)/shard_map/eq | solution.py:212
  770.7 5.6 add_convert_fusion
  776.3 5.7 convert_element_type.173
  782.0 8.6 fusion.55
  790.6 7.8 fusion.39
  806.0 9.7 copy.109
  815.7 58.3 %all-to-all-done.3 = f32[48,64,512]{2,0,1:T(8,128)} async-done(((f32[48,64,512]{2,0,1:T(8,128)}), f32[48,64,512]{2,0,1:T(8,128)}, u32[]{:S(2)}, u32[]{:S(2)}) %all-to-all-start.3) | async-done | bytes 6291488 | tf_op jit(solution)/shard_map/all_to_all | solution.py:250
  874.1 9.6 copy.114
  883.7 290.4 %all-reduce.19 = (bf16[768,4,512]{2,1,0:T(4,128)(2,1)}, bf16[768,4,512]{2,1,0:T(4,128)(2,1)}) all-reduce(f32[768,4,512]{2,1,0:T(4,128)} %bitcast.176, f32[768,4,512]{2,1,0:T(4,128)} %bitcast.177), channel_id=2, replica_groups=mesh['gx'=16,'gy'=2] {'gy'}, use_global_device_ids=true, to_apply=%region_9.10.clone | all-reduce | flops 3145728 | bytes 18874368
  1174.0 3.1 dynamic-slice_convert_fusion
  1177.1 2.4 reshape.396
  1179.5 4.6 fusion.50
  1184.1 3.3 convert_reduce_fusion.1
  1187.4 102.3 %all-reduce.3 = (f32[512]{0:T(512)}, f32[512]{0:T(512)}, f32[1024]{0:T(1024)}, f32[512]{0:T(512)}) all-reduce(f32[512]{0:T(512)S(1)} %get-tuple-element.146, f32[512]{0:T(512)S(1)} %get-tuple-element.150, f32[1024]{0:T(1024)S(1)} %copy-done.49, f32[512]{0:T(512)S(1)} %convert_reduce_fusion.1), channel_id=1, replica_groups=mesh['gx'=16,'gy'=2] {'gx'}, use_global_device_ids=true, to_apply=%region_32.33 | all-reduce | flops 2560 | bytes 20480 | tf_op jit(solution)/shard_map/psum | solution.py:290
  1290.2 38.1 %all-reduce.2 = (f32[18,512]{1,0:T(8,128)}, f32[512]{0:T(512)}, f32[512]{0:T(512)}) all-reduce(f32[18,512]{1,0:T(8,128)S(1)} %fusion.33, f32[512]{0:T(512)S(1)} %get-tuple-element.148, f32[512]{0:T(512)S(1)} %get-tuple-element.151), channel_id=1, replica_groups=mesh['gx'=16,'gy'=2] {'gx','gy'}, use_global_device_ids=true, to_apply=%region_22.23 | all-reduce | flops 10240 | bytes 81920 | tf_op jit(solution)/shard_map/psum | solution.py:276
  1328.3 3.1 dynamic-slice_convert_fusion.1
  1331.4 32.2 %all-reduce.16.cloned.1.call-done = f32[1024,512]{1,0:T(8,128)} async-done(((f32[1024,512]{1,0:T(8,128)}), f32[1024,512]{1,0:T(8,128)}) %all-reduce.16.cloned.1.call-update) | async-done | bytes 2097168 | tf_op jit(solution)/shard_map/psum | solution.py:276
  1363.7 3.2 copy.208
  (432 shorter events, 160.2 us)
Async XLA Ops:
  7.2 405.5 %copy-start = (bf16[512,1024]{1,0:T(8,128)(2,1)S(1)}, bf16[512,1024]{1,0:T(8,128)(2,1)}, u32[]{:S(2)}) copy-start(bf16[512,1024]{1,0:T(8,128)(2,1)} %param.36) | copy-start | bytes 3145732
  7.2 86.7 %all-gather.3.cloned.1.call-start = ((), (), s32[]{:S(2)}) async-start(), calls=%async_computation.4 | async-start | bytes 4718592 | tf_op jit(solution)/shard_map/all_gather | solution.py:223
  8.6 9.8 copy-start.17
  18.4 20.0 %copy-start.48 = (s32[384,4]{0,1:T(4,128)S(1)}, s32[384,4]{0,1:T(4,128)}, u32[]{:S(2)}) copy-start(s32[384,4]{0,1:T(4,128)} %param.23) | copy-start | bytes 18436
  38.7 4.9 copy-start.40
  38.7 4.9 copy-start.44
  93.9 65.1 %all-to-all-start = ((bf16[768,4,512]{2,1,0:T(4,128)(2,1)}), bf16[768,4,512]{2,1,0:T(4,128)(2,1)}, u32[]{:S(2)}, u32[]{:S(2)}) async-start(bf16[768,4,512]{2,1,0:T(4,128)(2,1)} %all-gather.3.cloned.1.call-done), calls=%async_computation | async-start | bytes 6291456 | tf_op jit(solution)/shard_map/all_to_all | solution.py:227
  99.5 142.5 %all-gather.5.cloned.1.call-start = ((), (), s32[]{:S(2)}) async-start(), calls=%async_computation.6 | async-start | bytes 4718592 | tf_op jit(solution)/shard_map/all_gather | solution.py:224
  100.3 304.9 %all-reduce.12.cloned.1.call-start = ((), (), s32[]{:S(2)}) async-start(), calls=%async_computation.5 | async-start | bytes 12582912 | tf_op jit(solution)/shard_map/psum | solution.py:122
  162.2 11.0 copy-start.19
  166.9 15.1 %copy-start.34 = (f32[3072]{0:T(1024)}, f32[3072]{0:T(1024)S(1)}, u32[]{:S(2)}) copy-start(f32[3072]{0:T(1024)S(1)} %div.59) | copy-start | bytes 36868
  174.2 7.7 copy-start.38
  174.3 7.7 copy-start.36
  174.3 7.7 copy-start.42
  174.3 7.7 copy-start.45
  182.0 3.8 copy-start.28
  182.0 5.9 copy-start.31
  185.8 4.3 copy-start.32
  193.5 43.5 %copy-start.30 = (bf16[256,512]{1,0:T(8,128)(2,1)S(1)}, bf16[256,512]{1,0:T(8,128)(2,1)}, u32[]{:S(2)}) copy-start(bf16[256,512]{1,0:T(8,128)(2,1)} %param.33) | copy-start | bytes 786436
  242.0 355.7 %all-reduce.14.cloned.1.call-start = ((), (), s32[]{:S(2)}) async-start(), calls=%async_computation.7 | async-start | bytes 12582912 | tf_op jit(solution)/shard_map/psum | solution.py:139
  410.5 12.2 copy-start.3
  412.7 10.0 copy-start.7
  412.7 10.0 copy-start.50
  436.0 2.6 copy-start.57
  461.0 277.4 %all-to-all-start.1 = ((f32[48,64,512]{2,0,1:T(8,128)}), f32[48,64,512]{2,0,1:T(8,128)}, u32[]{:S(2)}, u32[]{:S(2)}) async-start(f32[48,64,512]{2,0,1:T(8,128)} %copy.108), calls=%async_computation.1 | async-start | bytes 12582912 | tf_op jit(solution)/shard_map/all_to_all | solution.py:249
  597.7 6.4 copy-start.10
  604.2 5.5 copy-start.8
  609.7 2.6 copy-start.4
  708.1 2.6 copy-start.12
  708.1 2.7 copy-start.33
  710.7 4.3 slice-start
  710.7 4.3 copy-start.14
  710.7 4.3 copy-start.29
  710.7 4.3 copy-start.35
  710.7 4.3 copy-start.37
  710.7 4.3 copy-start.43
  710.8 5.7 slice-start.1
  710.8 19.7 %slice-start.4 = ((s8[6291456]{0:T(1024)(128)(4,1)}), s8[4194304]{0:T(1024)(128)(4,1)S(1)}, s32[]{:S(2)}) async-start(s8[6291456]{0:T(1024)(128)(4,1)} %bitcast.170), calls=%async_computation.14 | async-start | bytes 8388608
  716.4 8.2 copy-start.39
  716.4 14.1 %slice-start.5 = ((s8[6291456]{0:T(1024)(128)(4,1)}), s8[2097152]{0:T(1024)(128)(4,1)S(1)}, s32[]{:S(2)}) async-start(s8[6291456]{0:T(1024)(128)(4,1)} %bitcast.170), calls=%async_computation.15 | async-start | bytes 4194304
  724.7 5.9 copy-start.9
  738.4 5.9 copy-start.18
  738.4 135.6 %all-to-all-start.3 = ((f32[48,64,512]{2,0,1:T(8,128)}), f32[48,64,512]{2,0,1:T(8,128)}, u32[]{:S(2)}, u32[]{:S(2)}) async-start(f32[48,64,512]{2,0,1:T(8,128)} %copy.113), calls=%async_computation.3 | async-start | bytes 12582912 | tf_op jit(solution)/shard_map/all_to_all | solution.py:250
  744.2 587.2 %all-reduce.18.cloned.1.call-start = ((), (), s32[]{:S(2)}) async-start(), calls=%async_computation.9 | async-start | bytes 12582912 | tf_op jit(solution)/shard_map/psum | solution.py:290
  744.3 25.1 %copy-start.55 = (u32[32]{0:T(128)S(1)}, u32[32]{0:T(128)}, u32[]{:S(2)}) copy-start(u32[32]{0:T(128)} %constant.93) | copy-start | bytes 388
  744.3 26.4 %copy-start.20 = (f32[48,16,4]{2,1,0:T(8,128)S(1)}, f32[48,16,4]{2,1,0:T(8,128)}, u32[]{:S(2)}) copy-start(f32[48,16,4]{2,1,0:T(8,128)} %copy-done.19) | copy-start | bytes 36868
  744.3 26.4 %copy-start.25 = (f32[48,16,4]{2,1,0:T(8,128)S(1)}, f32[48,16,4]{2,1,0:T(8,128)}, u32[]{:S(2)}) copy-start(f32[48,16,4]{2,1,0:T(8,128)} %get-tuple-element.209) | copy-start | bytes 36868
  744.3 26.4 %copy-start.46 = (f32[512]{0:T(512)S(1)}, f32[512]{0:T(512)}, u32[]{:S(2)}) copy-start(f32[512]{0:T(512)} %param.29) | copy-start | bytes 6148
  776.3 14.3 %slice-start.2 = ((s8[6291456]{0:T(1024)(128)(4,1)}), s8[2097152]{0:T(1024)(128)(4,1)S(1)}, s32[]{:S(2)}) async-start(s8[6291456]{0:T(1024)(128)(4,1)} %bitcast.168), calls=%async_computation.12 | async-start | bytes 4194304
  782.0 8.6 slice-start.3
  782.0 8.6 copy-start.54
  790.6 7.9 copy-start.16
  790.6 7.9 copy-start.22
  790.6 9.6 copy-start.15
  798.5 3.7 copy-start.13
  800.4 3.6 copy-start.11
  805.8 557.8 %all-reduce.16.cloned.1.call-start = ((), (), s32[]{:S(2)}) async-start(), calls=%async_computation.8 | async-start | bytes 4194304 | tf_op jit(solution)/shard_map/psum | solution.py:276
  1179.5 7.9 copy-start.49
  1179.5 110.1 %copy-start.41 = (s32[1536]{0:T(1024)S(1)}, s32[1536]{0:T(1024)}, u32[]{:S(2)}) copy-start(s32[1536]{0:T(1024)} %copy-done.40) | copy-start | bytes 18436
  1331.4 40.8 %copy-start.24 = (f32[512,1024]{1,0:T(8,128)S(1)}, f32[512,1024]{1,0:T(8,128)}, u32[]{:S(2)}) copy-start(f32[512,1024]{1,0:T(8,128)} %get-tuple-element.383) | copy-start | bytes 6291460
  1363.7 7.0 copy-start.27
  1363.7 7.8 copy-start.26
  1363.7 9.9 copy-start.23
  1363.7 11.2 copy-start.1
  (19 other events, 24.4 us)
Sparse Core Ops, SparseCore 0:
  46.2 47.6 all-gather.2
  101.9 45.2 all-gather.4
  242.1 163.0 all-reduce.11
  444.5 153.1 all-reduce.13
  805.9 207.0 all-reduce.17
  1184.2 179.3 all-reduce.15
where the time goes:
time: 1390 us; the launch traced here: 1380 us
  blocking collectives  516 us (37%)
  waiting for transfers between devices  394 us (28%)
  local copies, waits for them, and re-layouts  220 us (16%)
  matrix products  136 us (10%)
  other arithmetic  80.8 us (6%)
  starting transfers between devices  17.9 us (1%)
  between operations  15.8 us (1%)
    unnamed x1, blocking collectives  290 us
    psum x1, waiting for transfers between devices, layer_pass(): d_normed_two = lax.psum(d_normed_two, 'gy')  131 us
    psum x1, blocking collectives, per_device(): lax.psum((query_part, key_part, value_part, out_part_grad, second_gain_pa...  102 us
    all_to_all x1, blocking collectives, per_device(): lax.all_to_all(cot_all, 'gx', split_axis=0, concat_axis=1, tiled=True)  85.7 us
    psum x1, waiting for transfers between devices, layer_pass(): branch = lax.psum(branch, 'gy')  66.7 us
    all_to_all x1, waiting for transfers between devices, per_device(): lax.all_to_all(grad_seq, 'gx', split_axis=1, concat_axis=0, tiled=True)  58.3 us
    all_to_all x1, waiting for transfers between devices, per_device(): lax.all_to_all(token_all, 'gx', split_axis=0, concat_axis=1, tiled=True)  57.4 us
    all_gather x1, waiting for transfers between devices, per_device(): lax.all_gather(tokens, 'gy', axis=0, tiled=True)  47.8 us
  transfers between devices with their start and end apart: 9, of which 6 were waited for; matrix products, arithmetic and copies ran while one was open for 24% of the time, Pallas kernels for 0%

commit v1 on v0

v1 whole, which is shorter than its diff:
```python
import functools

import jax
import jax.numpy as jnp
from jax import lax
from jax.experimental import pallas as pl
from jax.experimental.pallas import tpu as pltpu
from jax.sharding import PartitionSpec as P

HD = 64
PACK = 256
EPSILON = 1e-05
FLOAT = jnp.float32
BFLOAT = jnp.bfloat16
TILE = 512
FFB = 512
HOT_PAD = 128
GELU_C = 0.7978845608028654
GELU_A = 0.044715


def dot(left, right):
    return lax.dot_general(left, right, (((1,), (0,)), ((), ())), preferred_element_type=FLOAT)


def dot_t(left, right):
    return lax.dot_general(left, right, (((1,), (1,)), ((), ())), preferred_element_type=FLOAT)


def t_dot(left, right):
    return lax.dot_general(left, right, (((0,), (0,)), ((), ())), preferred_element_type=FLOAT)


def iota(shape, dim):
    return lax.broadcasted_iota(jnp.int32, shape, dim)


def norm_stats(values):
    average = jnp.mean(values, axis=-1, keepdims=True)
    centred = values - average
    spread = jnp.mean(centred * centred, axis=-1, keepdims=True)
    scale = lax.rsqrt(spread + EPSILON)
    return centred * scale, scale


def norm_back(grad, xhat, scale, gain):
    scaled = grad * gain
    mean_e = jnp.mean(scaled, axis=-1, keepdims=True)
    mean_x = jnp.mean(scaled * xhat, axis=-1, keepdims=True)
    return (scaled - mean_e - xhat * mean_x) * scale


def col_sum(values):
    return jnp.sum(values, axis=0, keepdims=True)


def head_reduce(values, op, fill):
    parts = []
    for half in range(PACK // 128):
        piece = values[:, half * 128 : (half + 1) * 128]
        low = iota(piece.shape, 1) < HD
        first = op(jnp.where(low, piece, fill), axis=-1, keepdims=True)
        second = op(jnp.where(low, fill, piece), axis=-1, keepdims=True)
        parts.append((low, first, second))
    return parts


def head_spread(parts):
    return jnp.concatenate([jnp.where(low, a, b) for low, a, b in parts], axis=1)


def block_diag(rows):
    mask = (iota((PACK, PACK), 0) // HD) == (iota((PACK, PACK), 1) // HD)
    return jnp.where(mask, jnp.concatenate([rows] * (PACK // HD), axis=0), jnp.zeros((), rows.dtype))


def diag_rows(full):
    lane_head = iota((HD, PACK), 1) // HD
    result = full[:HD]
    for head in range(1, PACK // HD):
        result = jnp.where(lane_head == head, full[head * HD : (head + 1) * HD], result)
    return result


def unrolled_loop(count, body):
    if count == 1:
        body(0)
    else:
        pl.loop(0, count)(body)


def compute_kernel(
    local_len,
    lat_ref,
    mask_ref,
    cot_ref,
    stem_ref,
    wqkv_ref,
    wout_ref,
    wup_ref,
    wdown_ref,
    vec_ref,
    upb_ref,
    out_ref,
    tg_ref,
    gstem_ref,
    gqkv_ref,
    gout_ref,
    gup_ref,
    gdown_ref,
    gvec_ref,
    gupb_ref,
    tok_s,
    n1_s,
    qkv_s,
    prob_s,
    mix_s,
    dbr_s,
    acc_s,
    dn_s,
    n2_s,
    cotp_s,
):
    rows, width = tok_s.shape
    length = cot_ref.shape[0] * local_len
    packs = width // PACK
    group_seqs = 16 // local_len
    group_rows = group_seqs * length
    tile = max(TILE, group_rows)
    tiles = rows // tile
    ff = wup_ref.shape[1]
    hot_width = stem_ref.shape[0]
    classes = (hot_width - HOT_PAD) // 32

    def perm(shape_rows):
        dest = iota((shape_rows, shape_rows), 0)
        src = iota((shape_rows, shape_rows), 1)
        want = ((dest % length) // local_len) * 16 + (dest // length) * local_len + dest % local_len
        return jnp.where(want == src, 1.0, 0.0).astype(BFLOAT)

    def perm_back(shape_rows):
        dest = iota((shape_rows, shape_rows), 1)
        src = iota((shape_rows, shape_rows), 0)
        want = ((dest % length) // local_len) * 16 + (dest // length) * local_len + dest % local_len
        return jnp.where(want == src, 1.0, 0.0).astype(BFLOAT)

    def make_hot(r0):
        lats = lat_ref[pl.ds(r0, tile), :]
        kk = lats.shape[1]
        parts = []
        for block in range(0, hot_width, 128):
            g = iota((kk, 128), 0)
            c = iota((kk, 128), 1) + block
            spread = jnp.where(jnp.minimum(c // classes, 32) == g, 1.0, 0.0).astype(BFLOAT)
            val = dot(lats, spread)
            lane = iota((tile, 128), 1)
            target = (lane + block) % classes if block < hot_width - HOT_PAD else lane
            parts.append(jnp.where(val == target.astype(FLOAT), 1.0, 0.0).astype(BFLOAT))
        return jnp.concatenate(parts, axis=1)

    gstem_ref[...] = jnp.zeros_like(gstem_ref)
    gqkv_ref[...] = jnp.zeros_like(gqkv_ref)
    gout_ref[...] = jnp.zeros_like(gout_ref)
    gup_ref[...] = jnp.zeros_like(gup_ref)
    gdown_ref[...] = jnp.zeros_like(gdown_ref)
    gvec_ref[...] = jnp.zeros_like(gvec_ref)
    gupb_ref[...] = jnp.zeros_like(gupb_ref)

    g1 = vec_ref[0:1, :]
    b1 = vec_ref[1:2, :]
    g2 = vec_ref[2:3, :]
    b2 = vec_ref[3:4, :]
    bd = vec_ref[4:5, :]

    @pl.loop(0, tiles)
    def phase_one(t):
        r0 = pl.multiple_of(t * tile, tile)
        here = pl.ds(r0, tile)
        tokens = dot(make_hot(r0), stem_ref[...]).astype(BFLOAT)
        tok_s[here, :] = tokens
        xhat, _ = norm_stats(tokens.astype(FLOAT))
        normed = (xhat * g1 + b1).astype(BFLOAT)
        n1_s[here, :] = normed
        for part in range(3):
            cols = slice(part * width, (part + 1) * width)
            value = dot(normed, wqkv_ref[:, cols])
            if part == 0:
                value = value.astype(BFLOAT).astype(FLOAT) * 0.125
            qkv_s[here, cols] = value.astype(BFLOAT)

        @pl.loop(0, tile // 256)
        def attend(sub):
            for seq in range(256 // length):
                s0 = pl.multiple_of(r0 + sub * 256 + seq * length, length)
                bias = mask_ref[pl.ds(s0, length), :].astype(FLOAT)
                for pack in range(packs):
                    c0 = pack * PACK
                    q = qkv_s[pl.ds(s0, length), c0 : c0 + PACK]
                    k = qkv_s[pl.ds(s0, length), width + c0 : width + c0 + PACK]
                    v = qkv_s[pl.ds(s0, length), 2 * width + c0 : 2 * width + c0 + PACK]
                    scores = dot_t(q, block_diag(k)) + bias
                    top = head_spread(head_reduce(scores, jnp.max, -3e38))
                    e = jnp.exp(scores - top)
                    sums = head_reduce(e, jnp.sum, 0.0)
                    inv = head_spread([(low, 1.0 / a, 1.0 / b) for low, a, b in sums])
                    probs = (e * inv).astype(BFLOAT)
                    prob_s[pl.ds(s0, length), c0 : c0 + PACK] = probs
                    mix_s[pl.ds(s0, length), c0 : c0 + PACK] = dot(probs, block_diag(v)).astype(BFLOAT)

    @pl.loop(0, tiles)
    def phase_two(t):
        r0 = pl.multiple_of(t * tile, tile)
        here = pl.ds(r0, tile)
        mixed = mix_s[here, :]
        resid = tok_s[here, :].astype(FLOAT) + dot(mixed, wout_ref[...])
        xhat, scale = norm_stats(resid)
        n2_s[...] = (xhat * g2 + b2).astype(BFLOAT)
        for g in range(tile // group_rows):
            k0 = pl.multiple_of((t * (tile // group_rows) + g) * 16, 16)
            raw = cot_ref[:, pl.ds(k0, 16), :].reshape(group_rows, width)
            cotp_s[g * group_rows : (g + 1) * group_rows, :] = dot(perm(group_rows), raw).astype(BFLOAT)
        acc_s[...] = resid + bd
        dn_s[...] = jnp.zeros_like(dn_s)

        @pl.loop(0, ff // FFB)
        def feed(f):
            f0 = pl.multiple_of(f * FFB, FFB)
            fs = pl.ds(f0, FFB)
            n2 = n2_s[...]
            cot = cotp_s[...]
            up = wup_ref[:, fs]
            down = wdown_ref[fs, :]
            pre = dot(n2, up) + upb_ref[0:1, fs]
            square = pre * pre
            tanh = jnp.tanh(GELU_C * pre * (1.0 + GELU_A * square))
            half = 0.5 * (1.0 + tanh)
            hidden = (pre * half).astype(BFLOAT)
            slope = half + (0.5 * GELU_C) * pre * (1.0 - tanh * tanh) * (1.0 + 3.0 * GELU_A * square)
            acc_s[...] += dot(hidden, down)
            gdown_ref[fs, :] += t_dot(hidden, cot)
            d_pre_f = (dot_t(cot, down) * slope).astype(BFLOAT)
            gupb_ref[0:1, fs] += col_sum(d_pre_f.astype(FLOAT))
            gup_ref[:, fs] += t_dot(n2, d_pre_f)
            dn_s[...] += dot_t(d_pre_f, up)

        cot_f = cotp_s[...].astype(FLOAT)
        gvec_ref[4:5, :] += col_sum(cot_f)
        out = acc_s[...].astype(BFLOAT)
        for g in range(tile // group_rows):
            k0 = pl.multiple_of((t * (tile // group_rows) + g) * 16, 16)
            back = dot(perm_back(group_rows), out[g * group_rows : (g + 1) * group_rows, :])
            out_ref[:, pl.ds(k0, 16), :] = back.astype(BFLOAT).reshape(length // local_len, 16, width)
        resid = tok_s[here, :].astype(FLOAT) + dot(mix_s[here, :], wout_ref[...])
        xhat, scale = norm_stats(resid)
        dn = dn_s[...]
        gvec_ref[2:3, :] += col_sum(dn * xhat)
        gvec_ref[3:4, :] += col_sum(dn)
        d_branch = (cot_f + norm_back(dn, xhat, scale, g2)).astype(BFLOAT)
        dbr_s[here, :] = d_branch
        gout_ref[...] += t_dot(mix_s[here, :], d_branch)
        mix_s[here, :] = dot_t(d_branch, wout_ref[...]).astype(BFLOAT)

    @pl.loop(0, tiles)
    def phase_three(t):
        r0 = pl.multiple_of(t * tile, tile)
        here = pl.ds(r0, tile)

        @pl.loop(0, tile // 256)
        def attend(sub):
            for seq in range(256 // length):
                s0 = pl.multiple_of(r0 + sub * 256 + seq * length, length)
                rs = pl.ds(s0, length)
                for pack in range(packs):
                    c0 = pack * PACK
                    q = qkv_s[rs, c0 : c0 + PACK]
                    k = qkv_s[rs, width + c0 : width + c0 + PACK]
                    v = qkv_s[rs, 2 * width + c0 : 2 * width + c0 + PACK]
                    grad = mix_s[rs, c0 : c0 + PACK]
                    low = prob_s[rs, c0 : c0 + PACK]
                    probs = low.astype(FLOAT)
                    d_probs = dot_t(grad, block_diag(v)).astype(BFLOAT).astype(FLOAT)
                    centre = head_spread(head_reduce(probs * d_probs, jnp.sum, 0.0))
                    d_scores = (probs * (d_probs - centre)).astype(BFLOAT)
                    d_query = 0.125 * dot(d_scores, block_diag(k))
                    d_key = diag_rows(t_dot(d_scores, q))
                    d_value = diag_rows(t_dot(low, grad))
                    qkv_s[rs, c0 : c0 + PACK] = d_query.astype(BFLOAT)
                    qkv_s[rs, width + c0 : width + c0 + PACK] = d_key.astype(BFLOAT)
                    qkv_s[rs, 2 * width + c0 : 2 * width + c0 + PACK] = d_value.astype(BFLOAT)

        normed = n1_s[here, :]
        dn = jnp.zeros((tile, width), FLOAT)
        for part in range(3):
            cols = slice(part * width, (part + 1) * width)
            piece = qkv_s[here, cols]
            gqkv_ref[:, cols] += t_dot(normed, piece)
            dn += dot_t(piece, wqkv_ref[:, cols])
        xhat, scale = norm_stats(tok_s[here, :].astype(FLOAT))
        gvec_ref[0:1, :] += col_sum(dn * xhat)
        gvec_ref[1:2, :] += col_sum(dn)
        token_grad = (dbr_s[here, :].astype(FLOAT) + norm_back(dn, xhat, scale, g1)).astype(BFLOAT)
        gstem_ref[...] += t_dot(make_hot(r0), token_grad)
        for g in range(tile // group_rows):
            k0 = pl.multiple_of((t * (tile // group_rows) + g) * 16, 16)
            back = dot(perm_back(group_rows), token_grad[g * group_rows : (g + 1) * group_rows, :])
            tg_ref[:, pl.ds(k0, 16), :] = back.astype(BFLOAT).reshape(length // local_len, 16, width)


def run_compute(local_len, lat, mask, cot, stem, wqkv, wout, wup, wdown, vec, upb):
    rows, width = lat.shape[0], stem.shape[1]
    ff = wup.shape[1]
    group_rows = 16 // local_len * (cot.shape[0] * local_len)
    tile = max(TILE, group_rows)
    shape = jax.ShapeDtypeStruct
    vm = pl.BlockSpec(memory_space=pltpu.VMEM)
    return pl.pallas_call(
        functools.partial(compute_kernel, local_len),
        out_shape=(
            shape(cot.shape, BFLOAT),
            shape(cot.shape, BFLOAT),
            shape(stem.shape, FLOAT),
            shape(wqkv.shape, FLOAT),
            shape(wout.shape, FLOAT),
            shape(wup.shape, FLOAT),
            shape(wdown.shape, FLOAT),
            shape(vec.shape, FLOAT),
            shape(upb.shape, FLOAT),
        ),
        in_specs=[vm] * 10,
        out_specs=[vm] * 9,
        scratch_shapes=[
            pltpu.VMEM((rows, width), BFLOAT),
            pltpu.VMEM((rows, width), BFLOAT),
            pltpu.VMEM((rows, 3 * width), BFLOAT),
            pltpu.VMEM((rows, width), BFLOAT),
            pltpu.VMEM((rows, width), BFLOAT),
            pltpu.VMEM((rows, width), BFLOAT),
            pltpu.VMEM((tile, width), FLOAT),
            pltpu.VMEM((tile, width), FLOAT),
            pltpu.VMEM((tile, width), BFLOAT),
            pltpu.VMEM((tile, width), BFLOAT),
        ],
        compiler_params=pltpu.CompilerParams(vmem_limit_bytes=60 * 1024 * 1024),
    )(lat, mask, cot, stem, wqkv, wout, wup, wdown, vec, upb)


def per_device(
    latents,
    actions,
    segment_ids,
    cotangent,
    stem_weight,
    action_table,
    first_gain,
    first_bias,
    query_weight,
    key_weight,
    value_weight,
    out_weight,
    second_gain,
    second_bias,
    up_weight,
    up_bias,
    down_weight,
    down_bias,
):
    half_seqs, local_len, groups = latents.shape
    width = stem_weight.shape[1]
    places = lax.axis_size("gx")
    length = places * local_len
    seqs = half_seqs // places
    rows = seqs * length
    actions_n = action_table.shape[0]

    lat = jnp.concatenate([latents, actions[..., None]], axis=-1).astype(BFLOAT)
    lat = lat.reshape(places, seqs, local_len, groups + 1)
    lat = lax.all_to_all(lat, "gx", split_axis=0, concat_axis=0, tiled=True)
    lat = lat.transpose(1, 0, 2, 3).reshape(rows, groups + 1)
    lat = jnp.pad(lat, ((0, 0), (0, 128 - groups - 1)))
    cot = cotangent.reshape(places, seqs * local_len, width)
    cot = lax.all_to_all(cot, "gx", split_axis=0, concat_axis=0, tiled=True)
    first_seq = (lax.axis_index("gy") * places + lax.axis_index("gx")) * seqs
    seg = lax.dynamic_slice_in_dim(segment_ids, first_seq, seqs, 0)
    place = jnp.arange(length)
    allowed = (seg[:, :, None] == seg[:, None, :]) & (place[:, None] >= place[None, :])[None]
    mask = jnp.where(allowed, 0.0, -1e30).astype(BFLOAT).reshape(rows, length)
    mask = jnp.tile(mask, (1, PACK // length))
    stem = jnp.concatenate(
        [stem_weight, jnp.pad(action_table, ((0, HOT_PAD - actions_n), (0, 0)))], axis=0
    )
    gather = functools.partial(lax.all_gather, axis_name="gy", tiled=True)
    wqkv = jnp.concatenate(
        [gather(item, axis=1) for item in (query_weight, key_weight, value_weight)], axis=1
    )
    wout = gather(out_weight, axis=0)
    wup = gather(up_weight, axis=1)
    wdown = gather(down_weight, axis=0)
    upb = jnp.broadcast_to(gather(up_bias, axis=0)[None], (8, wup.shape[1]))
    vec = jnp.stack([first_gain, first_bias, second_gain, second_bias, down_bias] + [down_bias] * 3)
    out, tg, gstem, gqkv, gout, gup, gdown, gvec, gupb = run_compute(
        local_len, lat, mask, cot, stem, wqkv, wout, wup, wdown, vec, upb
    )
    out = lax.all_to_all(out, "gx", split_axis=0, concat_axis=0, tiled=True)
    tg = lax.all_to_all(tg, "gx", split_axis=0, concat_axis=0, tiled=True)
    out = out.reshape(half_seqs, local_len, width)
    tg = tg.reshape(half_seqs, local_len, width)
    both = ("gx", "gy")
    gstem, gvec = lax.psum((gstem, gvec), both)

    def shard(value, dim):
        return lax.psum(lax.psum_scatter(value, "gy", scatter_dimension=dim, tiled=True), "gx")

    gq = shard(gqkv[:, :width], 1)
    gk = shard(gqkv[:, width : 2 * width], 1)
    gv = shard(gqkv[:, 2 * width :], 1)
    return (
        out,
        tg,
        gstem[: groups * 32],
        gstem[groups * 32 : groups * 32 + actions_n],
        gvec[0],
        gvec[1],
        gq,
        gk,
        gv,
        shard(gout, 0),
        gvec[2],
        gvec[3],
        shard(gup, 1),
        shard(gupb[0], 0),
        shard(gdown, 0),
        gvec[4],
    )


def solution(mesh):
    return jax.shard_map(
        per_device,
        mesh=mesh,
        in_specs=(
            P("gy", "gx", None),
            P("gy", "gx"),
            P(),
            P("gy", "gx", None),
            P(),
            P(),
            P(),
            P(),
            P(None, "gy"),
            P(None, "gy"),
            P(None, "gy"),
            P("gy", None),
            P(),
            P(),
            P(None, "gy"),
            P("gy"),
            P("gy", None),
            P(),
        ),
        out_specs=(
            P("gy", "gx", None),
            P("gy", "gx", None),
            P(),
            P(),
            P(),
            P(),
            P(None, "gy"),
            P(None, "gy"),
            P(None, "gy"),
            P("gy", None),
            P(),
            P(),
            P(None, "gy"),
            P("gy"),
            P("gy", None),
            P(),
        ),
        check_vma=False,
    )
```

time: 1390 us -> 722 us (0.52)
  blocking collectives: 516 us -> 158 us
  local copies, waits for them, and re-layouts: 220 us -> 33.2 us
  matrix products: 136 us -> 0 us
  Pallas kernels: 0 us -> 102 us
  other arithmetic: 80.8 us -> 4.3 us
    unnamed x1, blocking collectives: 290 us -> 4.98 us
    reduce_scatter x0 -> x6, waiting for transfers between devices: none -> 193 us  [shard(): lax.psum_scatter(value, 'gy', scatter_dimension=dim, tiled=True)]
    dot_general x64 -> x0, matrix products: 136 us -> none  [the longest x8 36.4 us: product(): return jnp.dot(left, right, preferred_element_type=FLOAT)]
    all_to_all x3 -> x4, waiting for transfers between devices: 116 us -> 5.68 us  [the longest x1 5.67 us: per_device(): lat = lax.all_to_all(lat, 'gx', split_axis=0, concat_axis=0, tiled=True)]
    pallas_call x0 -> x1, Pallas kernels: none -> 102 us  [run_compute(): pl.pallas_call(functools.partial(compute_kernel, local_len), out_shape=(s...]
    all_to_all x1 -> x0, blocking collectives: 85.7 us -> none  [per_device(): lax.all_to_all(cot_all, 'gx', split_axis=0, concat_axis=1, tiled=True)]
    all_gather x0 -> x5, blocking collectives: none -> 53.9 us  [the longest x3 34.7 us: per_device(): gather(item, axis=1)]
    psum x4 -> x2, waiting for transfers between devices: 230 us -> 182 us  [the longest x1 137 us: shard(): lax.psum(lax.psum_scatter(value, 'gy', scatter_dimension=dim, tiled=True)...]
  transfers between devices with their start and end apart: 9 -> 14, of which waited for: 6 -> 10; matrix products, arithmetic and copies ran while one was open for 24% -> 3% of each run, Pallas kernels for 0% -> 0%
where the time goes in v1:
time: 722 us; the launch traced here: 721 us
  waiting for transfers between devices  386 us (53%)
  blocking collectives  158 us (22%)
  Pallas kernels  102 us (14%)
  local copies, waits for them, and re-layouts  33.2 us (5%)
  starting transfers between devices  22.7 us (3%)
  between operations  15.1 us (2%)
    reduce_scatter x6, waiting for transfers between devices, shard(): lax.psum_scatter(value, 'gy', scatter_dimension=dim, tiled=True)  193 us
    psum x1, waiting for transfers between devices, shard(): lax.psum(lax.psum_scatter(value, 'gy', scatter_dimension=dim, tiled=True)...  137 us
    pallas_call x1, Pallas kernels, run_compute(): pl.pallas_call(functools.partial(compute_kernel, local_len), out_shape=(s...  102 us
    psum x1, blocking collectives, shard(): lax.psum(lax.psum_scatter(value, 'gy', scatter_dimension=dim, tiled=True)...  54.7 us
    psum x1, waiting for transfers between devices, per_device(): gstem, gvec = lax.psum((gstem, gvec), both)  45 us
    psum x1, blocking collectives, per_device(): gstem, gvec = lax.psum((gstem, gvec), both)  44.2 us
    all_gather x3, blocking collectives, per_device(): gather(item, axis=1)  34.7 us
    all_gather x1, blocking collectives, per_device(): wout = gather(out_weight, axis=0)  14.8 us
  transfers between devices with their start and end apart: 14, of which 10 were waited for; matrix products, arithmetic and copies ran while one was open for 3% of the time, Pallas kernels for 0%

profile of v1, /device:TPU:0, one launch (start us, length us, event | category | flops | bytes accessed | tf_op | source)
XLA Modules:
  0.0 721.0 jit_solution(13004393739896737447)
XLA Ops:
  7.2 0.7 all-gather.3.cloned.1.call-update
  7.9 1.1 convert.8
  9.0 0.7 concatenate.15
  9.7 0.7 convert.9
  10.6 0.7 copy.40
  11.3 1.2 reshape.97
  12.4 7.4 %all-to-all-start = ((bf16[16,2,1584]{2,1,0:T(2,128)(2,1)}), bf16[16,2,1584]{2,1,0:T(2,128)(2,1)S(1)}, u32[]{:S(2)}, u32[]{:S(2)}) async-start(bf16[16,2,1584]{2,1,0:T(2,128)(2,1)} %reshape.97), calls=%async_computation | async-start | bytes 212992 | tf_op jit(solution)/shard_map/all_to_all | solution.py:377
  19.8 1.9 reshape.93
  21.7 5.7 all-to-all-done
  27.4 3.7 all-to-all-start.1
  31.1 0.7 all-gather.5.cloned.1.call-update
  32.1 0.3 eq.23
  32.3 0.2 eq.24
  32.8 0.3 and.17
  33.3 1.1 copy.43.mask_ref
  34.5 0.6 stack.26.vec_ref
  35.1 4.4 all_gather.27
  39.5 11.4 %all_gather.21 = bf16[512,512]{1,0:T(8,128)(2,1)S(1)} all-gather(bf16[512,256]{1,0:T(8,128)(2,1)S(1)} %copy-done.9), channel_id=1, replica_groups=mesh['gx'=16,'gy'=2] {'gy'}, dimensions={1}, use_global_device_ids=true | all-gather | bytes 786432 | tf_op jit(solution)/shard_map/all_gather | solution.py:393
  50.9 8.5 %all_gather.22 = bf16[512,512]{1,0:T(8,128)(2,1)S(1)} all-gather(bf16[512,256]{1,0:T(8,128)(2,1)S(1)} %copy-done.10), channel_id=1, replica_groups=mesh['gx'=16,'gy'=2] {'gy'}, dimensions={1}, use_global_device_ids=true | all-gather | bytes 786432 | tf_op jit(solution)/shard_map/all_gather | solution.py:393
  59.4 14.8 %all_gather.23 = bf16[512,512]{1,0:T(8,128)(2,1)S(1)} all-gather(bf16[512,256]{1,0:T(8,128)(2,1)} %param.28), channel_id=1, replica_groups=mesh['gx'=16,'gy'=2] {'gy'}, dimensions={1}, use_global_device_ids=true | all-gather | bytes 786432 | tf_op jit(solution)/shard_map/all_gather | solution.py:393
  74.2 14.8 %all_gather.24.wout_ref = bf16[512,512]{1,0:T(8,128)(2,1)} all-gather(bf16[256,512]{1,0:T(8,128)(2,1)} %param.29), channel_id=1, replica_groups=mesh['gx'=16,'gy'=2] {'gy'}, dimensions={0}, use_global_device_ids=true | all-gather | bytes 786432 | tf_op jit(solution)/shard_map/all_gather | solution.py:395
  89.0 1.1 fusion.1.stem_ref
  90.1 1.2 pad_maximum_fusion.wqkv_ref
  91.3 0.6 reshape.98
  92.0 0.2 copy.41
  92.2 0.8 pad.8.lat_ref
  93.0 1.0 all-gather.5.cloned.1.call-done.wdown_ref
  94.0 0.7 broadcast_in_dim.12.upb_ref
  94.7 0.5 copy-done.2
  95.2 101.6 %shard_map.297 = (bf16[16,96,512]{2,1,0:T(8,128)(2,1)}, bf16[16,96,512]{2,1,0:T(8,128)(2,1)}, f32[1152,512]{1,0:T(8,128)}, f32[512,1536]{1,0:T(8,128)}, f32[512,...) custom-call(bf16[1536,128]{1,0:T(8,128)(2,1)} %pad.8.lat_ref, ...), custom_call_target="tpu_custom_call" | custom-call | tf_op jit(solution)/shard_map/pallas_call | solution.py:316
  196.8 3.6 fusion.2
  200.4 0.5 reduce-scatter.7.cloned.1.call-update
  201.0 0.5 reduce-scatter.9.cloned.1.call-update
  201.6 0.5 reduce-scatter.13.cloned.1.call-update
  202.2 0.7 reduce-scatter.15.cloned.1.call-update
  202.9 0.7 reduce-scatter.17.cloned.1.call-update
  203.6 5.6 all-to-all-start.2
  209.3 0.7 all-reduce.7.cloned.1.call-update
  210.0 10.8 %reduce-scatter.11.cloned.1.call-done = f32[512,256]{1,0:T(8,128)} async-done(((f32[512,512]{1,0:T(8,128)}), f32[512,256]{1,0:T(8,128)}) %reduce-scatter.11.cloned.1.call-update) | async-done | bytes 524304 | tf_op jit(solution)/shard_map/reduce_scatter | solution.py:411
  220.8 23.1 %reduce-scatter.7.cloned.1.call-done = f32[512,256]{1,0:T(8,128)} async-done(((f32[512,512]{1,0:T(8,128)}), f32[512,256]{1,0:T(8,128)}) %reduce-scatter.7.cloned.1.call-update) | async-done | bytes 524304 | tf_op jit(solution)/shard_map/reduce_scatter | solution.py:411
  244.0 23.0 %reduce-scatter.9.cloned.1.call-done = f32[512,256]{1,0:T(8,128)} async-done(((f32[512,512]{1,0:T(8,128)}), f32[512,256]{1,0:T(8,128)}) %reduce-scatter.9.cloned.1.call-update) | async-done | bytes 524304 | tf_op jit(solution)/shard_map/reduce_scatter | solution.py:411
  267.0 22.5 %reduce-scatter.13.cloned.1.call-done = f32[256,512]{1,0:T(8,128)} async-done(((f32[512,512]{1,0:T(8,128)}), f32[256,512]{1,0:T(8,128)}) %reduce-scatter.13.cloned.1.call-update) | async-done | bytes 524304 | tf_op jit(solution)/shard_map/reduce_scatter | solution.py:411
  289.5 56.6 %reduce-scatter.15.cloned.1.call-done = f32[512,1024]{1,0:T(8,128)} async-done(((f32[512,2048]{1,0:T(8,128)}), f32[512,1024]{1,0:T(8,128)}) %reduce-scatter.15.cloned.1.call-update) | async-done | bytes 2097168 | tf_op jit(solution)/shard_map/reduce_scatter | solution.py:411
  346.1 56.7 %reduce-scatter.17.cloned.1.call-done = f32[1024,512]{1,0:T(8,128)} async-done(((f32[2048,512]{1,0:T(8,128)}), f32[1024,512]{1,0:T(8,128)}) %reduce-scatter.17.cloned.1.call-update) | async-done | bytes 2097168 | tf_op jit(solution)/shard_map/reduce_scatter | solution.py:411
  402.9 5.6 all-to-all-start.3
  408.6 0.6 dynamic-slice
  409.8 0.8 slice.42
  410.7 5.0 all-reduce.2
  415.6 54.7 %psum.70 = f32[1024]{0:T(1024)} all-reduce(f32[1024]{0:T(1024)S(1)} %dynamic-slice.1), channel_id=1, replica_groups=mesh['gx'=16,'gy'=2] {'gx'}, use_global_device_ids=true, to_apply=%region_13.14 | all-reduce | flops 1024 | bytes 8192 | tf_op jit(solution)/shard_map/psum | solution.py:411
  470.3 44.2 %psum.64 = f32[8,512]{1,0:T(8,128)S(1)} all-reduce(f32[8,512]{1,0:T(8,128)S(1)} %copy-done.13), channel_id=1, replica_groups=mesh['gx'=16,'gy'=2] {'gx','gy'}, use_global_device_ids=true, to_apply=%region_1.2 | all-reduce | flops 4096 | bytes 32768 | tf_op jit(solution)/shard_map/psum | solution.py:408
  514.6 0.6 fusion.3
  515.2 45.0 %all-reduce.7.cloned.1.call-done = f32[1152,512]{1,0:T(8,128)} async-done(((f32[1152,512]{1,0:T(8,128)}), f32[1152,512]{1,0:T(8,128)}) %all-reduce.7.cloned.1.call-update) | async-done | bytes 2359312 | tf_op jit(solution)/shard_map/psum | solution.py:408
  560.2 3.1 slice.44
  563.3 1.4 slice.45
  564.7 1.8 reshape.94
  566.5 1.8 reshape.95
  568.4 136.7 %all-reduce.9.cloned.1.call-done = (f32[512,256]{1,0:T(8,128)}, f32[512,256]{1,0:T(8,128)}, f32[512,256]{1,0:T(8,128)}, f32[256,512]{1,0:T(8,128)}, f32[512,1024]{1,0:T(8,128)}, /*index=5*/f32[1024,512]{1,0:T(8,128)}) async-done(((f32[512,256]{1,0:T(8,128)}, f32[512,256]{1,0:T(8,128)}, f32[512,256]{1,0:T(8,128)}, f32[256,512]{1,0:T(8,128)}, f32[512,1024]{1,0:T(8,128)}, /*index=5*/f32[1024,512]{1,0:T(8,128)}), ...) | async-done | bytes 6291472 | tf_op jit(solution)/shard_map/psum | solution.py:411
  705.0 2.0 copy.51
  707.1 1.9 copy.52
  708.9 0.8 copy.53
  709.7 0.8 copy.54
  710.5 1.3 copy.55
  711.8 1.0 copy-done.3
  712.9 1.3 copy.56
  (65 shorter events, 1.2 us)
Async XLA Ops:
  7.2 24.7 %copy-start = (s32[768,64]{0,1:T(8,128)S(1)}, s32[768,64]{0,1:T(8,128)}, u32[]{:S(2)}) copy-start(s32[768,64]{0,1:T(8,128)} %param.20) | copy-start | bytes 589828
  7.2 85.8 %all-gather.3.cloned.1.call-start = ((), (), s32[]{:S(2)}) async-start(), calls=%async_computation.10 | async-start | bytes 3145728 | tf_op jit(solution)/shard_map/all_gather | solution.py:396
  7.9 11.9 %copy-start.5 = (bf16[384,4,512]{2,1,0:T(4,128)(2,1)S(1)}, bf16[384,4,512]{2,1,0:T(4,128)(2,1)}, u32[]{:S(2)}) copy-start(bf16[384,4,512]{2,1,0:T(4,128)(2,1)} %param.21) | copy-start | bytes 4718596
  12.4 14.9 %all-to-all-start = ((bf16[16,2,1584]{2,1,0:T(2,128)(2,1)}), bf16[16,2,1584]{2,1,0:T(2,128)(2,1)S(1)}, u32[]{:S(2)}, u32[]{:S(2)}) async-start(bf16[16,2,1584]{2,1,0:T(2,128)(2,1)} %reshape.97), calls=%async_computation | async-start | bytes 212992 | tf_op jit(solution)/shard_map/all_to_all | solution.py:377
  27.4 66.6 %all-to-all-start.1 = ((bf16[16,96,512]{2,1,0:T(8,128)(2,1)}), bf16[16,96,512]{2,1,0:T(8,128)(2,1)S(1)}, u32[]{:S(2)}, u32[]{:S(2)}) async-start(bf16[16,96,512]{2,1,0:T(8,128)(2,1)} %reshape.93), calls=%async_computation.1 | async-start | bytes 3145728 | tf_op jit(solution)/shard_map/all_to_all | solution.py:381
  31.1 62.9 %all-gather.5.cloned.1.call-start = ((), (), s32[]{:S(2)}) async-start(), calls=%async_computation.11 | async-start | bytes 3145728 | tf_op jit(solution)/shard_map/all_gather | solution.py:397
  31.8 189.0 %reduce-scatter.11.cloned.1.call-start = ((), (), s32[]{:S(2)}) async-start(), calls=%async_computation.15 | async-start | bytes 1572864 | tf_op jit(solution)/shard_map/reduce_scatter | solution.py:411
  32.6 1.9 copy-start.11
  32.6 1.9 copy-start.15
  32.6 1.9 copy-start.16
  32.6 1.8 copy-start.17
  32.6 1.8 copy-start.18
  32.6 2.5 copy-start.14
  32.6 6.9 copy-start.9
  33.1 17.8 %copy-start.10 = (bf16[512,256]{1,0:T(8,128)(2,1)S(1)}, bf16[512,256]{1,0:T(8,128)(2,1)}, u32[]{:S(2)}) copy-start(bf16[512,256]{1,0:T(8,128)(2,1)} %param.27) | copy-start | bytes 786436
  33.3 55.7 %copy-start.12 = (bf16[18,512]{1,0:T(8,128)(2,1)S(1)}, bf16[18,512]{1,0:T(8,128)(2,1)}, u32[]{:S(2)}) copy-start(bf16[18,512]{1,0:T(8,128)(2,1)} %param.23) | copy-start | bytes 55300
  34.4 54.6 %copy-start.6 = (bf16[1024,512]{1,0:T(8,128)(2,1)S(1)}, bf16[1024,512]{1,0:T(8,128)(2,1)}, u32[]{:S(2)}) copy-start(bf16[1024,512]{1,0:T(8,128)(2,1)} %param.22) | copy-start | bytes 3145732
  94.0 1.2 copy-start.2
  200.4 43.6 %reduce-scatter.7.cloned.1.call-start = ((), (), s32[]{:S(2)}) async-start(), calls=%async_computation.13 | async-start | bytes 1572864 | tf_op jit(solution)/shard_map/reduce_scatter | solution.py:411
  201.0 66.0 %reduce-scatter.9.cloned.1.call-start = ((), (), s32[]{:S(2)}) async-start(), calls=%async_computation.14 | async-start | bytes 1572864 | tf_op jit(solution)/shard_map/reduce_scatter | solution.py:411
  201.5 88.0 %reduce-scatter.13.cloned.1.call-start = ((), (), s32[]{:S(2)}) async-start(), calls=%async_computation.16 | async-start | bytes 1572864 | tf_op jit(solution)/shard_map/reduce_scatter | solution.py:411
  202.1 144.0 %reduce-scatter.15.cloned.1.call-start = ((), (), s32[]{:S(2)}) async-start(), calls=%async_computation.17 | async-start | bytes 6291456 | tf_op jit(solution)/shard_map/reduce_scatter | solution.py:411
  202.9 200.0 %reduce-scatter.17.cloned.1.call-start = ((), (), s32[]{:S(2)}) async-start(), calls=%async_computation.18 | async-start | bytes 6291456 | tf_op jit(solution)/shard_map/reduce_scatter | solution.py:411
  203.6 199.3 %all-to-all-start.2 = ((bf16[16,96,512]{2,1,0:T(8,128)(2,1)}), bf16[16,96,512]{2,1,0:T(8,128)(2,1)S(1)}, u32[]{:S(2)}, u32[]{:S(2)}) async-start(bf16[16,96,512]{2,1,0:T(8,128)(2,1)} %get-tuple-element.25), calls=%async_computation.2 | async-start | bytes 3145728 | tf_op jit(solution)/shard_map/all_to_all | solution.py:403
  209.3 350.9 %all-reduce.7.cloned.1.call-start = ((), (), s32[]{:S(2)}) async-start(), calls=%async_computation.12 | async-start | bytes 4718592 | tf_op jit(solution)/shard_map/psum | solution.py:408
  210.0 495.0 %all-reduce.9.cloned.1.call-start = ((), (), s32[]{:S(2)}) async-start(), calls=%async_computation.19 | async-start | bytes 12582912 | tf_op jit(solution)/shard_map/psum | solution.py:411
  402.9 5.7 copy-start.19
  402.9 67.4 %copy-start.13 = (f32[8,512]{1,0:T(8,128)S(1)}, f32[8,512]{1,0:T(8,128)}, u32[]{:S(2)}) copy-start(f32[8,512]{1,0:T(8,128)} %get-tuple-element.28) | copy-start | bytes 49156
  402.9 163.6 %all-to-all-start.3 = ((bf16[16,96,512]{2,1,0:T(8,128)(2,1)}), bf16[16,96,512]{2,1,0:T(8,128)(2,1)S(1)}, u32[]{:S(2)}, u32[]{:S(2)}) async-start(bf16[16,96,512]{2,1,0:T(8,128)(2,1)} %get-tuple-element.26), calls=%async_computation.3 | async-start | bytes 3145728 | tf_op jit(solution)/shard_map/all_to_all | solution.py:404
  705.0 3.9 copy-start.8
  705.0 4.7 copy-start.7
  705.0 5.5 copy-start.4
  710.5 2.3 copy-start.3
  710.5 3.7 copy-start.1
Sparse Core Ops, SparseCore 0:
  9.6 38.6 all-gather.2
  49.9 44.0 all-gather.4
  200.5 20.3 reduce-scatter.10
  223.6 20.3 reduce-scatter.6
  246.6 20.3 reduce-scatter.8
  269.2 20.3 reduce-scatter.12
  291.8 54.2 reduce-scatter.14
  348.5 54.3 reduce-scatter.16
  408.4 151.7 all-reduce.6
  565.0 140.0 all-reduce.8

commit v2 on v1

v2 whole, which is shorter than its diff:
```python
import functools

import jax
import jax.numpy as jnp
from jax import lax
from jax.experimental import pallas as pl
from jax.experimental.pallas import tpu as pltpu
from jax.sharding import PartitionSpec as P

HD = 64
PACK = 256
EPSILON = 1e-05
FLOAT = jnp.float32
BFLOAT = jnp.bfloat16
TILE = 512
MAX_ROWS = 2048
VMEM_LIMIT = 60 * 1024 * 1024
UNIT = 4
FFB = 512
HOT_PAD = 128
GELU_C = 0.7978845608028654
GELU_A = 0.044715


def dot(left, right):
    return lax.dot_general(left, right, (((1,), (0,)), ((), ())), preferred_element_type=FLOAT)


def dot_t(left, right):
    return lax.dot_general(left, right, (((1,), (1,)), ((), ())), preferred_element_type=FLOAT)


def t_dot(left, right):
    return lax.dot_general(left, right, (((0,), (0,)), ((), ())), preferred_element_type=FLOAT)


def iota(shape, dim):
    return lax.broadcasted_iota(jnp.int32, shape, dim)


def norm_stats(values):
    average = jnp.mean(values, axis=-1, keepdims=True)
    centred = values - average
    spread = jnp.mean(centred * centred, axis=-1, keepdims=True)
    scale = lax.rsqrt(spread + EPSILON)
    return centred * scale, scale


def norm_back(grad, xhat, scale, gain):
    scaled = grad * gain
    mean_e = jnp.mean(scaled, axis=-1, keepdims=True)
    mean_x = jnp.mean(scaled * xhat, axis=-1, keepdims=True)
    return (scaled - mean_e - xhat * mean_x) * scale


def col_sum(values):
    return jnp.sum(values, axis=0, keepdims=True)


def head_reduce(values, op, fill):
    parts = []
    for half in range(PACK // 128):
        piece = values[:, half * 128 : (half + 1) * 128]
        low = iota(piece.shape, 1) < HD
        first = op(jnp.where(low, piece, fill), axis=-1, keepdims=True)
        second = op(jnp.where(low, fill, piece), axis=-1, keepdims=True)
        parts.append((low, first, second))
    return parts


def head_spread(parts):
    return jnp.concatenate([jnp.where(low, a, b) for low, a, b in parts], axis=1)


def block_diag(rows):
    mask = (iota((PACK, PACK), 0) // HD) == (iota((PACK, PACK), 1) // HD)
    return jnp.where(mask, jnp.concatenate([rows] * (PACK // HD), axis=0), jnp.zeros((), rows.dtype))


def diag_rows(full):
    lane_head = iota((HD, PACK), 1) // HD
    result = full[:HD]
    for head in range(1, PACK // HD):
        result = jnp.where(lane_head == head, full[head * HD : (head + 1) * HD], result)
    return result


def unrolled_loop(count, body):
    if count == 1:
        body(0)
    else:
        pl.loop(0, count)(body)


def row_maps(local_len, length, count, back):
    dest = iota((count, count), 1 if back else 0)
    src = iota((count, count), 0 if back else 1)
    want = ((dest % length) // local_len) * 16 + (dest // length) * local_len + dest % local_len
    return jnp.where(want == src, 1.0, 0.0).astype(BFLOAT)


def block_compute(local_len, refs, hooks):
    lat_ref, mask_ref, cot_ref, stem_ref, wqkv_ref, wout_ref, wup_ref, wdown_ref, vec_ref, upb_ref = refs["in"]
    out_ref, tg_ref = refs["stage"]
    gstem_ref, gqkv_ref, gout_ref, gup_ref, gdown_ref, gvec_ref = refs["grads"]
    tok_s, qkv_s, prob_s, mix_s, dbr_s, acc_s, dn_s, n2_s, cotp_s = refs["work"]
    rows, width = tok_s.shape
    places = cot_ref.shape[0]
    length = places * local_len
    packs = width // PACK
    group_rows = 16 // local_len * length
    tile = acc_s.shape[0]
    tiles = rows // tile
    groups = tile // group_rows
    ff = wup_ref.shape[1]
    hot_width = stem_ref.shape[0]
    classes = (hot_width - HOT_PAD) // 32

    def to_frames(ref, t, values):
        for g in range(groups):
            k0 = pl.multiple_of((t * groups + g) * 16, 16)
            back = dot(
                row_maps(local_len, length, group_rows, True),
                values[g * group_rows : (g + 1) * group_rows, :],
            )
            ref[:, pl.ds(k0, 16), :] = back.astype(BFLOAT).reshape(places, 16, width)

    def from_frames(ref, t):
        parts = []
        for g in range(groups):
            k0 = pl.multiple_of((t * groups + g) * 16, 16)
            raw = ref[:, pl.ds(k0, 16), :].reshape(group_rows, ref.shape[2])
            parts.append(dot(row_maps(local_len, length, group_rows, False), raw).astype(BFLOAT))
        return jnp.concatenate(parts, axis=0) if groups > 1 else parts[0]

    def make_hot(t):
        lats = from_frames(lat_ref, t)
        kk = lats.shape[1]
        parts = []
        for block in range(0, hot_width, 128):
            g = iota((kk, 128), 0)
            c = iota((kk, 128), 1) + block
            spread = jnp.where(jnp.minimum(c // classes, 32) == g, 1.0, 0.0).astype(BFLOAT)
            val = dot(lats, spread)
            lane = iota((tile, 128), 1)
            target = (lane + block) % classes if block < hot_width - HOT_PAD else lane
            parts.append(jnp.where(val == target.astype(FLOAT), 1.0, 0.0).astype(BFLOAT))
        return jnp.concatenate(parts, axis=1)

    def gvec_add(row, values):
        gvec_ref[row : row + 1, :] += values

    gstem_ref[...] = jnp.zeros_like(gstem_ref)
    gqkv_ref[...] = jnp.zeros_like(gqkv_ref)
    gout_ref[...] = jnp.zeros_like(gout_ref)
    gup_ref[...] = jnp.zeros_like(gup_ref)
    gdown_ref[...] = jnp.zeros_like(gdown_ref)
    gvec_ref[...] = jnp.zeros_like(gvec_ref)

    g1 = vec_ref[0:1, :]
    b1 = vec_ref[1:2, :]
    g2 = vec_ref[2:3, :]
    b2 = vec_ref[3:4, :]
    bd = vec_ref[4:5, :]

    hooks["start"]()

    @pl.loop(0, tiles)
    def phase_one(t):
        r0 = pl.multiple_of(t * tile, tile)
        here = pl.ds(r0, tile)
        hooks["lat_ready"](t)
        tokens = dot(make_hot(t), stem_ref[...]).astype(BFLOAT)
        tok_s[here, :] = tokens
        xhat, _ = norm_stats(tokens.astype(FLOAT))
        normed = (xhat * g1 + b1).astype(BFLOAT)
        hooks["qkv_ready"](t)
        for part in range(3):
            cols = slice(part * width, (part + 1) * width)
            value = dot(normed, wqkv_ref[:, cols])
            if part == 0:
                value = value.astype(BFLOAT).astype(FLOAT) * 0.125
            qkv_s[here, cols] = value.astype(BFLOAT)

        @pl.loop(0, tile // 256)
        def attend(sub):
            for seq0 in range(0, 256 // length, UNIT):
                units = []
                for seq in range(seq0, seq0 + UNIT):
                    s0 = pl.multiple_of(r0 + sub * 256 + seq * length, length)
                    units += [(pl.ds(s0, length), pack * PACK) for pack in range(packs)]
                qs = [block_diag(qkv_s[rs, c0 : c0 + PACK]) for rs, c0 in units]
                ks = [qkv_s[rs, width + c0 : width + c0 + PACK] for rs, c0 in units]
                scores = [dot_t(k, q) + mask_ref[rs, :].astype(FLOAT) for q, k, (rs, _) in zip(qs, ks, units)]
                es = [jnp.exp(x - jnp.max(x, axis=0, keepdims=True)) for x in scores]
                ps = [(e * (1.0 / jnp.sum(e, axis=0, keepdims=True))).astype(BFLOAT) for e in es]
                vs = [qkv_s[rs, 2 * width + c0 : 2 * width + c0 + PACK] for rs, c0 in units]
                ms = [diag_rows(t_dot(p, v)).astype(BFLOAT) for p, v in zip(ps, vs)]
                for p, m, (rs, c0) in zip(ps, ms, units):
                    prob_s[rs, c0 : c0 + PACK] = p
                    mix_s[rs, c0 : c0 + PACK] = m

    hooks["forward_done"]()

    @pl.loop(0, tiles)
    def phase_two(t):
        r0 = pl.multiple_of(t * tile, tile)
        here = pl.ds(r0, tile)
        resid = tok_s[here, :].astype(FLOAT) + dot(mix_s[here, :], wout_ref[...])
        xhat, scale = norm_stats(resid)
        n2_s[...] = (xhat * g2 + b2).astype(BFLOAT)
        hooks["cot_ready"](t)
        cotp_s[...] = from_frames(cot_ref, t)
        acc_s[...] = resid + bd
        dn_s[...] = jnp.zeros_like(dn_s)

        @pl.loop(0, ff // FFB)
        def feed(f):
            f0 = pl.multiple_of(f * FFB, FFB)
            fs = pl.ds(f0, FFB)
            n2 = n2_s[...]
            cot = cotp_s[...]
            up = wup_ref[:, fs]
            down = wdown_ref[fs, :]
            pre = dot(n2, up) + upb_ref[0:1, fs]
            square = pre * pre
            tanh = jnp.tanh(GELU_C * pre * (1.0 + GELU_A * square))
            half = 0.5 * (1.0 + tanh)
            hidden = (pre * half).astype(BFLOAT)
            slope = half + (0.5 * GELU_C) * pre * (1.0 - tanh * tanh) * (1.0 + 3.0 * GELU_A * square)
            acc_s[...] += dot(hidden, down)
            gdown_ref[fs, :] += t_dot(hidden, cot)
            d_pre = (dot_t(cot, down) * slope).astype(BFLOAT)
            sums = col_sum(d_pre.astype(FLOAT))
            for part in range(FFB // width):
                row = pl.multiple_of((f * (FFB // width) + part) * 16, 16)
                gvec_ref[pl.ds(row, 1), :] += sums[:, part * width : (part + 1) * width]
            gup_ref[:, fs] += t_dot(n2, d_pre)
            dn_s[...] += dot_t(d_pre, up)

        cot_f = cotp_s[...].astype(FLOAT)
        gvec_add(5, col_sum(cot_f))
        to_frames(out_ref, t, acc_s[...].astype(BFLOAT))
        hooks["out_ready"](t)
        resid = tok_s[here, :].astype(FLOAT) + dot(mix_s[here, :], wout_ref[...])
        xhat, scale = norm_stats(resid)
        dn = dn_s[...]
        gvec_add(3, col_sum(dn * xhat))
        gvec_add(4, col_sum(dn))
        d_branch = (cot_f + norm_back(dn, xhat, scale, g2)).astype(BFLOAT)
        dbr_s[here, :] = d_branch
        gout_ref[...] += t_dot(mix_s[here, :], d_branch)
        mix_s[here, :] = dot_t(d_branch, wout_ref[...]).astype(BFLOAT)

    hooks["feed_done"]()

    @pl.loop(0, tiles)
    def phase_three(t):
        r0 = pl.multiple_of(t * tile, tile)
        here = pl.ds(r0, tile)

        @pl.loop(0, tile // 256)
        def attend(sub):
            for seq0 in range(0, 256 // length, UNIT):
                units = []
                for seq in range(seq0, seq0 + UNIT):
                    s0 = pl.multiple_of(r0 + sub * 256 + seq * length, length)
                    units += [(pl.ds(s0, length), pack * PACK) for pack in range(packs)]
                gs = [block_diag(mix_s[rs, c0 : c0 + PACK]) for rs, c0 in units]
                vs = [qkv_s[rs, 2 * width + c0 : 2 * width + c0 + PACK] for rs, c0 in units]
                dps = [dot_t(v, g).astype(BFLOAT).astype(FLOAT) for v, g in zip(vs, gs)]
                lows = [prob_s[rs, c0 : c0 + PACK] for rs, c0 in units]
                ws = [low.astype(FLOAT) * dp for low, dp in zip(lows, dps)]
                dss = [
                    (w - low.astype(FLOAT) * jnp.sum(w, axis=0, keepdims=True)).astype(BFLOAT)
                    for w, low in zip(ws, lows)
                ]
                dvs = [dot(low, g).astype(BFLOAT) for low, g in zip(lows, gs)]
                ks = [qkv_s[rs, width + c0 : width + c0 + PACK] for rs, c0 in units]
                qs = [block_diag(qkv_s[rs, c0 : c0 + PACK]) for rs, c0 in units]
                dks = [dot(ds, q).astype(BFLOAT) for ds, q in zip(dss, qs)]
                dqs = [(0.125 * diag_rows(t_dot(ds, k))).astype(BFLOAT) for ds, k in zip(dss, ks)]
                for dq, dk, dv, (rs, c0) in zip(dqs, dks, dvs, units):
                    qkv_s[rs, c0 : c0 + PACK] = dq
                    qkv_s[rs, width + c0 : width + c0 + PACK] = dk
                    qkv_s[rs, 2 * width + c0 : 2 * width + c0 + PACK] = dv

        xhat, scale = norm_stats(tok_s[here, :].astype(FLOAT))
        normed = (xhat * g1 + b1).astype(BFLOAT)
        for part in range(3):
            cols = slice(part * width, (part + 1) * width)
            gqkv_ref[:, cols] += t_dot(normed, qkv_s[here, cols])
        dn = dot_t(qkv_s[here, :], wqkv_ref[...])
        gvec_add(1, col_sum(dn * xhat))
        gvec_add(2, col_sum(dn))
        token_grad = (dbr_s[here, :].astype(FLOAT) + norm_back(dn, xhat, scale, g1)).astype(BFLOAT)
        hooks["tg_room"](t)
        to_frames(tg_ref, t, token_grad)
        hooks["tg_ready"](t)
        gstem_ref[...] += t_dot(make_hot(t), token_grad)
        hooks["tile_done"](t)


def no_tile_hook(t):
    return None


def no_hook():
    return None


NO_HOOKS = {
    "lat_ready": no_tile_hook,
    "qkv_ready": no_tile_hook,
    "cot_ready": no_tile_hook,
    "out_ready": no_tile_hook,
    "tg_room": no_tile_hook,
    "tg_ready": no_tile_hook,
    "tile_done": no_tile_hook,
    "start": no_hook,
    "forward_done": no_hook,
    "feed_done": no_hook,
}


def work_shapes(rows, width, tile):
    return [
        pltpu.VMEM((rows, width), BFLOAT),
        pltpu.VMEM((rows, 3 * width), BFLOAT),
        pltpu.VMEM((rows, width), BFLOAT),
        pltpu.VMEM((rows, width), BFLOAT),
        pltpu.VMEM((rows, width), BFLOAT),
        pltpu.VMEM((tile, width), FLOAT),
        pltpu.VMEM((tile, width), FLOAT),
        pltpu.VMEM((tile, width), BFLOAT),
        pltpu.VMEM((tile, width), BFLOAT),
    ]


def local_kernel(local_len, *refs):
    block_compute(
        local_len,
        {"in": refs[:10], "stage": refs[10:12], "grads": refs[12:18], "work": refs[18:]},
        NO_HOOKS,
    )


def run_local(local_len, lat, mask, cot, stem, wqkv, wout, wup, wdown, vec, upb):
    places, per, width = cot.shape
    group_rows = 16 // local_len * (places * local_len)
    shape = jax.ShapeDtypeStruct
    vm = pl.BlockSpec(memory_space=pltpu.VMEM)
    return pl.pallas_call(
        functools.partial(local_kernel, local_len),
        out_shape=(
            shape(cot.shape, BFLOAT),
            shape(cot.shape, BFLOAT),
            shape(stem.shape, FLOAT),
            shape(wqkv.shape, FLOAT),
            shape(wout.shape, FLOAT),
            shape(wup.shape, FLOAT),
            shape(wdown.shape, FLOAT),
            shape((wup.shape[1] // width * 16, width), FLOAT),
        ),
        in_specs=[vm] * 10,
        out_specs=[vm] * 8,
        scratch_shapes=work_shapes(places * per, width, max(TILE, group_rows)),
        compiler_params=pltpu.CompilerParams(vmem_limit_bytes=60 * 1024 * 1024),
    )(lat, mask, cot, stem, wqkv, wout, wup, wdown, vec, upb)


def wait_for(ref, sem):
    pltpu.make_async_copy(ref, ref, sem).wait()


class Reducer:
    def __init__(self, where, pieces, bufs, final, sems):
        self.i, self.j, self.peer = where
        self.pieces = pieces
        self.send, self.r1, self.r2, self.r3, self.r4, self.r5, self.own, self.fin = bufs
        self.final = final
        self.ssem, self.rsem = sems
        self.half = self.own.shape[0]
        self.core = lax.rem(self.i, 2)

    def copy(self, n, src, dst, device):
        return pltpu.make_async_remote_copy(
            src_ref=src,
            dst_ref=dst,
            send_sem=self.ssem.at[n],
            recv_sem=self.rsem.at[n],
            device_id=device,
            device_id_type=pl.DeviceIdType.MESH,
        )

    def near(self, bit):
        step = 1 << bit
        return (self.i + step - 2 * step * lax.rem(self.i // step, 2), self.j)

    def bit(self, n):
        return lax.rem(self.i // (1 << n), 2)

    def start_core(self):
        for h in range(2):
            for at, take in self.pieces(h, 1 - self.core):
                self.send[h, at[0], at[1]] = take().astype(BFLOAT)
        self.copy(0, self.send, self.r1, self.near(0)).start()

    def core_to_x(self):
        self.copy(0, self.send, self.r1, self.near(0)).wait()
        for at, take in self.pieces(1 - self.j, self.core):
            arrived = self.r1[1 - self.j, at[0], at[1]].astype(FLOAT)
            self.send[0, at[0], at[1]] = (take() + arrived).astype(BFLOAT)
        self.copy(1, self.send.at[0], self.r2, (self.i, 1 - self.j)).start()
        for at, take in self.pieces(self.j, self.core):
            self.own[at[0], at[1]] = take() + self.r1[self.j, at[0], at[1]].astype(FLOAT)

    def region(self, level):
        start, count = 0, self.half
        for n in range(1, level + 1):
            count //= 2
            start = start + self.bit(n) * count
        return start, count

    def halving(self, level):
        start, count = self.region(level - 1)
        half = count // 2
        theirs = pl.multiple_of(start + (1 - self.bit(level)) * half, 16)
        mine = pl.multiple_of(start + self.bit(level) * half, 16)
        base = self.half - 2 * half
        src = self.send.at[1, base : base + half, :]
        return half, theirs, mine, base, self.copy(1 + level, src, (self.r3, self.r4, self.r5)[level - 1], self.near(level))

    def start_level(self, level):
        half, theirs, mine, base, copy = self.halving(level)
        self.send[1, base : base + half, :] = self.own[pl.ds(theirs, half), :].astype(BFLOAT)
        copy.start()

    def finish_level(self, level):
        half, theirs, mine, base, copy = self.halving(level)
        copy.wait()
        rows = pl.ds(mine, half)
        self.own[rows, :] += (self.r3, self.r4, self.r5)[level - 1][...].astype(FLOAT)

    def x_to_level(self):
        self.copy(1, self.send.at[0], self.r2, (self.i, 1 - self.j)).wait()
        self.own[...] += self.r2[...].astype(FLOAT)
        self.start_level(1)

    def next_level(self, level):
        self.finish_level(level)
        self.start_level(level + 1)

    def place(self, level):
        start, count = self.region(level)
        return self.final.at[self.core, pl.ds(pl.multiple_of(start, 16), count), :]

    def gather_copy(self, level):
        src = self.place(level)
        return self.copy(4 + level, src, src, self.near(level))

    def last_level(self):
        self.finish_level(3)
        start, count = self.region(3)
        self.fin[...] = self.own[pl.ds(pl.multiple_of(start, 16), count), :].astype(BFLOAT)
        keep = pltpu.make_async_copy(self.fin, self.place(3), self.ssem.at[8])
        keep.start()
        keep.wait()
        self.gather_copy(3).start()

    def gather(self, level):
        self.gather_copy(level).wait()
        self.gather_copy(level - 1).start()

    def core_gather(self):
        return self.copy(9, self.final.at[self.core], self.final.at[self.core], self.near(0))


def wide_kernel(local_len, *refs):
    (
        lat_hbm, mask_ref, cot_hbm, stem_ref, wq_hbm, wk_hbm, wv_hbm, wo_hbm, wup_hbm, wdown_hbm, vec_ref, upb_hbm,
        out_hbm, tg_hbm, feed_hbm, rest_hbm, shared_hbm,
        lat_s, frame_s, wqkv_s, wout_s, wup_s, wdown_s, upb_s,
        gstem_s, gqkv_s, gout_s, gup_s, gdown_s, gvec_s,
    ) = refs[:30]
    work = refs[30:37]
    feed_bufs = refs[37:45]
    rest_bufs = refs[45:51] + (gdown_s.at[0 : refs[45].shape[1], :],) + refs[51:52]
    tile = work[5].shape[0]
    own_s = feed_bufs[6]
    work = work[:5] + (own_s.at[0:tile, :], own_s.at[tile : 2 * tile, :]) + work[5:]
    (
        lat_send, lat_recv, cot_send, cot_recv, own_sem, out_send, out_recv, tg_send, tg_recv,
        w_local, wx_send, wx_recv, wc_send, wc_recv, fs_send, fs_recv, rs_send, rs_recv, sh_send, sh_recv,
    ) = refs[52:]
    i, j = lax.axis_index("gx"), lax.axis_index("gy")
    places = lax.axis_size("gx")
    core = lax.rem(i, 2)
    sibling = (i + 1 - 2 * core, j)
    across = (i, 1 - j)
    tiles = work[0].shape[0] // tile
    width = work[0].shape[1]
    per = tile // places
    mesh_id = pl.DeviceIdType.MESH

    def remote(src, dst, send, recv, device):
        return pltpu.make_async_remote_copy(
            src_ref=src, dst_ref=dst, send_sem=send, recv_sem=recv, device_id=device, device_id_type=mesh_id
        )

    barrier = pltpu.get_barrier_semaphore()

    @pl.loop(1, places)
    def greet(k):
        pl.semaphore_signal(barrier, inc=1, device_id=(lax.rem(i + k, places), j), device_id_type=mesh_id)

    pl.semaphore_signal(barrier, inc=1, device_id=across, device_id_type=mesh_id)
    pl.semaphore_wait(barrier, places)

    def chunk(t):
        return pl.ds(pl.multiple_of(t * per, per), per)

    def scatter(src, dst, t, send, recv):
        @pl.loop(1, places)
        def each(k):
            d = lax.rem(i + k, places)
            remote(src.at[d, chunk(t), :], dst.at[i, chunk(t), :], send, recv, (d, j)).start()

    def keep(src, dst, t, sem):
        return pltpu.make_async_copy(src.at[i, chunk(t), :], dst.at[i, chunk(t), :], sem)

    def most(ref, t):
        return ref.at[0 : places - 1, chunk(t), :]

    half = wq_hbm.shape[1]
    cols = [pl.multiple_of(part * width + j * half, half) for part in range(3)]
    far_cols = [pl.multiple_of(part * width + (1 - j) * half, half) for part in range(3)]

    def weight_views(owner, whole):
        def rows_of(count):
            return pl.ds(0, count) if whole else pl.ds(pl.multiple_of(core * (count // 2), 16), count // 2)

        views = []
        for part, src in enumerate((wq_hbm, wk_hbm, wv_hbm)):
            r = rows_of(width)
            at = pl.ds(pl.multiple_of(part * width + owner * half, half), half)
            views.append((src.at[r, :], wqkv_s.at[r, at]))
        count = wo_hbm.shape[0]
        r = rows_of(count)
        base = 0 if whole else core * (count // 2)
        size = count if whole else count // 2
        views.append((wo_hbm.at[r, :], wout_s.at[pl.ds(pl.multiple_of(owner * count + base, 16), size), :]))
        r = rows_of(width)
        count = wup_hbm.shape[1]
        views.append((wup_hbm.at[r, :], wup_s.at[r, pl.ds(pl.multiple_of(owner * count, 128), count)]))
        count = wdown_hbm.shape[0]
        r = rows_of(count)
        base = 0 if whole else core * (count // 2)
        size = count if whole else count // 2
        views.append((wdown_hbm.at[r, :], wdown_s.at[pl.ds(pl.multiple_of(owner * count + base, 16), size), :]))
        return views

    here_views = weight_views(j, True)
    x_copies = [
        remote(src, dst, wx_send.at[n], wx_recv.at[n], across) for n, (src, dst) in enumerate(weight_views(j, False))
    ]
    c_copies = [
        remote(dst, dst, wc_send.at[n], wc_recv.at[n], sibling)
        for n, (_, dst) in enumerate(weight_views(1 - j, False))
    ]
    own_copies = [pltpu.make_async_copy(src, dst, w_local.at[n]) for n, (src, dst) in enumerate(here_views)]
    ff_half = upb_hbm.shape[1]
    upb_at = pl.ds(pl.multiple_of(j * ff_half, 128), ff_half)
    upb_x = remote(upb_hbm, upb_s.at[:, upb_at], wx_send.at[6], wx_recv.at[6], across)
    upb_own = pltpu.make_async_copy(upb_hbm, upb_s.at[:, upb_at], w_local.at[6])

    for n in range(3):
        x_copies[n].start()

    @pl.loop(0, tiles)
    def send_lat(t):
        keep(lat_hbm, lat_s, t, own_sem.at[t]).start()
        scatter(lat_hbm, lat_s, t, lat_send, lat_recv.at[t])

    for n in range(3):
        own_copies[n].start()

    @pl.loop(0, tiles)
    def send_cot(t):
        keep(cot_hbm, frame_s, t, own_sem.at[tiles + t]).start()
        scatter(cot_hbm, frame_s, t, cot_send, cot_recv.at[t])

    upb_x.start()
    upb_own.start()
    for n in range(3, 6):
        x_copies[n].start()
        own_copies[n].start()

    def pass_on(first, last):
        for n in range(first, last):
            x_copies[n].wait()
            c_copies[n].start()

    def settle(first, last):
        for n in range(first, last):
            c_copies[n].wait()
            own_copies[n].wait()

    hooks = dict(NO_HOOKS)

    def lat_ready(t):
        keep(lat_hbm, lat_s, t, own_sem.at[t]).wait()
        wait_for(most(lat_s, t), lat_recv.at[t])

    def qkv_ready(t):
        @pl.when(t == 0)
        def _():
            pass_on(0, 3)
            settle(0, 3)

    def forward_done():
        pass_on(3, 6)
        upb_x.wait()
        upb_own.wait()
        settle(3, 6)

    def cot_ready(t):
        keep(cot_hbm, frame_s, t, own_sem.at[tiles + t]).wait()
        wait_for(most(frame_s, t), cot_recv.at[t])

    def out_ready(t):
        keep(frame_s, out_hbm, t, own_sem.at[2 * tiles + t]).start()
        scatter(frame_s, out_hbm, t, out_send.at[t], out_recv)

    def tg_room(t):
        keep(frame_s, out_hbm, t, own_sem.at[2 * tiles + t]).wait()
        wait_for(most(frame_s, t), out_send.at[t])

    def tg_ready(t):
        keep(frame_s, tg_hbm, t, own_sem.at[3 * tiles + t]).start()
        scatter(frame_s, tg_hbm, t, tg_send.at[t], tg_recv)

    def grab(ref, r0, nrows, c0, ncols):
        return lambda: ref[pl.ds(r0, nrows), pl.ds(c0, ncols)]

    def mult(value, by):
        return pl.multiple_of(value, by)

    up_half = gup_s.shape[1] // 2
    up_rows = width // 2
    down_rows = gdown_s.shape[0] // 4
    out_rows = gout_s.shape[0] // 4
    stem_rows = gstem_s.shape[0] // 4

    def feed_pieces(h, c):
        found, base = [], 0
        for block in range(up_half // width):
            found.append(
                (
                    (slice(base, base + up_rows), slice(None)),
                    grab(gup_s, mult(c * up_rows, 16), up_rows, mult(h * up_half + block * width, 128), width),
                )
            )
            base += up_rows
        found.append(
            (
                (slice(base, base + down_rows), slice(None)),
                grab(gdown_s, mult((h * 2 + c) * down_rows, 16), down_rows, 0, width),
            )
        )
        base += down_rows
        found.append(
            (
                (slice(base, base + out_rows), slice(None)),
                grab(gout_s, mult((h * 2 + c) * out_rows, 16), out_rows, 0, width),
            )
        )
        return found

    def rest_pieces(h, c):
        found, base = [], 0
        qrows = width // 2
        for part in range(2):
            found.append(
                (
                    (slice(0, qrows), slice(part * half, (part + 1) * half)),
                    grab(gqkv_s, mult(c * qrows, 16), qrows, mult(part * width + h * half, 128), half),
                )
            )
        base = qrows
        for part in range(2):
            found.append(
                (
                    (slice(base, base + qrows // 2), slice(part * half, (part + 1) * half)),
                    grab(gqkv_s, mult(c * qrows + part * (qrows // 2), 16), qrows // 2, mult(2 * width + h * half, 128), half),
                )
            )
        base += qrows // 2
        found.append(
            (
                (slice(base, base + stem_rows), slice(None)),
                grab(gstem_s, mult((h * 2 + c) * stem_rows, 16), stem_rows, 0, width),
            )
        )
        base += stem_rows
        found.append(
            ((slice(base, base + 16), slice(None)), grab(gvec_s, mult((h * 2 + c) * 16, 16), 16, 0, width))
        )
        base += 16
        end = rest_bufs[6].shape[0]
        found.append(
            ((slice(base, end), slice(None)), lambda base=base: jnp.zeros((end - base, width), FLOAT))
        )
        return found

    where = (i, j, places)
    feed = Reducer(where, feed_pieces, feed_bufs, feed_hbm, (fs_send, fs_recv))
    rest = Reducer(where, rest_pieces, rest_bufs, rest_hbm, (rs_send, rs_recv))

    def feed_done():
        feed.start_core()

    def tile_done(t):
        @pl.when(t == 0)
        def _():
            feed.core_to_x()

    hooks.update(
        lat_ready=lat_ready,
        qkv_ready=qkv_ready,
        forward_done=forward_done,
        cot_ready=cot_ready,
        out_ready=out_ready,
        tg_room=tg_room,
        tg_ready=tg_ready,
        feed_done=feed_done,
        tile_done=tile_done,
    )
    block_compute(
        local_len,
        {
            "in": (lat_s, mask_ref, frame_s, stem_ref, wqkv_s, wout_s, wup_s, wdown_s, vec_ref, upb_s),
            "stage": (frame_s, frame_s),
            "grads": (gstem_s, gqkv_s, gout_s, gup_s, gdown_s, gvec_s),
            "work": work,
        },
        hooks,
    )
    rest.start_core()
    rest.core_to_x()
    feed.x_to_level()
    feed.next_level(1)
    rest.x_to_level()
    feed.next_level(2)
    rest.next_level(1)
    feed.last_level()
    rest.next_level(2)
    feed.gather(3)
    rest.last_level()
    feed.gather(2)
    rest.gather(3)
    feed.gather_copy(1).wait()
    feed.core_gather().start()
    rest.gather(2)
    rest.gather_copy(1).wait()
    rest.core_gather().start()
    first = shared_hbm.shape[2]
    tail_at = rest.half - first
    tail = rest_hbm.at[core, tail_at : tail_at + first, :]
    mine = shared_hbm.at[j, core]
    to_x = remote(tail, mine, sh_send.at[0], sh_recv.at[0], across)
    to_x.start()
    stay = pltpu.make_async_copy(tail, mine, sh_send.at[2])
    stay.start()
    stay.wait()
    to_x.wait()
    to_core = remote(shared_hbm.at[:, core], shared_hbm.at[:, core], sh_send.at[1], sh_recv.at[1], sibling)
    to_core.start()
    feed.core_gather().wait()
    rest.core_gather().wait()
    to_core.wait()
    wait_for(lat_hbm.at[0 : places - 1], lat_send)
    wait_for(cot_hbm.at[0 : places - 1], cot_send)
    wait_for(out_hbm.at[0 : places - 1], out_recv)
    wait_for(tg_hbm.at[0 : places - 1], tg_recv)

    @pl.loop(0, tiles)
    def drain(t):
        keep(frame_s, tg_hbm, t, own_sem.at[3 * tiles + t]).wait()
        wait_for(most(frame_s, t), tg_send.at[t])


def reduce_shapes(half, width, own):
    return [
        pltpu.VMEM((2, half, width), BFLOAT),
        pltpu.VMEM((2, half, width), BFLOAT),
        pltpu.VMEM((half, width), BFLOAT),
        pltpu.VMEM((half // 2, width), BFLOAT),
        pltpu.VMEM((half // 4, width), BFLOAT),
        pltpu.VMEM((half // 8, width), BFLOAT),
    ] + [pltpu.VMEM((half, width), FLOAT)] * own + [pltpu.VMEM((half // 8, width), BFLOAT)]


def run_wide(local_len, lat, mask, cot, stem, wq, wk, wv, wo, wup, wdown, vec, upb):
    places, per, width = cot.shape
    rows = places * per
    ff = 2 * wup.shape[1]
    shape = jax.ShapeDtypeStruct
    vm = pl.BlockSpec(memory_space=pltpu.VMEM)
    hbm = pl.BlockSpec(memory_space=pl.ANY)
    feed_half = (width // 2) * (wup.shape[1] // width) + ff // 4 + width // 4
    rest_used = width // 2 + width // 4 + stem.shape[0] // 4 + 16
    rest_half = -(-rest_used // 128) * 128
    shared = rest_half - (width // 2 + width // 4)
    tiles = rows // TILE
    dma = pltpu.SemaphoreType.DMA
    return pl.pallas_call(
        functools.partial(wide_kernel, local_len),
        out_shape=(
            shape(cot.shape, BFLOAT),
            shape(cot.shape, BFLOAT),
            shape((2, feed_half, width), BFLOAT),
            shape((2, rest_half, width), BFLOAT),
            shape((2, 2, shared, width), BFLOAT),
        ),
        in_specs=[hbm, vm, hbm, vm, hbm, hbm, hbm, hbm, hbm, hbm, vm, hbm],
        out_specs=[hbm] * 5,
        scratch_shapes=[
            pltpu.VMEM(lat.shape, BFLOAT),
            pltpu.VMEM(cot.shape, BFLOAT),
            pltpu.VMEM((width, 3 * width), BFLOAT),
            pltpu.VMEM((width, width), BFLOAT),
            pltpu.VMEM((width, ff), BFLOAT),
            pltpu.VMEM((ff, width), BFLOAT),
            pltpu.VMEM((8, ff), FLOAT),
            pltpu.VMEM(stem.shape, FLOAT),
            pltpu.VMEM((width, 3 * width), FLOAT),
            pltpu.VMEM((width, width), FLOAT),
            pltpu.VMEM((width, ff), FLOAT),
            pltpu.VMEM((ff, width), FLOAT),
            pltpu.VMEM((ff // width * 16, width), FLOAT),
        ]
        + [item for n, item in enumerate(work_shapes(rows, width, TILE)) if n not in (5, 6)]
        + reduce_shapes(feed_half, width, 1)
        + reduce_shapes(rest_half, width, 0)
        + [
            dma,
            dma((tiles,)),
            dma,
            dma((tiles,)),
            dma((4 * tiles,)),
            dma((tiles,)),
            dma,
            dma((tiles,)),
            dma,
            dma((7,)),
            dma((7,)),
            dma((7,)),
            dma((6,)),
            dma((6,)),
            dma((10,)),
            dma((10,)),
            dma((10,)),
            dma((10,)),
            dma((3,)),
            dma((3,)),
        ],
        compiler_params=pltpu.CompilerParams(
            vmem_limit_bytes=VMEM_LIMIT, collective_id=0, has_side_effects=True
        ),
    )(lat, mask, cot, stem, wq, wk, wv, wo, wup, wdown, vec, upb)


def per_device(
    latents,
    actions,
    segment_ids,
    cotangent,
    stem_weight,
    action_table,
    first_gain,
    first_bias,
    query_weight,
    key_weight,
    value_weight,
    out_weight,
    second_gain,
    second_bias,
    up_weight,
    up_bias,
    down_weight,
    down_bias,
):
    half_seqs, local_len, groups = latents.shape
    width = stem_weight.shape[1]
    places = lax.axis_size("gx")
    length = places * local_len
    seqs = half_seqs // places
    rows = seqs * length
    actions_n = action_table.shape[0]

    lat = jnp.concatenate([latents, actions[..., None]], axis=-1).astype(BFLOAT)
    lat = lat.reshape(places, seqs * local_len, groups + 1)
    lat = jnp.pad(lat, ((0, 0), (0, 0), (0, 128 - groups - 1)))
    cot = cotangent.reshape(places, seqs * local_len, width)
    first_seq = (lax.axis_index("gy") * places + lax.axis_index("gx")) * seqs
    seg = lax.dynamic_slice_in_dim(segment_ids, first_seq, seqs, 0)
    place = jnp.arange(length)
    allowed = (seg[:, :, None] == seg[:, None, :]) & (place[:, None] >= place[None, :])[None]
    mask = jnp.where(allowed.swapaxes(1, 2), 0.0, -1e30).astype(BFLOAT).reshape(rows, length)
    mask = jnp.tile(mask, (1, PACK // length))
    stem = jnp.concatenate(
        [stem_weight, jnp.pad(action_table, ((0, HOT_PAD - actions_n), (0, 0)))], axis=0
    )
    vec = jnp.stack([first_gain, first_bias, second_gain, second_bias, down_bias] + [down_bias] * 3)
    if rows % TILE == 0 and rows <= MAX_ROWS and places == 16:
        upb = jnp.broadcast_to(up_bias[None], (8, up_bias.shape[0]))
        out, tg, feed, rest, shared = run_wide(
            local_len, lat, mask, cot, stem, query_weight, key_weight, value_weight,
            out_weight, up_weight, down_weight, vec, upb,
        )
        out = out.reshape(half_seqs, local_len, width)
        tg = tg.reshape(half_seqs, local_len, width)
        feed = feed.astype(FLOAT)
        rest = rest.astype(FLOAT)
        shared = shared.astype(FLOAT)
        half = width // 2
        cols = query_weight.shape[1]
        blocks = up_weight.shape[1] // width
        gup = jnp.concatenate([feed[:, b * half : (b + 1) * half] for b in range(blocks)], axis=2)
        gup = gup.reshape(up_weight.shape)
        base = blocks * half
        quarter = down_weight.shape[0] // 2
        gdown = feed[:, base : base + quarter].reshape(down_weight.shape)
        gout = feed[:, base + quarter :].reshape(out_weight.shape)
        gq = rest[:, :half, :cols].reshape(width, cols)
        gk = rest[:, :half, cols:].reshape(width, cols)
        part = rest[:, half : half + half // 2]
        gv = jnp.concatenate([part[:, :, :cols], part[:, :, cols:]], axis=1).reshape(width, cols)
        stem_rows = stem.shape[0] // 4
        gstem = shared[:, :, :stem_rows].reshape(stem.shape)
        first = shared[0, 0, stem_rows:]
        at = half + half // 2 + stem_rows
        return (
            out,
            tg,
            gstem[: groups * 32],
            gstem[groups * 32 : groups * 32 + actions_n],
            first[1],
            first[2],
            gq,
            gk,
            gv,
            gout,
            first[3],
            first[4],
            gup,
            rest[:, at].reshape(up_bias.shape),
            gdown,
            first[5],
        )
    lat = lax.all_to_all(lat, "gx", split_axis=0, concat_axis=0, tiled=True)
    cot = lax.all_to_all(cot, "gx", split_axis=0, concat_axis=0, tiled=True)
    gather = functools.partial(lax.all_gather, axis_name="gy", tiled=True)
    wqkv = jnp.concatenate(
        [gather(item, axis=1) for item in (query_weight, key_weight, value_weight)], axis=1
    )
    wout = gather(out_weight, axis=0)
    wup = gather(up_weight, axis=1)
    wdown = gather(down_weight, axis=0)
    upb = jnp.broadcast_to(gather(up_bias, axis=0)[None], (8, wup.shape[1]))
    out, tg, gstem, gqkv, gout, gup, gdown, gvec = run_local(
        local_len, lat, mask, cot, stem, wqkv, wout, wup, wdown, vec, upb
    )
    out = lax.all_to_all(out, "gx", split_axis=0, concat_axis=0, tiled=True)
    tg = lax.all_to_all(tg, "gx", split_axis=0, concat_axis=0, tiled=True)
    out = out.reshape(half_seqs, local_len, width)
    tg = tg.reshape(half_seqs, local_len, width)
    both = ("gx", "gy")
    gstem, gvec = lax.psum((gstem, gvec), both)
    upb_grad = gvec[::16].reshape(-1)
    upb_grad = lax.dynamic_slice_in_dim(upb_grad, lax.axis_index("gy") * up_bias.shape[0], up_bias.shape[0])

    def shard(value, dim):
        return lax.psum(lax.psum_scatter(value, "gy", scatter_dimension=dim, tiled=True), "gx")

    gq = shard(gqkv[:, :width], 1)
    gk = shard(gqkv[:, width : 2 * width], 1)
    gv = shard(gqkv[:, 2 * width :], 1)
    return (
        out,
        tg,
        gstem[: groups * 32],
        gstem[groups * 32 : groups * 32 + actions_n],
        gvec[1],
        gvec[2],
        gq,
        gk,
        gv,
        shard(gout, 0),
        gvec[3],
        gvec[4],
        shard(gup, 1),
        upb_grad,
        shard(gdown, 0),
        gvec[5],
    )


def solution(mesh):
    return jax.shard_map(
        per_device,
        mesh=mesh,
        in_specs=(
            P("gy", "gx", None),
            P("gy", "gx"),
            P(),
            P("gy", "gx", None),
            P(),
            P(),
            P(),
            P(),
            P(None, "gy"),
            P(None, "gy"),
            P(None, "gy"),
            P("gy", None),
            P(),
            P(),
            P(None, "gy"),
            P("gy"),
            P("gy", None),
            P(),
        ),
        out_specs=(
            P("gy", "gx", None),
            P("gy", "gx", None),
            P(),
            P(),
            P(),
            P(),
            P(None, "gy"),
            P(None, "gy"),
            P(None, "gy"),
            P("gy", None),
            P(),
            P(),
            P(None, "gy"),
            P("gy"),
            P("gy", None),
            P(),
        ),
        check_vma=False,
    )
```

time: 722 us -> 239 us (0.33)
  waiting for transfers between devices: 386 us -> 0 us
  blocking collectives: 158 us -> 0 us
  Pallas kernels: 102 us -> 206 us
  starting transfers between devices: 22.7 us -> 0 us
  between operations: 15.1 us -> 0.8 us
  local copies, waits for them, and re-layouts: 33.2 us -> 24.8 us
    reduce_scatter x6 -> x0, waiting for transfers between devices: 193 us -> none  [shard(): lax.psum_scatter(value, 'gy', scatter_dimension=dim, tiled=True)]
    psum x2 -> x0, waiting for transfers between devices: 182 us -> none  [the longest x1 137 us: shard(): lax.psum(lax.psum_scatter(value, 'gy', scatter_dimension=dim, tiled=True)...]
    pallas_call x1, Pallas kernels: 102 us -> 206 us  [run_wide(): pl.pallas_call(functools.partial(wide_kernel, local_len), out_shape=(shap...]
    psum x2 -> x0, blocking collectives: 98.9 us -> none  [the longest x1 54.7 us: shard(): lax.psum(lax.psum_scatter(value, 'gy', scatter_dimension=dim, tiled=True)...]
    all_gather x5 -> x0, blocking collectives: 53.9 us -> none  [the longest x3 34.7 us: per_device(): gather(item, axis=1)]
    all_to_all x4 -> x0, starting transfers between devices: 22.4 us -> none  [the longest x1 7.39 us: per_device(): lat = lax.all_to_all(lat, 'gx', split_axis=0, concat_axis=0, tiled=True)]
    unnamed x50 -> x12, local copies, waits for them, and re-layouts: 12.1 us -> 0.03 us
  transfers between devices with their start and end apart: 14 -> 0, of which waited for: 10 -> 0; matrix products, arithmetic and copies ran while one was open for 3% -> 0% of each run, Pallas kernels for 0% -> 0%
where the time goes in v2:
time: 239 us
  Pallas kernels  206 us (86%)
  local copies, waits for them, and re-layouts  24.8 us (10%)
  other arithmetic  7.4 us (3%)
    pallas_call x1, Pallas kernels, run_wide(): pl.pallas_call(functools.partial(wide_kernel, local_len), out_shape=(shap...  206 us

profile of v2, /device:TPU:0, one launch (start us, length us, event | category | flops | bytes accessed | tf_op | source)
XLA Modules:
  0.0 238.8 jit_solution(7261477958138438180)
XLA Ops:
  0.6 0.0 copy-start
  0.7 0.7 convert.9
  1.4 1.5 stack.26.refs_10_
  2.9 0.0 copy-done
  2.9 0.1 constant_dynamic-slice_fusion
  3.0 0.1 copy.56
  3.0 0.1 eq.24
  3.1 1.3 broadcast_in_dim.12.refs_11_
  4.4 0.2 copy.54
  4.6 1.0 convert.8
  5.6 0.1 and.17
  5.6 0.3 and.18
  5.9 0.3 copy.53
  6.2 0.2 concatenate.24
  6.4 1.0 fusion.4.refs_0_
  7.4 0.3 eq.22
  7.7 0.2 eq.23
  7.9 0.0 copy-start.5
  7.9 0.1 select_convert_fusion
  8.0 0.1 tile.8
  8.1 0.0 copy-start.4
  8.1 1.2 copy.57.refs_1_
  9.2 0.0 copy-done.5
  9.2 2.3 fusion.1.refs_3_
  11.5 0.0 copy-done.4
  11.5 1.8 reshape.120.refs_2_
  13.4 205.8 %shard_map.297 = (bf16[16,96,512]{2,1,0:T(8,128)(2,1)}, bf16[16,96,512]{2,1,0:T(8,128)(2,1)}, bf16[2,1152,512]{2,1,0:T(8,128)(2,1)}, bf16[2,768,512]{2,1,0:T(8,128)(2,1)}, bf16[2,2,384,512]{3,2,1,0:T(8,128)(2,1)}) custom-call(bf16[16,96,128]{2,1,0:T(8,128)(2,1)} %fusion.4.refs_0_, bf16[1536,256]{1,0:T(8,128)(2,1)} %copy.57.refs_1_, ...), custom_call_target="tpu_custom_call" | custom-call | tf_op jit(solution)/shard_map/pallas_call | solution.py:817
  219.2 0.0 copy-start.1
  219.2 3.6 %reshape.121 = bf16[384,4,512]{2,1,0:T(4,128)(2,1)} reshape(bf16[16,96,512]{2,1,0:T(8,128)(2,1)} %get-tuple-element.21) | data formatting | bytes 3145728 | tf_op jit(solution)/shard_map/reshape | solution.py:922
  222.8 0.0 copy-start.3
  222.9 1.4 slice.96
  224.3 1.5 fusion.6
  225.8 0.0 copy-done.1
  225.8 0.9 slice.91
  226.6 1.0 fusion.7
  227.6 0.0 copy-done.3
  227.6 0.0 copy-start.2
  227.7 1.1 fusion.8
  228.7 0.8 pad_maximum_fusion.1
  229.5 0.0 copy-done.2
  229.5 0.3 slice.82
  229.9 0.6 slice.84
  230.5 1.5 slice.83
  232.0 3.5 %reshape.122 = bf16[384,4,512]{2,1,0:T(4,128)(2,1)} reshape(bf16[16,96,512]{2,1,0:T(8,128)(2,1)} %get-tuple-element.22) | data formatting | bytes 3145728 | tf_op jit(solution)/shard_map/reshape | solution.py:923
  235.5 1.6 slice.97
  237.1 0.3 fusion.5
  237.4 1.5 pad_maximum_fusion
  (1 shorter events, 0.0 us)
Async XLA Ops:
  0.6 2.2 copy-start
  7.9 1.3 copy-start.5
  8.1 3.5 %copy-start.4 = (bf16[384,4,512]{2,1,0:T(4,128)(2,1)S(1)}, bf16[384,4,512]{2,1,0:T(4,128)(2,1)}, u32[]{:S(2)}) copy-start(bf16[384,4,512]{2,1,0:T(4,128)(2,1)} %param.21) | copy-start | bytes 4718596
  219.2 6.6 %copy-start.1 = (bf16[2,1152,512]{2,1,0:T(8,128)(2,1)S(1)}, bf16[2,1152,512]{2,1,0:T(8,128)(2,1)}, u32[]{:S(2)}) copy-start(bf16[2,1152,512]{2,1,0:T(8,128)(2,1)} %get-tuple-element.25) | copy-start | bytes 7077892
  222.8 4.8 %copy-start.3 = (bf16[2,768,512]{2,1,0:T(8,128)(2,1)S(1)}, bf16[2,768,512]{2,1,0:T(8,128)(2,1)}, u32[]{:S(2)}) copy-start(bf16[2,768,512]{2,1,0:T(8,128)(2,1)} %get-tuple-element.24) | copy-start | bytes 4718596
  227.6 1.9 copy-start.2

commit v3 on v2

v3 whole, which is shorter than its diff:
```python
import functools

import jax
import jax.numpy as jnp
from jax import lax
from jax.experimental import pallas as pl
from jax.experimental.pallas import tpu as pltpu
from jax.sharding import PartitionSpec as P

HD = 64
PACK = 256
EPSILON = 1e-05
FLOAT = jnp.float32
BFLOAT = jnp.bfloat16
TILE = 512
MAX_ROWS = 2048
VMEM_LIMIT = 60 * 1024 * 1024
UNIT = 4
SUB = 512
FFB = 512
HOT_PAD = 128
GELU_C = 0.7978845608028654
GELU_A = 0.044715


def dot(left, right):
    return lax.dot_general(left, right, (((1,), (0,)), ((), ())), preferred_element_type=FLOAT)


def dot_t(left, right):
    return lax.dot_general(left, right, (((1,), (1,)), ((), ())), preferred_element_type=FLOAT)


def t_dot(left, right):
    return lax.dot_general(left, right, (((0,), (0,)), ((), ())), preferred_element_type=FLOAT)


def iota(shape, dim):
    return lax.broadcasted_iota(jnp.int32, shape, dim)


def norm_stats(values):
    average = jnp.mean(values, axis=-1, keepdims=True)
    centred = values - average
    spread = jnp.mean(centred * centred, axis=-1, keepdims=True)
    scale = lax.rsqrt(spread + EPSILON)
    return centred * scale, scale


def norm_back(grad, xhat, scale, gain):
    scaled = grad * gain
    mean_e = jnp.mean(scaled, axis=-1, keepdims=True)
    mean_x = jnp.mean(scaled * xhat, axis=-1, keepdims=True)
    return (scaled - mean_e - xhat * mean_x) * scale


def col_sum(values):
    return jnp.sum(values, axis=0, keepdims=True)


def head_reduce(values, op, fill):
    parts = []
    for half in range(PACK // 128):
        piece = values[:, half * 128 : (half + 1) * 128]
        low = iota(piece.shape, 1) < HD
        first = op(jnp.where(low, piece, fill), axis=-1, keepdims=True)
        second = op(jnp.where(low, fill, piece), axis=-1, keepdims=True)
        parts.append((low, first, second))
    return parts


def head_spread(parts):
    return jnp.concatenate([jnp.where(low, a, b) for low, a, b in parts], axis=1)


def block_diag(rows):
    mask = (iota((PACK, PACK), 0) // HD) == (iota((PACK, PACK), 1) // HD)
    return jnp.where(mask, jnp.concatenate([rows] * (PACK // HD), axis=0), jnp.zeros((), rows.dtype))


def diag_rows(full):
    lane_head = iota((HD, PACK), 1) // HD
    result = full[:HD]
    for head in range(1, PACK // HD):
        result = jnp.where(lane_head == head, full[head * HD : (head + 1) * HD], result)
    return result


def unrolled_loop(count, body):
    if count == 1:
        body(0)
    else:
        pl.loop(0, count)(body)


def row_maps(local_len, length, count, back):
    dest = iota((count, count), 1 if back else 0)
    src = iota((count, count), 0 if back else 1)
    want = ((dest % length) // local_len) * 16 + (dest // length) * local_len + dest % local_len
    return jnp.where(want == src, 1.0, 0.0).astype(BFLOAT)


def block_compute(local_len, refs, hooks):
    lat_ref, seg_ref, cot_ref, stem_ref, wqkv_ref, wout_ref, wup_ref, wdown_ref, upb_ref = refs["in"]
    out_ref, tg_ref = refs["stage"]
    gstem_ref, gqkv_ref, gout_ref, gup_ref, gdown_ref, gvec_ref = refs["grads"]
    tok_s, qkv_s, prob_s, mix_s, dbr_s, acc_s, dn_s, n2_s, cotp_s = refs["work"]
    rows, width = tok_s.shape
    places = cot_ref.shape[0]
    length = places * local_len
    packs = width // PACK
    group_rows = 16 // local_len * length
    tile = acc_s.shape[0]
    tiles = rows // tile
    groups = tile // group_rows
    ff = wup_ref.shape[1]
    hot_width = stem_ref.shape[0]
    classes = (hot_width - HOT_PAD) // 32

    def to_frames(ref, t, values):
        for g in range(groups):
            k0 = pl.multiple_of((t * groups + g) * 16, 16)
            back = dot(
                row_maps(local_len, length, group_rows, True),
                values[g * group_rows : (g + 1) * group_rows, :],
            )
            ref[:, pl.ds(k0, 16), :] = back.astype(BFLOAT).reshape(places, 16, width)

    def from_frames(ref, t):
        parts = []
        for g in range(groups):
            k0 = pl.multiple_of((t * groups + g) * 16, 16)
            raw = ref[:, pl.ds(k0, 16), :].reshape(group_rows, ref.shape[2])
            parts.append(dot(row_maps(local_len, length, group_rows, False), raw).astype(BFLOAT))
        return jnp.concatenate(parts, axis=0) if groups > 1 else parts[0]

    pairs = refs["pairs"]
    lat_rows = tile // places // pairs
    slot = lat_ref.shape[2] // pairs

    def make_hot(t):
        k0 = pl.multiple_of(t * lat_rows, lat_rows)
        raw = lat_ref[:, pl.ds(k0, lat_rows), :].reshape(places * lat_rows, lat_ref.shape[2])
        dest = iota((tile, places * lat_rows), 0)
        src = iota((tile, places * lat_rows), 1)
        frame = dest % local_len
        want = ((dest % length) // local_len) * lat_rows
        want += (dest // length) * (local_len // pairs) + frame // pairs
        lats = dot(jnp.where(want == src, 1.0, 0.0).astype(BFLOAT), raw)
        if pairs > 1:
            turn = iota(lats.shape, 0) % pairs
            lats = jnp.where(iota(lats.shape, 1) // slot == turn, lats, 0.0)
        lats = lats.astype(BFLOAT)
        parts = []
        for block in range(0, hot_width, 128):
            g = iota((lats.shape[1], 128), 0) % slot
            c = iota((lats.shape[1], 128), 1) + block
            spread = jnp.where(jnp.minimum(c // classes, 32) == g, 1.0, 0.0).astype(BFLOAT)
            val = dot(lats, spread)
            lane = iota((tile, 128), 1)
            target = (lane + block) % classes if block < hot_width - HOT_PAD else lane
            parts.append(jnp.where(val == target.astype(FLOAT), 1.0, 0.0).astype(BFLOAT))
        return jnp.concatenate(parts, axis=1)

    def gvec_add(row, values):
        gvec_ref[row : row + 1, :] += values

    gstem_ref[...] = jnp.zeros_like(gstem_ref)
    gqkv_ref[...] = jnp.zeros_like(gqkv_ref)
    gout_ref[...] = jnp.zeros_like(gout_ref)
    gup_ref[...] = jnp.zeros_like(gup_ref)
    gdown_ref[...] = jnp.zeros_like(gdown_ref)
    gvec_ref[...] = jnp.zeros_like(gvec_ref)

    g1, b1, g2, b2, bd = [ref[...] for ref in refs["vec"]]

    def seg_bias(seq):
        row = seg_ref[pl.ds(seq, 1), :]
        lane = iota((length, PACK), 1) % length
        key = iota((length, PACK), 0)
        first = jnp.broadcast_to(row[:, :128], (length, 128))
        pick = iota((length, 128), 0) == iota((length, 128), 1)
        column = jnp.sum(jnp.where(pick, first, 0.0), axis=1, keepdims=True)
        return jnp.where((column == row) & (key <= lane), 0.0, -1e30)

    hooks["start"]()

    @pl.loop(0, tiles)
    def phase_zero(t):
        hooks["lat_ready"](t)
        r0 = pl.multiple_of(t * tile, tile)
        tok_s[pl.ds(r0, tile), :] = dot(make_hot(t), stem_ref[...]).astype(BFLOAT)
        hooks["stem_done"](t)

    @pl.loop(0, packs)
    def phase_one(turn):
        pack = lax.rem(turn + refs["own"], packs)

        @pl.loop(0, tiles)
        def each(t):
            r0 = pl.multiple_of(t * tile, tile)
            here = pl.ds(r0, tile)
            xhat, _ = norm_stats(tok_s[here, :].astype(FLOAT))
            normed = (xhat * g1 + b1).astype(BFLOAT)
            col0 = pl.multiple_of(pack * PACK, PACK)
            cols = [pl.ds(pl.multiple_of(part * width + pack * PACK, PACK), PACK) for part in range(3)]
            for part in range(3):
                value = dot(normed, wqkv_ref[:, cols[part]])
                if part == 0:
                    value = value.astype(BFLOAT).astype(FLOAT) * 0.125
                qkv_s[here, cols[part]] = value.astype(BFLOAT)

            @pl.loop(0, tile // SUB)
            def attend(sub):
                units, bias = [], []
                for seq in range(SUB // length):
                    s0 = pl.multiple_of(r0 + sub * SUB + seq * length, length)
                    units.append(pl.ds(s0, length))
                    bias.append(seg_bias(t * (tile // length) + sub * (SUB // length) + seq))
                qs = [block_diag(qkv_s[rs, cols[0]]) for rs in units]
                ks = [qkv_s[rs, cols[1]] for rs in units]
                scores = [dot_t(k, q) + b for q, k, b in zip(qs, ks, bias)]
                es = [jnp.exp(x - jnp.max(x, axis=0, keepdims=True)) for x in scores]
                ps = [(e * (1.0 / jnp.sum(e, axis=0, keepdims=True))).astype(BFLOAT) for e in es]
                vs = [qkv_s[rs, cols[2]] for rs in units]
                ms = [diag_rows(t_dot(p, v)).astype(BFLOAT) for p, v in zip(ps, vs)]
                for p, m, rs in zip(ps, ms, units):
                    prob_s[rs, pl.ds(col0, PACK)] = p
                    mix_s[rs, pl.ds(col0, PACK)] = m

            hooks["attend_done"](turn, t)

    hooks["forward_done"]()

    @pl.loop(0, tiles)
    def phase_two(t):
        r0 = pl.multiple_of(t * tile, tile)
        here = pl.ds(r0, tile)
        resid = tok_s[here, :].astype(FLOAT) + dot(mix_s[here, :], wout_ref[...])
        xhat, scale = norm_stats(resid)
        n2_s[...] = (xhat * g2 + b2).astype(BFLOAT)
        hooks["cot_ready"](t)
        cotp_s[...] = from_frames(cot_ref, t)
        acc_s[...] = resid + bd
        dn_s[...] = jnp.zeros_like(dn_s)

        @pl.loop(0, ff // FFB)
        def feed(turn):
            hooks["feed_block"](t, turn)
            blocks = ff // FFB
            f = lax.rem(turn + refs["own"] * (blocks // 2), blocks)
            f0 = pl.multiple_of(f * FFB, FFB)
            fs = pl.ds(f0, FFB)
            n2 = n2_s[...]
            cot = cotp_s[...]
            up = wup_ref[:, fs]
            down = wdown_ref[fs, :]
            pre = dot(n2, up) + upb_ref[0:1, fs]
            square = pre * pre
            tanh = jnp.tanh(GELU_C * pre * (1.0 + GELU_A * square))
            half = 0.5 * (1.0 + tanh)
            hidden = (pre * half).astype(BFLOAT)
            slope = half + (0.5 * GELU_C) * pre * (1.0 - tanh * tanh) * (1.0 + 3.0 * GELU_A * square)
            acc_s[...] += dot(hidden, down)
            gdown_ref[fs, :] += t_dot(hidden, cot)
            d_pre = (dot_t(cot, down) * slope).astype(BFLOAT)
            sums = col_sum(d_pre.astype(FLOAT))
            for part in range(FFB // width):
                row = pl.multiple_of((f * (FFB // width) + part) * 16, 16)
                gvec_ref[pl.ds(row, 1), :] += sums[:, part * width : (part + 1) * width]
            gup_ref[:, fs] += t_dot(n2, d_pre)
            dn_s[...] += dot_t(d_pre, up)

        cot_f = cotp_s[...].astype(FLOAT)
        gvec_add(5, col_sum(cot_f))
        to_frames(out_ref, t, acc_s[...].astype(BFLOAT))
        hooks["out_ready"](t)
        resid = tok_s[here, :].astype(FLOAT) + dot(mix_s[here, :], wout_ref[...])
        xhat, scale = norm_stats(resid)
        dn = dn_s[...]
        gvec_add(3, col_sum(dn * xhat))
        gvec_add(4, col_sum(dn))
        d_branch = (cot_f + norm_back(dn, xhat, scale, g2)).astype(BFLOAT)
        dbr_s[here, :] = d_branch
        gout_ref[...] += t_dot(mix_s[here, :], d_branch)
        mix_s[here, :] = dot_t(d_branch, wout_ref[...]).astype(BFLOAT)

    hooks["feed_done"]()

    @pl.loop(0, tiles)
    def phase_three(t):
        r0 = pl.multiple_of(t * tile, tile)
        here = pl.ds(r0, tile)

        @pl.loop(0, tile // 256)
        def attend(sub):
            for seq0 in range(0, 256 // length, UNIT):
                units = []
                for seq in range(seq0, seq0 + UNIT):
                    s0 = pl.multiple_of(r0 + sub * 256 + seq * length, length)
                    units += [(pl.ds(s0, length), pack * PACK) for pack in range(packs)]
                gs = [block_diag(mix_s[rs, c0 : c0 + PACK]) for rs, c0 in units]
                vs = [qkv_s[rs, 2 * width + c0 : 2 * width + c0 + PACK] for rs, c0 in units]
                dps = [dot_t(v, g).astype(BFLOAT).astype(FLOAT) for v, g in zip(vs, gs)]
                lows = [prob_s[rs, c0 : c0 + PACK] for rs, c0 in units]
                ws = [low.astype(FLOAT) * dp for low, dp in zip(lows, dps)]
                dss = [
                    (w - low.astype(FLOAT) * jnp.sum(w, axis=0, keepdims=True)).astype(BFLOAT)
                    for w, low in zip(ws, lows)
                ]
                dvs = [dot(low, g).astype(BFLOAT) for low, g in zip(lows, gs)]
                ks = [qkv_s[rs, width + c0 : width + c0 + PACK] for rs, c0 in units]
                qs = [block_diag(qkv_s[rs, c0 : c0 + PACK]) for rs, c0 in units]
                dks = [dot(ds, q).astype(BFLOAT) for ds, q in zip(dss, qs)]
                dqs = [(0.125 * diag_rows(t_dot(ds, k))).astype(BFLOAT) for ds, k in zip(dss, ks)]
                for dq, dk, dv, (rs, c0) in zip(dqs, dks, dvs, units):
                    qkv_s[rs, c0 : c0 + PACK] = dq
                    qkv_s[rs, width + c0 : width + c0 + PACK] = dk
                    qkv_s[rs, 2 * width + c0 : 2 * width + c0 + PACK] = dv

        hooks["attend_back_done"](t)
        xhat, scale = norm_stats(tok_s[here, :].astype(FLOAT))
        normed = (xhat * g1 + b1).astype(BFLOAT)
        for part in range(3):
            cols = slice(part * width, (part + 1) * width)
            gqkv_ref[:, cols] += t_dot(normed, qkv_s[here, cols])
        dn = dot_t(qkv_s[here, :], wqkv_ref[...])
        gvec_add(1, col_sum(dn * xhat))
        gvec_add(2, col_sum(dn))
        token_grad = (dbr_s[here, :].astype(FLOAT) + norm_back(dn, xhat, scale, g1)).astype(BFLOAT)
        hooks["tg_room"](t)
        to_frames(tg_ref, t, token_grad)
        hooks["tg_ready"](t)
        gstem_ref[...] += t_dot(make_hot(t), token_grad)
        hooks["tile_done"](t)


def no_tile_hook(t):
    return None


def no_pair_hook(a, b):
    return None


def no_hook():
    return None


NO_HOOKS = {
    "lat_ready": no_tile_hook,
    "stem_done": no_tile_hook,
    "attend_done": no_pair_hook,
    "feed_block": no_pair_hook,
    "attend_back_done": no_tile_hook,
    "cot_ready": no_tile_hook,
    "out_ready": no_tile_hook,
    "tg_room": no_tile_hook,
    "tg_ready": no_tile_hook,
    "tile_done": no_tile_hook,
    "start": no_hook,
    "forward_done": no_hook,
    "feed_done": no_hook,
}


def work_shapes(rows, width, tile):
    return [
        pltpu.VMEM((rows, width), BFLOAT),
        pltpu.VMEM((rows, 3 * width), BFLOAT),
        pltpu.VMEM((rows, width), BFLOAT),
        pltpu.VMEM((rows, width), BFLOAT),
        pltpu.VMEM((rows, width), BFLOAT),
        pltpu.VMEM((tile, width), FLOAT),
        pltpu.VMEM((tile, width), FLOAT),
        pltpu.VMEM((tile, width), BFLOAT),
        pltpu.VMEM((tile, width), BFLOAT),
    ]


def local_kernel(local_len, *refs):
    block_compute(
        local_len,
        {"in": refs[:9], "vec": refs[9:14], "stage": refs[14:16], "grads": refs[16:22], "work": refs[22:], "own": 0, "pairs": 1},
        NO_HOOKS,
    )


def run_local(local_len, lat, seg, cot, stem, wqkv, wout, wup, wdown, upb, *vec):
    places, per, width = cot.shape
    group_rows = 16 // local_len * (places * local_len)
    shape = jax.ShapeDtypeStruct
    vm = pl.BlockSpec(memory_space=pltpu.VMEM)
    return pl.pallas_call(
        functools.partial(local_kernel, local_len),
        out_shape=(
            shape(cot.shape, BFLOAT),
            shape(cot.shape, BFLOAT),
            shape(stem.shape, FLOAT),
            shape(wqkv.shape, FLOAT),
            shape(wout.shape, FLOAT),
            shape(wup.shape, FLOAT),
            shape(wdown.shape, FLOAT),
            shape((wup.shape[1] // width * 16, width), FLOAT),
        ),
        in_specs=[vm] * 14,
        out_specs=[vm] * 8,
        scratch_shapes=work_shapes(places * per, width, max(TILE, group_rows)),
        compiler_params=pltpu.CompilerParams(vmem_limit_bytes=60 * 1024 * 1024),
    )(lat, seg, cot, stem, wqkv, wout, wup, wdown, upb, *vec)


def wait_for(ref, sem):
    pltpu.make_async_copy(ref, ref, sem).wait()


Y_FIRST = (False, False, True, False)
DOWN, UP, STEM, QUERY = range(4)
EARLY = ((0, DOWN, 1), (1, UP, 1), (2, DOWN, 2))
ORDER = (
    (STEM, 1),
    (QUERY, 1),
    (DOWN, 3),
    (UP, 2),
    (STEM, 2),
    (QUERY, 2),
    (DOWN, 4),
    (STEM, 3),
    (UP, 3),
    (STEM, 4),
    (QUERY, 3),
    (UP, 4),
    (QUERY, 4),
    (DOWN, 5),
    (STEM, 5),
    (DOWN, 6),
    (STEM, 6),
    (UP, 5),
    (DOWN, 7),
    (QUERY, 5),
    (UP, 6),
    (STEM, 7),
    (QUERY, 6),
    (UP, 7),
    (STEM, 8),
    (QUERY, 7),
)


class Reducer:
    def __init__(self, where, pieces, bufs, final, sems, y_first):
        self.i, self.j = where
        self.pieces = pieces
        self.send, self.r1, self.r2, self.r3, self.r4, self.r5, self.fin, self.own = bufs
        self.final = final
        self.ssem, self.rsem = sems
        self.half = self.send.shape[1]
        self.core = self.bit(0)
        self.y_first = y_first
        self.across = (self.i, 1 - self.j)
        count = self.half // 2
        start = self.bit(1) * count
        self.y_rows = pl.ds(pl.multiple_of(start, 16), count)
        self.y_other = pl.ds(pl.multiple_of(count - start, 16), count)
        count = count // 2
        self.z_rows = pl.ds(pl.multiple_of(start + self.bit(2) * count, 16), count)
        self.z_other = pl.ds(pl.multiple_of(start + (1 - self.bit(2)) * count, 16), count)
        if y_first:
            self.zbuf = [self.send.at[self.j, pl.ds(pl.multiple_of(start + n * count, 16), count), :] for n in range(2)]
        else:
            self.zbuf = [self.send.at[1, (2 + n) * count : (3 + n) * count, :] for n in range(2)]

    def bit(self, n):
        return lax.rem(self.i // (1 << n), 2)

    def near(self, bit):
        step = 1 << bit
        return (self.i + step - 2 * step * self.bit(bit), self.j)

    def copy(self, n, src, dst, device):
        return pltpu.make_async_remote_copy(
            src_ref=src,
            dst_ref=dst,
            send_sem=self.ssem.at[n],
            recv_sem=self.rsem.at[n],
            device_id=device,
            device_id_type=pl.DeviceIdType.MESH,
        )

    def core_copy(self):
        return self.copy(0, self.send, self.r1, self.near(0))

    def first_copy(self):
        if self.y_first:
            return self.copy(1, self.send.at[:, self.y_other, :], self.r2, self.near(1))
        return self.copy(1, self.send.at[0], self.r2, self.across)

    def second_copy(self):
        if self.y_first:
            return self.copy(2, self.send.at[1 - self.j, self.y_rows, :], self.r3, self.across)
        return self.copy(2, self.send.at[1, 0 : self.half // 2, :], self.r3, self.near(1))

    def start_core(self):
        for h in range(2):
            for at, take in self.pieces(h, 1 - self.core):
                self.send[h, at[0], at[1]] = take().astype(BFLOAT)
        self.core_copy().start()

    def core_to_first(self):
        self.core_copy().wait()
        if self.y_first:
            for h in range(2):
                for at, take in self.pieces(h, self.core):
                    arrived = self.r1[h, at[0], at[1]].astype(FLOAT)
                    self.send[h, at[0], at[1]] = (take() + arrived).astype(BFLOAT)
            self.first_copy().start()
            return
        for at, take in self.pieces(1 - self.j, self.core):
            arrived = self.r1[1 - self.j, at[0], at[1]].astype(FLOAT)
            self.send[0, at[0], at[1]] = (take() + arrived).astype(BFLOAT)
        self.first_copy().start()
        for at, take in self.pieces(self.j, self.core):
            self.own[at[0], at[1]] = take() + self.r1[self.j, at[0], at[1]].astype(FLOAT)

    def first_to_second(self):
        self.first_copy().wait()
        if self.y_first:
            far = self.send[1 - self.j, self.y_rows, :].astype(FLOAT) + self.r2[1 - self.j].astype(FLOAT)
            self.send[1 - self.j, self.y_rows, :] = far.astype(BFLOAT)
            self.second_copy().start()
            near = self.send[self.j, self.y_rows, :].astype(FLOAT) + self.r2[self.j].astype(FLOAT)
            self.own[self.y_rows, :] = near
            return
        far = self.own[self.y_other, :] + self.r2[self.y_other, :].astype(FLOAT)
        self.send[1, 0 : self.half // 2, :] = far.astype(BFLOAT)
        self.second_copy().start()
        self.own[self.y_rows, :] += self.r2[self.y_rows, :].astype(FLOAT)

    def third_copy(self):
        return self.copy(3, self.zbuf[0], self.r4, self.near(2))

    def fourth_copy(self):
        return self.copy(4, self.zbuf[1], self.r5, self.near(3))

    def second_to_third(self):
        self.second_copy().wait()
        self.own[self.y_rows, :] += self.r3[...].astype(FLOAT)
        self.zbuf[0][...] = self.own[self.z_other, :].astype(BFLOAT)
        self.third_copy().start()

    def third_to_fourth(self):
        self.third_copy().wait()
        total = self.own[self.z_rows, :] + self.r4[...].astype(FLOAT)
        self.zbuf[1][...] = total.astype(BFLOAT)
        self.fourth_copy().start()

    def keep_copy(self):
        return pltpu.make_async_copy(self.fin, self.final.at[self.core, self.z_rows, :], self.ssem.at[8])

    def z_gather(self):
        return self.copy(5, self.fin, self.final.at[self.core, self.z_rows, :], self.near(2))

    def y_gather(self):
        place = self.final.at[self.core, self.y_rows, :]
        return self.copy(6, place, place, self.near(1))

    def core_gather(self):
        place = self.final.at[self.core]
        return self.copy(7, place, place, self.near(0))

    def fourth_done(self):
        self.fourth_copy().wait()
        self.fin[...] = (self.zbuf[1][...].astype(FLOAT) + self.r5[...].astype(FLOAT)).astype(BFLOAT)
        self.keep_copy().start()
        self.z_gather().start()

    def z_to_y(self):
        self.keep_copy().wait()
        self.z_gather().wait()
        self.y_gather().start()

    def y_done(self):
        self.y_gather().wait()

    def step(self, n):
        (
            self.start_core,
            self.core_to_first,
            self.first_to_second,
            self.second_to_third,
            self.third_to_fourth,
            self.fourth_done,
            self.z_to_y,
            self.y_done,
        )[n]()


def wide_kernel(local_len, *refs):
    (
        lat_hbm, seg_ref, cot_hbm, stem_hbm, extra_hbm,
        wq_hbm, wk_hbm, wv_hbm, wo_hbm, wup_hbm, wdown_hbm, upb_hbm,
    ) = refs[:12]
    vec = refs[12:17]
    out_hbm, tg_hbm, down_hbm, up_hbm, query_hbm, shared_hbm = refs[17:23]
    (
        lat_s, frame_s, stem_s, wqkv_s, wout_s, wup_s, wdown_s, upb_s,
        gstem_s, gqkv_s, gout_s, gup_s, gdown_s, gvec_s,
    ) = refs[23:37]
    work = refs[37:44]
    own_s = refs[44]
    group_bufs = [refs[45 + 7 * n : 52 + 7 * n] for n in range(4)]
    sizes = [bufs[0].shape[1] for bufs in group_bufs]
    owns = (
        own_s.at[0 : sizes[0], :],
        own_s.at[sizes[0] : sizes[0] + sizes[1], :],
        gdown_s.at[0 : sizes[2], :],
        gdown_s.at[sizes[2] : sizes[2] + sizes[3], :],
    )
    tile = work[5].shape[0]
    work = work[:5] + (own_s.at[0:tile, :], own_s.at[tile : 2 * tile, :]) + work[5:]
    (
        lat_send, lat_recv, cot_send, cot_recv, own_sem, out_send, out_recv, tg_send, tg_recv,
        w_local, wx_send, wx_recv, wc_send, wc_recv, sh_send, sh_recv,
    ) = refs[73:89]
    group_sems = [refs[89 + 2 * n : 91 + 2 * n] for n in range(4)]
    i, j = lax.axis_index("gx"), lax.axis_index("gy")
    places = lax.axis_size("gx")
    core = lax.rem(i, 2)
    sibling = (i + 1 - 2 * core, j)
    ybit = lax.rem(i // 2, 2)
    beside = (i + 2 - 4 * ybit, j)
    across = (i, 1 - j)
    tiles = work[0].shape[0] // tile
    width = work[0].shape[1]
    mesh_id = pl.DeviceIdType.MESH

    def remote(src, dst, send, recv, device):
        return pltpu.make_async_remote_copy(
            src_ref=src, dst_ref=dst, send_sem=send, recv_sem=recv, device_id=device, device_id_type=mesh_id
        )

    barrier = pltpu.get_barrier_semaphore()

    @pl.loop(1, places)
    def greet(k):
        pl.semaphore_signal(barrier, inc=1, device_id=(lax.rem(i + k, places), j), device_id_type=mesh_id)

    pl.semaphore_signal(barrier, inc=1, device_id=across, device_id_type=mesh_id)
    pl.semaphore_wait(barrier, places)

    def part(ref, t):
        count = ref.shape[1] // tiles
        return pl.ds(pl.multiple_of(t * count, count), count)

    def scatter(src, dst, t, send, recv):
        @pl.loop(1, places)
        def each(k):
            d = lax.rem(i + k, places)
            remote(src.at[d, part(src, t), :], dst.at[i, part(src, t), :], send, recv, (d, j)).start()

    def keep(src, dst, t, sem):
        return pltpu.make_async_copy(src.at[i, part(src, t), :], dst.at[i, part(src, t), :], sem)

    def most(ref, t):
        return ref.at[0 : places - 1, part(ref, t), :]

    half = wq_hbm.shape[1]

    ff_half = upb_hbm.shape[1]
    blocks = ff_half // FFB

    def weight_views(owner, whole):
        def rows_of(count):
            return (0, count) if whole else (pl.multiple_of(core * (count // 2), 16), count // 2)

        start, size = rows_of(width)
        r = pl.ds(start, size)
        views = []
        for n, src in enumerate((wq_hbm, wk_hbm, wv_hbm)):
            at = pl.ds(pl.multiple_of(n * width + owner * half, half), half)
            views.append((src.at[r, :], wqkv_s.at[r, at]))
        count = wo_hbm.shape[0]
        start, size = rows_of(count)
        there = pl.ds(pl.multiple_of(owner * count + start, 16), size)
        views.append((wo_hbm.at[pl.ds(start, size), :], wout_s.at[there, :]))
        start, size = rows_of(FFB)
        for block in range(blocks):
            at = pl.ds(pl.multiple_of(owner * ff_half + block * FFB, 128), FFB)
            views.append((wup_hbm.at[r, block * FFB : (block + 1) * FFB], wup_s.at[r, at]))
            here = pl.ds(pl.multiple_of(block * FFB + start, 16), size)
            there = pl.ds(pl.multiple_of(owner * ff_half + block * FFB + start, 16), size)
            views.append((wdown_hbm.at[here, :], wdown_s.at[there, :]))
        return views

    here_views = weight_views(j, True)
    x_copies = [
        remote(src, dst, wx_send.at[n], wx_recv.at[n], across)
        for n, (src, dst) in enumerate(weight_views(j, False))
    ]
    c_copies = [
        remote(dst, dst, wc_send.at[n], wc_recv.at[n], sibling)
        for n, (_, dst) in enumerate(weight_views(1 - j, False))
    ]
    own_copies = [pltpu.make_async_copy(src, dst, w_local.at[n]) for n, (src, dst) in enumerate(here_views)]
    n_weights = len(x_copies)
    upb_at = pl.ds(pl.multiple_of(j * ff_half, 128), ff_half)
    upb_x = remote(upb_hbm, upb_s.at[:, upb_at], wx_send.at[n_weights], wx_recv.at[n_weights], across)
    upb_own = pltpu.make_async_copy(upb_hbm, upb_s.at[:, upb_at], w_local.at[n_weights])

    for n in range(4):
        x_copies[n].start()

    @pl.loop(0, tiles)
    def send_lat(t):
        keep(lat_hbm, lat_s, t, own_sem.at[t]).start()
        scatter(lat_hbm, lat_s, t, lat_send, lat_recv.at[t])

    stem_rows_in = stem_hbm.shape[0]
    stem_copies = [
        pltpu.make_async_copy(stem_hbm, stem_s.at[0:stem_rows_in, :], w_local.at[n_weights + 1]),
        pltpu.make_async_copy(extra_hbm, stem_s.at[stem_rows_in:, :], w_local.at[n_weights + 2]),
    ]
    for copy in stem_copies:
        copy.start()
    for n in range(4, n_weights):
        x_copies[n].start()
    for copy in own_copies:
        copy.start()
    upb_x.start()
    upb_own.start()

    @pl.loop(0, tiles)
    def send_cot(t):
        keep(cot_hbm, frame_s, t, own_sem.at[tiles + t]).start()
        scatter(cot_hbm, frame_s, t, cot_send, cot_recv.at[t])

    def move(first, last, before, after):
        for n in range(first, last):
            before[n].wait()
            if after is not None:
                after[n].start()

    last_tile = tiles - 1
    middle = min(1, last_tile)

    hooks = dict(NO_HOOKS)

    def lat_ready(t):
        keep(lat_hbm, lat_s, t, own_sem.at[t]).wait()
        wait_for(most(lat_s, t), lat_recv.at[t])

        @pl.when(t == 0)
        def _():
            for copy in stem_copies:
                copy.wait()

    def stem_done(t):
        @pl.when(t == last_tile)
        def _():
            move(0, 4, own_copies, None)

    def attend_done(turn, t):
        @pl.when((turn == 0) & (t == middle))
        def _():
            move(0, 4, x_copies, c_copies)

        @pl.when((turn == 0) & (t == last_tile))
        def _():
            move(0, 4, c_copies, None)

        @pl.when((turn == 1) & (t == last_tile))
        def _():
            move(4, 6, x_copies, c_copies)

    def forward_done():
        upb_x.wait()
        upb_own.wait()
        move(4, n_weights, own_copies, None)

    def feed_block(t, turn):
        for block in range(blocks):

            @pl.when((t == 0) & (turn == blocks + block))
            def _():
                first = 4 + 2 * block
                if block > 0:
                    move(first, first + 2, x_copies, c_copies)
                move(first, first + 2, c_copies, None)

    def cot_ready(t):
        keep(cot_hbm, frame_s, t, own_sem.at[tiles + t]).wait()
        wait_for(most(frame_s, t), cot_recv.at[t])

    def out_ready(t):
        keep(frame_s, out_hbm, t, own_sem.at[2 * tiles + t]).start()
        scatter(frame_s, out_hbm, t, out_send.at[t], out_recv)

    def tg_room(t):
        keep(frame_s, out_hbm, t, own_sem.at[2 * tiles + t]).wait()
        wait_for(most(frame_s, t), out_send.at[t])

    def tg_ready(t):
        keep(frame_s, tg_hbm, t, own_sem.at[3 * tiles + t]).start()
        scatter(frame_s, tg_hbm, t, tg_send.at[t], tg_recv)

    def grab(ref, r0, nrows, c0, ncols):
        return lambda: ref[pl.ds(r0, nrows), pl.ds(c0, ncols)]

    def mult(value, by):
        return pl.multiple_of(value, by)

    up_half = gup_s.shape[1] // 2
    up_rows = width // 2
    down_rows = gdown_s.shape[0] // 4
    out_rows = gout_s.shape[0] // 4
    stem_rows = gstem_s.shape[0] // 4

    qrows = width // 2

    def down_pieces(h, c):
        return [((slice(None), slice(None)), grab(gdown_s, mult((h * 2 + c) * down_rows, 16), down_rows, 0, width))]

    def up_pieces(h, c):
        found, base = [], 0
        for block in range(up_half // width):
            found.append(
                (
                    (slice(base, base + up_rows), slice(None)),
                    grab(gup_s, mult(c * up_rows, 16), up_rows, mult(h * up_half + block * width, 128), width),
                )
            )
            base += up_rows
        found.append(
            (
                (slice(base, base + out_rows), slice(None)),
                grab(gout_s, mult((h * 2 + c) * out_rows, 16), out_rows, 0, width),
            )
        )
        return found

    def stem_pieces(h, c):
        found = [
            (
                (slice(0, stem_rows), slice(None)),
                grab(gstem_s, mult((h * 2 + c) * stem_rows, 16), stem_rows, 0, width),
            ),
            (
                (slice(stem_rows, stem_rows + 16), slice(None)),
                grab(gvec_s, mult((h * 2 + c) * 16, 16), 16, 0, width),
            ),
        ]
        base, end = stem_rows + 16, sizes[2]
        if end > base:
            found.append(((slice(base, end), slice(None)), lambda: jnp.zeros((end - base, width), FLOAT)))
        return found

    def query_pieces(h, c):
        found = [
            (
                (slice(0, qrows), slice(n * half, (n + 1) * half)),
                grab(gqkv_s, mult(c * qrows, 16), qrows, mult(n * width + h * half, 128), half),
            )
            for n in range(2)
        ]
        for n in range(2):
            found.append(
                (
                    (slice(qrows, qrows + qrows // 2), slice(n * half, (n + 1) * half)),
                    grab(gqkv_s, mult(c * qrows + n * (qrows // 2), 16), qrows // 2, mult(2 * width + h * half, 128), half),
                )
            )
        return found

    where = (i, j)
    down, up, stem, query = [
        Reducer(where, pieces, bufs + (own,), final, sems, y_first)
        for pieces, bufs, own, final, sems, y_first in zip(
            (down_pieces, up_pieces, stem_pieces, query_pieces),
            group_bufs,
            owns,
            (down_hbm, up_hbm, shared_hbm.at[j], query_hbm),
            group_sems,
            Y_FIRST,
        )
    ]

    def feed_done():
        down.start_core()
        up.start_core()

    def attend_back_done(t):
        for at, group, n in EARLY:

            @pl.when(t == min(at, last_tile))
            def _():
                (down, up)[group].step(n)

    hooks.update(
        lat_ready=lat_ready,
        stem_done=stem_done,
        attend_done=attend_done,
        feed_block=feed_block,
        attend_back_done=attend_back_done,
        forward_done=forward_done,
        cot_ready=cot_ready,
        out_ready=out_ready,
        tg_room=tg_room,
        tg_ready=tg_ready,
        feed_done=feed_done,
    )
    block_compute(
        local_len,
        {
            "in": (lat_s, seg_ref, frame_s, stem_s, wqkv_s, wout_s, wup_s, wdown_s, upb_s),
            "vec": vec,
            "own": j,
            "pairs": frame_s.shape[1] // lat_s.shape[1],
            "stage": (frame_s, frame_s),
            "grads": (gstem_s, gqkv_s, gout_s, gup_s, gdown_s, gvec_s),
            "work": work,
        },
        hooks,
    )
    stem.start_core()
    query.start_core()
    to_x = remote(shared_hbm.at[j, core], shared_hbm.at[j, core], sh_send.at[0], sh_recv.at[0], across)
    to_core = remote(shared_hbm.at[:, core], shared_hbm.at[:, core], sh_send.at[1], sh_recv.at[1], sibling)
    for g, n in ORDER:
        group = (down, up, stem, query)[g]
        if n == 8 and g == STEM:
            to_x.wait()
            to_core.start()
            continue
        group.step(n)
        if n == 7:
            (to_x if g == STEM else group.core_gather()).start()
    for group in (down, up, query):
        group.core_gather().wait()
    to_core.wait()
    wait_for(lat_hbm.at[0 : places - 1], lat_send)
    wait_for(cot_hbm.at[0 : places - 1], cot_send)
    wait_for(out_hbm.at[0 : places - 1], out_recv)
    wait_for(tg_hbm.at[0 : places - 1], tg_recv)

    @pl.loop(0, tiles)
    def drain(t):
        keep(frame_s, tg_hbm, t, own_sem.at[3 * tiles + t]).wait()
        wait_for(most(frame_s, t), tg_send.at[t])


def reduce_shapes(half, width, y_first):
    return [
        pltpu.VMEM((2, half, width), BFLOAT),
        pltpu.VMEM((2, half, width), BFLOAT),
        pltpu.VMEM((2, half // 2, width) if y_first else (half, width), BFLOAT),
        pltpu.VMEM((half // 2, width), BFLOAT),
        pltpu.VMEM((half // 4, width), BFLOAT),
        pltpu.VMEM((half // 4, width), BFLOAT),
        pltpu.VMEM((half // 4, width), BFLOAT),
    ]


def run_wide(local_len, lat, seg, cot, stem, extra, wq, wk, wv, wo, wup, wdown, upb, *vec):
    places, per, width = cot.shape
    rows = places * per
    ff = 2 * wup.shape[1]
    hot_width = stem.shape[0] + extra.shape[0]
    shape = jax.ShapeDtypeStruct
    vm = pl.BlockSpec(memory_space=pltpu.VMEM)
    hbm = pl.BlockSpec(memory_space=pl.ANY)
    stem_used = hot_width // 4 + 16
    sizes = (
        ff // 4,
        (width // 2) * (wup.shape[1] // width) + width // 4,
        -(-stem_used // 64) * 64,
        width // 2 + width // 4,
    )
    tiles = rows // TILE
    n_weights = 4 + 2 * (wup.shape[1] // FFB)
    dma = pltpu.SemaphoreType.DMA
    scratch = [
        pltpu.VMEM(lat.shape, BFLOAT),
        pltpu.VMEM(cot.shape, BFLOAT),
        pltpu.VMEM((hot_width, width), BFLOAT),
        pltpu.VMEM((width, 3 * width), BFLOAT),
        pltpu.VMEM((width, width), BFLOAT),
        pltpu.VMEM((width, ff), BFLOAT),
        pltpu.VMEM((ff, width), BFLOAT),
        pltpu.VMEM((1, ff), FLOAT),
        pltpu.VMEM((hot_width, width), FLOAT),
        pltpu.VMEM((width, 3 * width), FLOAT),
        pltpu.VMEM((width, width), FLOAT),
        pltpu.VMEM((width, ff), FLOAT),
        pltpu.VMEM((ff, width), FLOAT),
        pltpu.VMEM((ff // width * 16, width), FLOAT),
    ]
    scratch += [item for n, item in enumerate(work_shapes(rows, width, TILE)) if n not in (5, 6)]
    scratch += [pltpu.VMEM((sizes[0] + sizes[1], width), FLOAT)]
    for size, y_first in zip(sizes, Y_FIRST):
        scratch += reduce_shapes(size, width, y_first)
    scratch += [
        dma,
        dma((tiles,)),
        dma,
        dma((tiles,)),
        dma((4 * tiles,)),
        dma((tiles,)),
        dma,
        dma((tiles,)),
        dma,
        dma((n_weights + 3,)),
        dma((n_weights + 1,)),
        dma((n_weights + 1,)),
        dma((n_weights,)),
        dma((n_weights,)),
        dma((2,)),
        dma((2,)),
    ]
    scratch += [dma((9,))] * 8
    return pl.pallas_call(
        functools.partial(wide_kernel, local_len),
        out_shape=(shape(cot.shape, BFLOAT), shape(cot.shape, BFLOAT))
        + tuple(shape((2, sizes[n], width), BFLOAT) for n in (0, 1, 3))
        + (shape((2, 2, sizes[2], width), BFLOAT),),
        in_specs=[hbm, vm] + [hbm] * 10 + [vm] * 5,
        out_specs=[hbm] * 6,
        scratch_shapes=scratch,
        compiler_params=pltpu.CompilerParams(
            vmem_limit_bytes=VMEM_LIMIT, collective_id=0, has_side_effects=True
        ),
    )(lat, seg, cot, stem, extra, wq, wk, wv, wo, wup, wdown, upb, *vec)


def per_device(
    latents,
    actions,
    segment_ids,
    cotangent,
    stem_weight,
    action_table,
    first_gain,
    first_bias,
    query_weight,
    key_weight,
    value_weight,
    out_weight,
    second_gain,
    second_bias,
    up_weight,
    up_bias,
    down_weight,
    down_bias,
):
    half_seqs, local_len, groups = latents.shape
    width = stem_weight.shape[1]
    places = lax.axis_size("gx")
    length = places * local_len
    seqs = half_seqs // places
    rows = seqs * length
    actions_n = action_table.shape[0]

    lat = jnp.concatenate([latents, actions[..., None]], axis=-1).astype(BFLOAT)
    lat = lat.reshape(places, seqs, local_len, groups + 1)
    cot = cotangent.reshape(places, seqs * local_len, width)
    first_seq = (lax.axis_index("gy") * places + lax.axis_index("gx")) * seqs
    seg = lax.dynamic_slice_in_dim(segment_ids, first_seq, seqs, 0)
    seg = jnp.tile(seg.astype(FLOAT), (1, PACK // length))
    extra = jnp.pad(action_table, ((0, HOT_PAD - actions_n), (0, 0)))
    vec = [item[None] for item in (first_gain, first_bias, second_gain, second_bias, down_bias)]
    if rows % TILE == 0 and rows <= MAX_ROWS and places == 16:
        lat = jnp.pad(lat, ((0, 0), (0, 0), (0, 0), (0, 64 - groups - 1)))
        lat = lat.reshape(places, seqs * local_len // 2, 128)
        out, tg, gdown, up, query, shared = run_wide(
            local_len, lat, seg, cot, stem_weight, extra, query_weight, key_weight, value_weight,
            out_weight, up_weight, down_weight, up_bias[None], *vec,
        )
        out = out.reshape(half_seqs, local_len, width)
        tg = tg.reshape(half_seqs, local_len, width)
        half = width // 2
        cols = query_weight.shape[1]
        blocks = up_weight.shape[1] // width
        gdown = gdown.astype(FLOAT).reshape(down_weight.shape)
        gup = jnp.concatenate([up[:, b * half : (b + 1) * half] for b in range(blocks)], axis=2)
        gup = gup.astype(FLOAT).reshape(up_weight.shape)
        gout = up[:, blocks * half :].astype(FLOAT).reshape(out_weight.shape)
        query = query.astype(FLOAT)
        gq = query[:, :half, :cols].reshape(width, cols)
        gk = query[:, :half, cols:].reshape(width, cols)
        part = query[:, half:]
        gv = jnp.concatenate([part[:, :, :cols], part[:, :, cols:]], axis=1).reshape(width, cols)
        stem_rows = (stem_weight.shape[0] + HOT_PAD) // 4
        gstem = shared[:, :, :stem_rows].astype(FLOAT).reshape(4 * stem_rows, width)
        first = shared[0, 0, stem_rows : stem_rows + 16].astype(FLOAT)
        upb_grad = lax.dynamic_index_in_dim(shared[:, :, stem_rows], lax.axis_index("gy"), 0, False)
        upb_grad = upb_grad.astype(FLOAT).reshape(up_bias.shape)
        return (
            out,
            tg,
            gstem[: groups * 32],
            gstem[groups * 32 : groups * 32 + actions_n],
            first[1],
            first[2],
            gq,
            gk,
            gv,
            gout,
            first[3],
            first[4],
            gup,
            upb_grad,
            gdown,
            first[5],
        )
    lat = lat.reshape(places, seqs * local_len, groups + 1)
    lat = jnp.pad(lat, ((0, 0), (0, 0), (0, 128 - groups - 1)))
    lat = lax.all_to_all(lat, "gx", split_axis=0, concat_axis=0, tiled=True)
    cot = lax.all_to_all(cot, "gx", split_axis=0, concat_axis=0, tiled=True)
    gather = functools.partial(lax.all_gather, axis_name="gy", tiled=True)
    wqkv = jnp.concatenate(
        [gather(item, axis=1) for item in (query_weight, key_weight, value_weight)], axis=1
    )
    wout = gather(out_weight, axis=0)
    wup = gather(up_weight, axis=1)
    wdown = gather(down_weight, axis=0)
    upb = gather(up_bias, axis=0)[None]
    stem = jnp.concatenate([stem_weight, extra], axis=0)
    out, tg, gstem, gqkv, gout, gup, gdown, gvec = run_local(
        local_len, lat, seg, cot, stem, wqkv, wout, wup, wdown, upb, *vec
    )
    out = lax.all_to_all(out, "gx", split_axis=0, concat_axis=0, tiled=True)
    tg = lax.all_to_all(tg, "gx", split_axis=0, concat_axis=0, tiled=True)
    out = out.reshape(half_seqs, local_len, width)
    tg = tg.reshape(half_seqs, local_len, width)
    both = ("gx", "gy")
    gstem, gvec = lax.psum((gstem, gvec), both)
    upb_grad = gvec[::16].reshape(-1)
    upb_grad = lax.dynamic_slice_in_dim(upb_grad, lax.axis_index("gy") * up_bias.shape[0], up_bias.shape[0])

    def shard(value, dim):
        return lax.psum(lax.psum_scatter(value, "gy", scatter_dimension=dim, tiled=True), "gx")

    gq = shard(gqkv[:, :width], 1)
    gk = shard(gqkv[:, width : 2 * width], 1)
    gv = shard(gqkv[:, 2 * width :], 1)
    return (
        out,
        tg,
        gstem[: groups * 32],
        gstem[groups * 32 : groups * 32 + actions_n],
        gvec[1],
        gvec[2],
        gq,
        gk,
        gv,
        shard(gout, 0),
        gvec[3],
        gvec[4],
        shard(gup, 1),
        upb_grad,
        shard(gdown, 0),
        gvec[5],
    )


def solution(mesh):
    return jax.shard_map(
        per_device,
        mesh=mesh,
        in_specs=(
            P("gy", "gx", None),
            P("gy", "gx"),
            P(),
            P("gy", "gx", None),
            P(),
            P(),
            P(),
            P(),
            P(None, "gy"),
            P(None, "gy"),
            P(None, "gy"),
            P("gy", None),
            P(),
            P(),
            P(None, "gy"),
            P("gy"),
            P("gy", None),
            P(),
        ),
        out_specs=(
            P("gy", "gx", None),
            P("gy", "gx", None),
            P(),
            P(),
            P(),
            P(),
            P(None, "gy"),
            P(None, "gy"),
            P(None, "gy"),
            P("gy", None),
            P(),
            P(),
            P(None, "gy"),
            P("gy"),
            P("gy", None),
            P(),
        ),
        check_vma=False,
    )
```

time: 239 us -> 199 us (0.83)
  Pallas kernels: 206 us -> 172 us
  local copies, waits for them, and re-layouts: 24.8 us -> 16 us
    pallas_call x1, Pallas kernels: 206 us -> 172 us  [run_wide(): pl.pallas_call(functools.partial(wide_kernel, local_len), out_shape=(shap...]
    slice x6 -> x5, local copies, waits for them, and re-layouts: 5.54 us -> 1.22 us  [the longest x1 1.05 us: per_device(): gk = query[:, :half, cols:].reshape(width, cols)]
    concatenate x2 -> x0, other arithmetic: 3.77 us -> none  [the longest x1 2.31 us: per_device(): jnp.concatenate([stem_weight, jnp.pad(action_table, ((0, HOT_PAD - action...]
    reshape x0 -> x3, other arithmetic: none -> 2.94 us  [the longest x1 1.68 us: per_device(): gdown = gdown.astype(FLOAT).reshape(down_weight.shape)]
where the time goes in v3:
time: 199 us; the launch traced here: 197 us
  Pallas kernels  172 us (86%)
  local copies, waits for them, and re-layouts  16 us (8%)
  other arithmetic  7.76 us (4%)
    pallas_call x1, Pallas kernels, run_wide(): pl.pallas_call(functools.partial(wide_kernel, local_len), out_shape=(shap...  172 us

profile of v3, /device:TPU:0, one launch (start us, length us, event | category | flops | bytes accessed | tf_op | source)
XLA Modules:
  0.0 196.9 jit_solution(17395067801279692547)
XLA Ops:
  0.6 0.0 copy-start
  0.7 0.7 convert.13
  1.4 0.1 concatenate.21
  1.5 0.9 convert.12
  2.4 0.7 concatenate.20
  3.1 0.0 copy-start.2
  3.1 0.1 pad_maximum_fusion
  3.3 0.7 copy.42
  4.0 0.2 pad.8.clone
  4.2 0.9 reshape.101.refs_0_
  5.1 0.0 copy-done
  5.1 0.1 constant_dynamic-slice_fusion
  5.1 0.1 copy.41
  5.2 0.7 tile.10.refs_1_
  6.0 0.0 copy-done.2
  6.0 0.0 copy-start.7
  6.0 1.8 reshape.102.refs_2_
  7.8 0.0 copy-done.7
  7.8 0.7 pad.9.refs_4_
  8.5 172.4 %shard_map.297 = (bf16[16,96,512]{2,1,0:T(8,128)(2,1)}, bf16[16,96,512]{2,1,0:T(8,128)(2,1)}, bf16[2,512,512]{2,1,0:T(8,128)(2,1)}, bf16[2,640,512]{2,1,0:T(8,12...) custom-call(bf16[16,48,128]{2,1,0:T(8,128)(2,1)} %reshape.101.refs_0_, f32[24,256]{1,0:T(8,128)} %tile.10.refs_1_, ...), custom_call_target="tpu_custom_call" | custom-call | tf_op jit(solution)/shard_map/pallas_call | solution.py:1020
  180.9 0.0 copy-start.3
  180.9 3.6 %reshape.103 = bf16[384,4,512]{2,1,0:T(4,128)(2,1)} reshape(bf16[16,96,512]{2,1,0:T(8,128)(2,1)} %get-tuple-element.22) | data formatting | bytes 3145728 | tf_op jit(solution)/shard_map/reshape | solution.py:1077
  184.5 0.0 copy-done.3
  184.5 0.0 copy-start.5
  184.5 1.8 reshape.104
  186.3 0.0 copy-done.5
  186.3 0.1 slice.59
  186.4 0.4 bitcast_convert_fusion
  186.8 0.0 copy-start.1
  186.8 1.5 slice.76
  188.3 0.6 slice.77
  188.9 0.6 fusion.3
  189.5 0.0 copy-done.1
  189.5 1.0 fusion.2
  190.6 0.0 copy-start.4
  190.6 0.8 pad_maximum_fusion.1
  191.5 0.6 copy-done.4
  192.1 0.9 bitcast_convert_fusion.2
  193.0 0.1 fusion
  193.1 0.0 copy-start.6
  193.1 1.6 maximum_convert_fusion
  194.7 0.6 dynamic-slice_convert_fusion
  195.3 0.0 copy-done.6
  195.3 1.7 bitcast_convert_fusion.1
  (6 shorter events, 0.1 us)
Async XLA Ops:
  0.6 4.4 %copy-start = (s32[768,64]{0,1:T(8,128)S(1)}, s32[768,64]{0,1:T(8,128)}, u32[]{:S(2)}) copy-start(s32[768,64]{0,1:T(8,128)} %param.20) | copy-start | bytes 589828
  3.1 2.8 %copy-start.2 = (bf16[384,4,512]{2,1,0:T(4,128)(2,1)S(1)}, bf16[384,4,512]{2,1,0:T(4,128)(2,1)}, u32[]{:S(2)}) copy-start(bf16[384,4,512]{2,1,0:T(4,128)(2,1)} %param.21) | copy-start | bytes 4718596
  6.0 1.8 copy-start.7
  180.9 3.6 %copy-start.3 = (bf16[16,96,512]{2,1,0:T(8,128)(2,1)S(1)}, bf16[16,96,512]{2,1,0:T(8,128)(2,1)}, u32[]{:S(2)}) copy-start(bf16[16,96,512]{2,1,0:T(8,128)(2,1)} %get-tuple-element.23) | copy-start | bytes 4718596
  184.5 1.8 copy-start.5
  186.8 2.7 %copy-start.1 = (bf16[2,384,512]{2,1,0:T(8,128)(2,1)S(1)}, bf16[2,384,512]{2,1,0:T(8,128)(2,1)}, u32[]{:S(2)}) copy-start(bf16[2,384,512]{2,1,0:T(8,128)(2,1)} %get-tuple-element.25) | copy-start | bytes 2359300
  190.6 1.5 copy-start.4
  193.1 2.2 %copy-start.6 = (bf16[2,512,512]{2,1,0:T(8,128)(2,1)S(1)}, bf16[2,512,512]{2,1,0:T(8,128)(2,1)}, u32[]{:S(2)}) copy-start(bf16[2,512,512]{2,1,0:T(8,128)(2,1)} %get-tuple-element.27) | copy-start | bytes 3145732

commit v4 on v3

--- a/solution.py
+++ b/solution.py
@@ -14,7 +14,7 @@
 BFLOAT = jnp.bfloat16
 TILE = 512
 MAX_ROWS = 2048
-VMEM_LIMIT = 60 * 1024 * 1024
+VMEM_LIMIT = 62 * 1024 * 1024
 UNIT = 4
 SUB = 512
 FFB = 512
@@ -232,8 +232,7 @@
 
     hooks["forward_done"]()
 
-    @pl.loop(0, tiles)
-    def phase_two(t):
+    def phase_two(t, leading):
         r0 = pl.multiple_of(t * tile, tile)
         here = pl.ds(r0, tile)
         resid = tok_s[here, :].astype(FLOAT) + dot(mix_s[here, :], wout_ref[...])
@@ -244,9 +243,9 @@
         acc_s[...] = resid + bd
         dn_s[...] = jnp.zeros_like(dn_s)
 
-        @pl.loop(0, ff // FFB)
         def feed(turn):
-            hooks["feed_block"](t, turn)
+            if leading:
+                hooks["feed_block"](turn)
             blocks = ff // FFB
             f = lax.rem(turn + refs["own"] * (blocks // 2), blocks)
             f0 = pl.multiple_of(f * FFB, FFB)
@@ -271,6 +270,9 @@
             gup_ref[:, fs] += t_dot(n2, d_pre)
             dn_s[...] += dot_t(d_pre, up)
 
+        for turn in range(ff // FFB):
+            feed(turn)
+
         cot_f = cotp_s[...].astype(FLOAT)
         gvec_add(5, col_sum(cot_f))
         to_frames(out_ref, t, acc_s[...].astype(BFLOAT))
@@ -285,6 +287,8 @@
         gout_ref[...] += t_dot(mix_s[here, :], d_branch)
         mix_s[here, :] = dot_t(d_branch, wout_ref[...]).astype(BFLOAT)
 
+    phase_two(0, True)
+    pl.loop(1, tiles)(functools.partial(phase_two, leading=False))
     hooks["feed_done"]()
 
     @pl.loop(0, tiles)
@@ -351,7 +355,7 @@
     "lat_ready": no_tile_hook,
     "stem_done": no_tile_hook,
     "attend_done": no_pair_hook,
-    "feed_block": no_pair_hook,
+    "feed_block": no_tile_hook,
     "attend_back_done": no_tile_hook,
     "cot_ready": no_tile_hook,
     "out_ready": no_tile_hook,
@@ -414,61 +418,41 @@
     pltpu.make_async_copy(ref, ref, sem).wait()
 
 
-Y_FIRST = (False, False, True, False)
 DOWN, UP, STEM, QUERY = range(4)
 EARLY = ((0, DOWN, 1), (1, UP, 1), (2, DOWN, 2))
 ORDER = (
     (STEM, 1),
     (QUERY, 1),
+    (UP, 2),
     (DOWN, 3),
-    (UP, 2),
     (STEM, 2),
+    (UP, 3),
     (QUERY, 2),
+    (STEM, 3),
     (DOWN, 4),
-    (STEM, 3),
-    (UP, 3),
-    (STEM, 4),
     (QUERY, 3),
     (UP, 4),
+    (STEM, 4),
+    (DOWN, 5),
     (QUERY, 4),
-    (DOWN, 5),
+    (UP, 5),
     (STEM, 5),
-    (DOWN, 6),
-    (STEM, 6),
-    (UP, 5),
-    (DOWN, 7),
     (QUERY, 5),
-    (UP, 6),
-    (STEM, 7),
-    (QUERY, 6),
-    (UP, 7),
-    (STEM, 8),
-    (QUERY, 7),
 )
+TURNS = tuple((dx, dy, dz) for dx in range(2) for dy in range(2) for dz in range(2))
 
 
 class Reducer:
-    def __init__(self, where, pieces, bufs, final, sems, y_first):
+    def __init__(self, where, pieces, bufs, final, sems, everywhere):
         self.i, self.j = where
         self.pieces = pieces
-        self.send, self.r1, self.r2, self.r3, self.r4, self.r5, self.fin, self.own = bufs
+        self.send, self.r1, self.r2, self.r3, self.r5, self.fin = bufs
         self.final = final
         self.ssem, self.rsem = sems
-        self.half = self.send.shape[1]
         self.core = self.bit(0)
-        self.y_first = y_first
-        self.across = (self.i, 1 - self.j)
-        count = self.half // 2
-        start = self.bit(1) * count
-        self.y_rows = pl.ds(pl.multiple_of(start, 16), count)
-        self.y_other = pl.ds(pl.multiple_of(count - start, 16), count)
-        count = count // 2
-        self.z_rows = pl.ds(pl.multiple_of(start + self.bit(2) * count, 16), count)
-        self.z_other = pl.ds(pl.multiple_of(start + (1 - self.bit(2)) * count, 16), count)
-        if y_first:
-            self.zbuf = [self.send.at[self.j, pl.ds(pl.multiple_of(start + n * count, 16), count), :] for n in range(2)]
-        else:
-            self.zbuf = [self.send.at[1, (2 + n) * count : (3 + n) * count, :] for n in range(2)]
+        self.part = self.send.shape[1] // 4
+        self.everywhere = everywhere
+        self.mine = self.rows(0, 0)
 
     def bit(self, n):
         return lax.rem(self.i // (1 << n), 2)
@@ -476,6 +460,18 @@
     def near(self, bit):
         step = 1 << bit
         return (self.i + step - 2 * step * self.bit(bit), self.j)
+
+    def rows(self, dy, dz):
+        y = self.bit(1) + dy - 2 * dy * self.bit(1)
+        z = self.bit(2) + dz - 2 * dz * self.bit(2)
+        return pl.ds(pl.multiple_of((y * 2 + z) * self.part, 16), self.part)
+
+    def plane(self, dx):
+        return 1 - self.j if dx else self.j
+
+    def member(self, dx, dy, dz):
+        place = self.i + dy * (2 - 4 * self.bit(1)) + dz * (4 - 8 * self.bit(2))
+        return (place, self.plane(dx))
 
     def copy(self, n, src, dst, device):
         return pltpu.make_async_remote_copy(
@@ -490,108 +486,81 @@
     def core_copy(self):
         return self.copy(0, self.send, self.r1, self.near(0))
 
-    def first_copy(self):
-        if self.y_first:
-            return self.copy(1, self.send.at[:, self.y_other, :], self.r2, self.near(1))
-        return self.copy(1, self.send.at[0], self.r2, self.across)
-
-    def second_copy(self):
-        if self.y_first:
-            return self.copy(2, self.send.at[1 - self.j, self.y_rows, :], self.r3, self.across)
-        return self.copy(2, self.send.at[1, 0 : self.half // 2, :], self.r3, self.near(1))
-
     def start_core(self):
         for h in range(2):
             for at, take in self.pieces(h, 1 - self.core):
                 self.send[h, at[0], at[1]] = take().astype(BFLOAT)
         self.core_copy().start()
 
-    def core_to_first(self):
+    def x_copy(self):
+        return self.copy(1, self.send.at[0], self.r2, (self.i, 1 - self.j))
+
+    def core_to_x(self):
         self.core_copy().wait()
-        if self.y_first:
-            for h in range(2):
-                for at, take in self.pieces(h, self.core):
-                    arrived = self.r1[h, at[0], at[1]].astype(FLOAT)
-                    self.send[h, at[0], at[1]] = (take() + arrived).astype(BFLOAT)
-            self.first_copy().start()
-            return
-        for at, take in self.pieces(1 - self.j, self.core):
-            arrived = self.r1[1 - self.j, at[0], at[1]].astype(FLOAT)
-            self.send[0, at[0], at[1]] = (take() + arrived).astype(BFLOAT)
-        self.first_copy().start()
-        for at, take in self.pieces(self.j, self.core):
-            self.own[at[0], at[1]] = take() + self.r1[self.j, at[0], at[1]].astype(FLOAT)
-
-    def first_to_second(self):
-        self.first_copy().wait()
-        if self.y_first:
-            far = self.send[1 - self.j, self.y_rows, :].astype(FLOAT) + self.r2[1 - self.j].astype(FLOAT)
-            self.send[1 - self.j, self.y_rows, :] = far.astype(BFLOAT)
-            self.second_copy().start()
-            near = self.send[self.j, self.y_rows, :].astype(FLOAT) + self.r2[self.j].astype(FLOAT)
-            self.own[self.y_rows, :] = near
-            return
-        far = self.own[self.y_other, :] + self.r2[self.y_other, :].astype(FLOAT)
-        self.send[1, 0 : self.half // 2, :] = far.astype(BFLOAT)
-        self.second_copy().start()
-        self.own[self.y_rows, :] += self.r2[self.y_rows, :].astype(FLOAT)
-
-    def third_copy(self):
-        return self.copy(3, self.zbuf[0], self.r4, self.near(2))
-
-    def fourth_copy(self):
-        return self.copy(4, self.zbuf[1], self.r5, self.near(3))
-
-    def second_to_third(self):
-        self.second_copy().wait()
-        self.own[self.y_rows, :] += self.r3[...].astype(FLOAT)
-        self.zbuf[0][...] = self.own[self.z_other, :].astype(BFLOAT)
-        self.third_copy().start()
-
-    def third_to_fourth(self):
-        self.third_copy().wait()
-        total = self.own[self.z_rows, :] + self.r4[...].astype(FLOAT)
-        self.zbuf[1][...] = total.astype(BFLOAT)
-        self.fourth_copy().start()
+        for n, h in enumerate((1 - self.j, self.j)):
+            for at, take in self.pieces(h, self.core):
+                arrived = self.r1[h, at[0], at[1]].astype(FLOAT)
+                self.send[n, at[0], at[1]] = (take() + arrived).astype(BFLOAT)
+            if n == 0:
+                self.x_copy().start()
+
+    def x_to_direct(self):
+        self.x_copy().wait()
+        self.send[1] = (self.send[1].astype(FLOAT) + self.r2[...].astype(FLOAT)).astype(BFLOAT)
+        for n, (dx, dy, dz) in enumerate(TURNS[3:0:-1]):
+            self.copy(6, self.send.at[1, self.rows(dy, dz), :], self.r3.at[n], self.member(dx, dy, dz)).start()
+
+    def z_copy(self):
+        return self.copy(2, self.send.at[1, self.mine, :], self.r5, self.near(3))
+
+    def direct_to_z(self):
+        wait_for(self.r3, self.ssem.at[6])
+        wait_for(self.r3, self.rsem.at[6])
+        total = self.send[1, self.mine, :].astype(FLOAT)
+        for n in range(3):
+            total += self.r3[n].astype(FLOAT)
+        self.send[1, self.mine, :] = total.astype(BFLOAT)
+        self.z_copy().start()
 
     def keep_copy(self):
-        return pltpu.make_async_copy(self.fin, self.final.at[self.core, self.z_rows, :], self.ssem.at[8])
-
-    def z_gather(self):
-        return self.copy(5, self.fin, self.final.at[self.core, self.z_rows, :], self.near(2))
-
-    def y_gather(self):
-        place = self.final.at[self.core, self.y_rows, :]
-        return self.copy(6, place, place, self.near(1))
+        return pltpu.make_async_copy(self.fin, self.final.at[self.core, self.mine, :], self.ssem.at[7])
+
+    def z_to_gather(self):
+        self.z_copy().wait()
+        total = self.send[1, self.mine, :].astype(FLOAT) + self.r5[...].astype(FLOAT)
+        self.fin[...] = total.astype(BFLOAT)
+        self.keep_copy().start()
+        dst = self.final.at[self.core, self.mine, :]
+        for dx, dy, dz in TURNS[:0:-1]:
+            if dx == 0 or self.everywhere is not None:
+                self.copy(3 + dx, self.fin, dst, self.member(dx, dy, dz)).start()
 
     def core_gather(self):
-        place = self.final.at[self.core]
-        return self.copy(7, place, place, self.near(0))
-
-    def fourth_done(self):
-        self.fourth_copy().wait()
-        self.fin[...] = (self.zbuf[1][...].astype(FLOAT) + self.r5[...].astype(FLOAT)).astype(BFLOAT)
-        self.keep_copy().start()
-        self.z_gather().start()
-
-    def z_to_y(self):
+        if self.everywhere is not None:
+            place = self.everywhere.at[:, self.core]
+        else:
+            place = self.final.at[self.core]
+        return self.copy(5, place, place, self.near(0))
+
+    def gather_to_core(self):
         self.keep_copy().wait()
-        self.z_gather().wait()
-        self.y_gather().start()
-
-    def y_done(self):
-        self.y_gather().wait()
+        three = self.final.at[self.core, 0 : 3 * self.part, :]
+        wait_for(three, self.ssem.at[3])
+        wait_for(three, self.rsem.at[3])
+        if self.everywhere is not None:
+            four = self.everywhere.at[1 - self.j, self.core]
+            wait_for(four, self.ssem.at[4])
+            wait_for(four, self.rsem.at[4])
+        self.core_gather().start()
 
     def step(self, n):
         (
             self.start_core,
-            self.core_to_first,
-            self.first_to_second,
-            self.second_to_third,
-            self.third_to_fourth,
-            self.fourth_done,
-            self.z_to_y,
-            self.y_done,
+            self.core_to_x,
+            self.x_to_direct,
+            self.direct_to_z,
+            self.z_to_gather,
+            self.gather_to_core,
         )[n]()
 
 
@@ -608,21 +577,15 @@
     ) = refs[23:37]
     work = refs[37:44]
     own_s = refs[44]
-    group_bufs = [refs[45 + 7 * n : 52 + 7 * n] for n in range(4)]
+    group_bufs = [refs[45 + 6 * n : 51 + 6 * n] for n in range(4)]
     sizes = [bufs[0].shape[1] for bufs in group_bufs]
-    owns = (
-        own_s.at[0 : sizes[0], :],
-        own_s.at[sizes[0] : sizes[0] + sizes[1], :],
-        gdown_s.at[0 : sizes[2], :],
-        gdown_s.at[sizes[2] : sizes[2] + sizes[3], :],
-    )
     tile = work[5].shape[0]
     work = work[:5] + (own_s.at[0:tile, :], own_s.at[tile : 2 * tile, :]) + work[5:]
     (
         lat_send, lat_recv, cot_send, cot_recv, own_sem, out_send, out_recv, tg_send, tg_recv,
-        w_local, wx_send, wx_recv, wc_send, wc_recv, sh_send, sh_recv,
-    ) = refs[73:89]
-    group_sems = [refs[89 + 2 * n : 91 + 2 * n] for n in range(4)]
+        w_local, wx_send, wx_recv, wy_send, wy_recv, wc_send, wc_recv,
+    ) = refs[69:85]
+    group_sems = [refs[85 + 2 * n : 87 + 2 * n] for n in range(4)]
     i, j = lax.axis_index("gx"), lax.axis_index("gy")
     places = lax.axis_size("gx")
     core = lax.rem(i, 2)
@@ -645,8 +608,11 @@
     def greet(k):
         pl.semaphore_signal(barrier, inc=1, device_id=(lax.rem(i + k, places), j), device_id_type=mesh_id)
 
-    pl.semaphore_signal(barrier, inc=1, device_id=across, device_id_type=mesh_id)
-    pl.semaphore_wait(barrier, places)
+    for dy in range(2):
+        for dz in range(2):
+            place = i + dy * (2 - 4 * ybit) + dz * (4 - 8 * lax.rem(i // 4, 2))
+            pl.semaphore_signal(barrier, inc=1, device_id=(place, 1 - j), device_id_type=mesh_id)
+    pl.semaphore_wait(barrier, places + 3)
 
     def part(ref, t):
         count = ref.shape[1] // tiles
@@ -669,9 +635,13 @@
     ff_half = upb_hbm.shape[1]
     blocks = ff_half // FFB
 
-    def weight_views(owner, whole):
+    def weight_views(owner, share):
         def rows_of(count):
-            return (0, count) if whole else (pl.multiple_of(core * (count // 2), 16), count // 2)
+            if share == "all":
+                return 0, count
+            if share == "half":
+                return pl.multiple_of(core * (count // 2), 16), count // 2
+            return pl.multiple_of((core * 2 + ybit) * (count // 4), 16), count // 4
 
         start, size = rows_of(width)
         r = pl.ds(start, size)
@@ -692,14 +662,18 @@
             views.append((wdown_hbm.at[here, :], wdown_s.at[there, :]))
         return views
 
-    here_views = weight_views(j, True)
+    here_views = weight_views(j, "all")
     x_copies = [
         remote(src, dst, wx_send.at[n], wx_recv.at[n], across)
-        for n, (src, dst) in enumerate(weight_views(j, False))
+        for n, (src, dst) in enumerate(weight_views(j, "quarter")[:4] + weight_views(j, "half")[4:])
+    ]
+    y_copies = [
+        remote(dst, dst, wy_send.at[n], wy_recv.at[n], beside)
+        for n, (_, dst) in enumerate(weight_views(1 - j, "quarter")[:4])
     ]
     c_copies = [
         remote(dst, dst, wc_send.at[n], wc_recv.at[n], sibling)
-        for n, (_, dst) in enumerate(weight_views(1 - j, False))
+        for n, (_, dst) in enumerate(weight_views(1 - j, "half"))
     ]
     own_copies = [pltpu.make_async_copy(src, dst, w_local.at[n]) for n, (src, dst) in enumerate(here_views)]
     n_weights = len(x_copies)
@@ -729,7 +703,6 @@
     upb_x.start()
     upb_own.start()
 
-    @pl.loop(0, tiles)
     def send_cot(t):
         keep(cot_hbm, frame_s, t, own_sem.at[tiles + t]).start()
         scatter(cot_hbm, frame_s, t, cot_send, cot_recv.at[t])
@@ -740,6 +713,9 @@
             if after is not None:
                 after[n].start()
 
+    for t in range(tiles):
+        send_cot(t)
+
     last_tile = tiles - 1
     middle = min(1, last_tile)
 
@@ -757,18 +733,16 @@
     def stem_done(t):
         @pl.when(t == last_tile)
         def _():
+            move(0, 4, x_copies, y_copies)
             move(0, 4, own_copies, None)
 
     def attend_done(turn, t):
-        @pl.when((turn == 0) & (t == middle))
-        def _():
-            move(0, 4, x_copies, c_copies)
-
         @pl.when((turn == 0) & (t == last_tile))
         def _():
+            move(0, 4, y_copies, c_copies)
             move(0, 4, c_copies, None)
 
-        @pl.when((turn == 1) & (t == last_tile))
+        @pl.when((turn == 1) & (t == middle))
         def _():
             move(4, 6, x_copies, c_copies)
 
@@ -777,15 +751,12 @@
         upb_own.wait()
         move(4, n_weights, own_copies, None)
 
-    def feed_block(t, turn):
-        for block in range(blocks):
-
-            @pl.when((t == 0) & (turn == blocks + block))
-            def _():
-                first = 4 + 2 * block
-                if block > 0:
-                    move(first, first + 2, x_copies, c_copies)
-                move(first, first + 2, c_copies, None)
+    def feed_block(turn):
+        first = 4 + 2 * (turn - blocks)
+        if turn > blocks:
+            move(first, first + 2, x_copies, c_copies)
+        if turn >= blocks:
+            move(first, first + 2, c_copies, None)
 
     def cot_ready(t):
         keep(cot_hbm, frame_s, t, own_sem.at[tiles + t]).wait()
@@ -799,9 +770,12 @@
         keep(frame_s, out_hbm, t, own_sem.at[2 * tiles + t]).wait()
         wait_for(most(frame_s, t), out_send.at[t])
 
-    def tg_ready(t):
+    def send_tg(t):
         keep(frame_s, tg_hbm, t, own_sem.at[3 * tiles + t]).start()
         scatter(frame_s, tg_hbm, t, tg_send.at[t], tg_recv)
+
+    def tg_ready(t):
+        send_tg(t)
 
     def grab(ref, r0, nrows, c0, ncols):
         return lambda: ref[pl.ds(r0, nrows), pl.ds(c0, ncols)]
@@ -873,14 +847,13 @@
 
     where = (i, j)
     down, up, stem, query = [
-        Reducer(where, pieces, bufs + (own,), final, sems, y_first)
-        for pieces, bufs, own, final, sems, y_first in zip(
+        Reducer(where, pieces, bufs, final, sems, everywhere)
+        for pieces, bufs, final, sems, everywhere in zip(
             (down_pieces, up_pieces, stem_pieces, query_pieces),
             group_bufs,
-            owns,
             (down_hbm, up_hbm, shared_hbm.at[j], query_hbm),
             group_sems,
-            Y_FIRST,
+            (None, None, shared_hbm, None),
         )
     ]
 
@@ -923,20 +896,11 @@
     )
     stem.start_core()
     query.start_core()
-    to_x = remote(shared_hbm.at[j, core], shared_hbm.at[j, core], sh_send.at[0], sh_recv.at[0], across)
-    to_core = remote(shared_hbm.at[:, core], shared_hbm.at[:, core], sh_send.at[1], sh_recv.at[1], sibling)
+    groups = (down, up, stem, query)
     for g, n in ORDER:
-        group = (down, up, stem, query)[g]
-        if n == 8 and g == STEM:
-            to_x.wait()
-            to_core.start()
-            continue
-        group.step(n)
-        if n == 7:
-            (to_x if g == STEM else group.core_gather()).start()
-    for group in (down, up, query):
+        groups[g].step(n)
+    for group in groups:
         group.core_gather().wait()
-    to_core.wait()
     wait_for(lat_hbm.at[0 : places - 1], lat_send)
     wait_for(cot_hbm.at[0 : places - 1], cot_send)
     wait_for(out_hbm.at[0 : places - 1], out_recv)
@@ -948,13 +912,12 @@
         wait_for(most(frame_s, t), tg_send.at[t])
 
 
-def reduce_shapes(half, width, y_first):
+def reduce_shapes(half, width):
     return [
         pltpu.VMEM((2, half, width), BFLOAT),
         pltpu.VMEM((2, half, width), BFLOAT),
-        pltpu.VMEM((2, half // 2, width) if y_first else (half, width), BFLOAT),
-        pltpu.VMEM((half // 2, width), BFLOAT),
-        pltpu.VMEM((half // 4, width), BFLOAT),
+        pltpu.VMEM((half, width), BFLOAT),
+        pltpu.VMEM((3, half // 4, width), BFLOAT),
         pltpu.VMEM((half // 4, width), BFLOAT),
         pltpu.VMEM((half // 4, width), BFLOAT),
     ]
@@ -995,9 +958,9 @@
         pltpu.VMEM((ff // width * 16, width), FLOAT),
     ]
     scratch += [item for n, item in enumerate(work_shapes(rows, width, TILE)) if n not in (5, 6)]
-    scratch += [pltpu.VMEM((sizes[0] + sizes[1], width), FLOAT)]
-    for size, y_first in zip(sizes, Y_FIRST):
-        scratch += reduce_shapes(size, width, y_first)
+    scratch += [pltpu.VMEM((2 * TILE, width), FLOAT)]
+    for size in sizes:
+        scratch += reduce_shapes(size, width)
     scratch += [
         dma,
         dma((tiles,)),
@@ -1013,10 +976,10 @@
         dma((n_weights + 1,)),
         dma((n_weights,)),
         dma((n_weights,)),
-        dma((2,)),
-        dma((2,)),
+        dma((n_weights,)),
+        dma((n_weights,)),
     ]
-    scratch += [dma((9,))] * 8
+    scratch += [dma((8,))] * 8
     return pl.pallas_call(
         functools.partial(wide_kernel, local_len),
         out_shape=(shape(cot.shape, BFLOAT), shape(cot.shape, BFLOAT))

time: 199 us -> 193 us (0.970)
  Pallas kernels: 172 us -> 168 us
    pallas_call x1, Pallas kernels: 172 us -> 168 us  [run_wide(): pl.pallas_call(functools.partial(wide_kernel, local_len), out_shape=(shap...]
where the time goes in v4:
time: 193 us
  Pallas kernels  168 us (87%)
  local copies, waits for them, and re-layouts  16 us (8%)
  other arithmetic  7.76 us (4%)
    pallas_call x1, Pallas kernels, run_wide(): pl.pallas_call(functools.partial(wide_kernel, local_len), out_shape=(shap...  168 us

profile of v4, /device:TPU:0, one launch (start us, length us, event | category | flops | bytes accessed | tf_op | source)
XLA Modules:
  0.0 192.9 jit_solution(2184976107515694242)
XLA Ops:
  0.6 0.0 copy-start
  0.7 0.7 convert.13
  1.4 0.1 concatenate.21
  1.5 0.9 convert.12
  2.4 0.7 concatenate.20
  3.1 0.0 copy-start.2
  3.1 0.1 pad_maximum_fusion
  3.3 0.7 copy.42
  4.0 0.2 pad.8.clone
  4.2 0.9 reshape.101.refs_0_
  5.1 0.0 copy-done
  5.1 0.1 constant_dynamic-slice_fusion
  5.1 0.1 copy.41
  5.2 0.7 tile.10.refs_1_
  6.0 0.0 copy-done.2
  6.0 0.0 copy-start.7
  6.0 1.8 reshape.102.refs_2_
  7.8 0.0 copy-done.7
  7.8 0.7 pad.9.refs_4_
  8.5 168.3 %shard_map.297 = (bf16[16,96,512]{2,1,0:T(8,128)(2,1)}, bf16[16,96,512]{2,1,0:T(8,128)(2,1)}, bf16[2,512,512]{2,1,0:T(8,128)(2,1)}, bf16[2,640,512]{2,1,0:T(8,12...) custom-call(bf16[16,48,128]{2,1,0:T(8,128)(2,1)} %reshape.101.refs_0_, f32[24,256]{1,0:T(8,128)} %tile.10.refs_1_, ...), custom_call_target="tpu_custom_call" | custom-call | tf_op jit(solution)/shard_map/pallas_call | solution.py:983
  176.8 0.0 copy-start.3
  176.8 3.6 %reshape.103 = bf16[384,4,512]{2,1,0:T(4,128)(2,1)} reshape(bf16[16,96,512]{2,1,0:T(8,128)(2,1)} %get-tuple-element.22) | data formatting | bytes 3145728 | tf_op jit(solution)/shard_map/reshape | solution.py:1040
  180.4 0.0 copy-done.3
  180.4 0.0 copy-start.5
  180.4 1.8 reshape.104
  182.3 0.0 copy-done.5
  182.3 0.1 slice.59
  182.4 0.4 bitcast_convert_fusion
  182.8 0.0 copy-start.1
  182.8 1.5 slice.76
  184.3 0.6 slice.77
  184.9 0.6 fusion.3
  185.5 0.0 copy-done.1
  185.5 1.0 fusion.2
  186.5 0.0 copy-start.4
  186.6 0.8 pad_maximum_fusion.1
  187.4 0.6 copy-done.4
  188.1 0.9 bitcast_convert_fusion.2
  188.9 0.1 fusion
  189.0 0.0 copy-start.6
  189.0 1.6 maximum_convert_fusion
  190.6 0.6 dynamic-slice_convert_fusion
  191.2 0.0 copy-done.6
  191.2 1.7 bitcast_convert_fusion.1
  (6 shorter events, 0.1 us)
Async XLA Ops:
  0.6 4.4 %copy-start = (s32[768,64]{0,1:T(8,128)S(1)}, s32[768,64]{0,1:T(8,128)}, u32[]{:S(2)}) copy-start(s32[768,64]{0,1:T(8,128)} %param.20) | copy-start | bytes 589828
  3.1 2.8 %copy-start.2 = (bf16[384,4,512]{2,1,0:T(4,128)(2,1)S(1)}, bf16[384,4,512]{2,1,0:T(4,128)(2,1)}, u32[]{:S(2)}) copy-start(bf16[384,4,512]{2,1,0:T(4,128)(2,1)} %param.21) | copy-start | bytes 4718596
  6.0 1.8 copy-start.7
  176.8 3.6 %copy-start.3 = (bf16[16,96,512]{2,1,0:T(8,128)(2,1)S(1)}, bf16[16,96,512]{2,1,0:T(8,128)(2,1)}, u32[]{:S(2)}) copy-start(bf16[16,96,512]{2,1,0:T(8,128)(2,1)} %get-tuple-element.23) | copy-start | bytes 4718596
  180.4 1.8 copy-start.5
  182.8 2.7 %copy-start.1 = (bf16[2,384,512]{2,1,0:T(8,128)(2,1)S(1)}, bf16[2,384,512]{2,1,0:T(8,128)(2,1)}, u32[]{:S(2)}) copy-start(bf16[2,384,512]{2,1,0:T(8,128)(2,1)} %get-tuple-element.25) | copy-start | bytes 2359300
  186.5 1.5 copy-start.4
  189.0 2.2 %copy-start.6 = (bf16[2,512,512]{2,1,0:T(8,128)(2,1)S(1)}, bf16[2,512,512]{2,1,0:T(8,128)(2,1)}, u32[]{:S(2)}) copy-start(bf16[2,512,512]{2,1,0:T(8,128)(2,1)} %get-tuple-element.27) | copy-start | bytes 3145732

commit v5 on v4

--- a/solution.py
+++ b/solution.py
@@ -1031,8 +1031,9 @@
     extra = jnp.pad(action_table, ((0, HOT_PAD - actions_n), (0, 0)))
     vec = [item[None] for item in (first_gain, first_bias, second_gain, second_bias, down_bias)]
     if rows % TILE == 0 and rows <= MAX_ROWS and places == 16:
-        lat = jnp.pad(lat, ((0, 0), (0, 0), (0, 0), (0, 64 - groups - 1)))
-        lat = lat.reshape(places, seqs * local_len // 2, 128)
+        lat = jnp.pad(latents, ((0, 0), (0, 0), (0, 64 - groups)))
+        lat += jnp.pad(actions[..., None], ((0, 0), (0, 0), (groups, 63 - groups)))
+        lat = lat.astype(BFLOAT).reshape(places, seqs * local_len // 2, 128)
         out, tg, gdown, up, query, shared = run_wide(
             local_len, lat, seg, cot, stem_weight, extra, query_weight, key_weight, value_weight,
             out_weight, up_weight, down_weight, up_bias[None], *vec,

time: 193 us -> 192 us (level)
  no operation moved by 1% of the time
where the time goes in v5:
time: 192 us
  Pallas kernels  168 us (88%)
  local copies, waits for them, and re-layouts  15.8 us (8%)
  other arithmetic  6.71 us (3%)
    pallas_call x1, Pallas kernels, run_wide(): pl.pallas_call(functools.partial(wide_kernel, local_len), out_shape=(shap...  168 us

profile of v5, /device:TPU:0, one launch (start us, length us, event | category | flops | bytes accessed | tf_op | source)
XLA Modules:
  0.0 191.6 jit_solution(4522322429505358089)
XLA Ops:
  0.6 0.0 copy-start
  0.7 0.0 copy-start.2
  0.7 1.2 copy.40
  1.9 0.7 add_convert_fusion
  2.6 0.3 copy.41
  2.9 0.9 reshape.95.refs_0_
  3.8 0.0 copy-done
  3.8 0.1 constant_dynamic-slice_fusion
  3.9 0.1 copy.43
  4.0 0.7 tile.10.refs_1_
  4.7 0.0 copy-done.2
  4.7 0.0 copy-start.7
  4.7 1.8 reshape.96.refs_2_
  6.5 0.0 copy-done.7
  6.5 0.7 pad.14.refs_4_
  7.2 168.4 %shard_map.297 = (bf16[16,96,512]{2,1,0:T(8,128)(2,1)}, bf16[16,96,512]{2,1,0:T(8,128)(2,1)}, bf16[2,512,512]{2,1,0:T(8,128)(2,1)}, bf16[2,640,512]{2,1,0:T(8,12...) custom-call(bf16[16,48,128]{2,1,0:T(8,128)(2,1)} %reshape.95.refs_0_, f32[24,256]{1,0:T(8,128)} %tile.10.refs_1_, ...), custom_call_target="tpu_custom_call" | custom-call | tf_op jit(solution)/shard_map/pallas_call | solution.py:983
  175.6 0.0 copy-start.3
  175.6 3.6 %reshape.97 = bf16[384,4,512]{2,1,0:T(4,128)(2,1)} reshape(bf16[16,96,512]{2,1,0:T(8,128)(2,1)} %get-tuple-element.22) | data formatting | bytes 3145728 | tf_op jit(solution)/shard_map/reshape | solution.py:1041
  179.2 0.0 copy-done.3
  179.2 0.0 copy-start.5
  179.2 1.8 reshape.98
  181.0 0.0 copy-done.5
  181.0 0.1 slice.59
  181.1 0.4 bitcast_convert_fusion
  181.5 0.0 copy-start.1
  181.5 1.5 slice.76
  183.0 0.6 slice.77
  183.6 0.6 fusion.3
  184.2 0.0 copy-done.1
  184.2 1.0 fusion.2
  185.3 0.0 copy-start.4
  185.3 0.8 pad_maximum_fusion
  186.2 0.6 copy-done.4
  186.8 0.9 bitcast_convert_fusion.2
  187.7 0.1 fusion
  187.8 0.0 copy-start.6
  187.8 1.6 maximum_convert_fusion
  189.4 0.6 dynamic-slice_convert_fusion
  190.0 0.0 copy-done.6
  190.0 1.7 bitcast_convert_fusion.1
  (6 shorter events, 0.1 us)
Async XLA Ops:
  0.6 3.1 %copy-start = (s32[768,64]{0,1:T(8,128)S(1)}, s32[768,64]{0,1:T(8,128)}, u32[]{:S(2)}) copy-start(s32[768,64]{0,1:T(8,128)} %param.20) | copy-start | bytes 589828
  0.7 4.0 %copy-start.2 = (bf16[384,4,512]{2,1,0:T(4,128)(2,1)S(1)}, bf16[384,4,512]{2,1,0:T(4,128)(2,1)}, u32[]{:S(2)}) copy-start(bf16[384,4,512]{2,1,0:T(4,128)(2,1)} %param.21) | copy-start | bytes 4718596
  4.7 1.8 copy-start.7
  175.6 3.6 %copy-start.3 = (bf16[16,96,512]{2,1,0:T(8,128)(2,1)S(1)}, bf16[16,96,512]{2,1,0:T(8,128)(2,1)}, u32[]{:S(2)}) copy-start(bf16[16,96,512]{2,1,0:T(8,128)(2,1)} %get-tuple-element.23) | copy-start | bytes 4718596
  179.2 1.8 copy-start.5
  181.5 2.7 %copy-start.1 = (bf16[2,384,512]{2,1,0:T(8,128)(2,1)S(1)}, bf16[2,384,512]{2,1,0:T(8,128)(2,1)}, u32[]{:S(2)}) copy-start(bf16[2,384,512]{2,1,0:T(8,128)(2,1)} %get-tuple-element.25) | copy-start | bytes 2359300
  185.3 1.5 copy-start.4
  187.8 2.2 %copy-start.6 = (bf16[2,512,512]{2,1,0:T(8,128)(2,1)S(1)}, bf16[2,512,512]{2,1,0:T(8,128)(2,1)}, u32[]{:S(2)}) copy-start(bf16[2,512,512]{2,1,0:T(8,128)(2,1)} %get-tuple-element.27) | copy-start | bytes 3145732
